TPU v7x, 32 devices: a whole 2x2x4 slice. The times are simulated.
32 devices in a mesh: cross: 4 (over x, core), along: 8 (over z, y).
Axes of the slice: x: 2, y: 2, z: 4, core: 2. Of those that a mesh axis runs over, the one named last changes fastest.
Arguments:
- surface: float32 [1024, 2048], P('cross', 'along'), may hold values from -6 to 6
- flux_cross: float32 [1024, 2048], P('cross', 'along'), may hold values from -6 to 6
- flux_along: float32 [1024, 2048], P('cross', 'along'), may hold values from -6 to 6
- celerity_sq: float32 [1024, 2048], P('cross', 'along'), may hold values from 0.05 to 1
- wet_mask: int32 [1024, 2048], P('cross', 'along'), may hold values from 0 to 1, as said below
- range_test: float32 [2048, 128], P('along'), may hold values from -0.125 to 0.125
- corange_test: float32 [128, 1024], P(None, 'cross'), may hold values from -0.1875 to 0.1875
- core_left: float32 [256, 1024], P(None, 'cross'), may hold values from -0.1875 to 0.1875
- core_right: float32 [2048, 256], P('along'), may hold values from -0.125 to 0.125
Outputs:
- surface_next: float32 [1024, 2048], P('cross', 'along')
- flux_cross_next: float32 [1024, 2048], P('cross', 'along')
- flux_along_next: float32 [1024, 2048], P('cross', 'along')
- range_sketch: float32 [1024, 128], P('cross')
- corange_sketch: float32 [128, 2048], P(None, 'along')
- core_sketch: float32 [256, 256], replicated
Inputs may be any that keep to these rules, and one draw needn't show every extreme that they name: `wet_mask`: 1 marks a wet cell, 0 a dry one.
All inputs are finite; a program needn't handle non-finite values.
Results may differ from a plain program's by a relative error of at most 0.000073.
Values sent between devices are 32-bit elements; how exact they have to be, the bound alone decides.
No kernel may reach another device: no remote copies, remote signals or barrier semaphores. Data moves between devices by JAX's collectives and lax.ppermute only.
A program may use at most 64 MiB of HBM per device.

v0:
```python
import jax
import jax.numpy as jnp
from jax import lax
from jax.sharding import PartitionSpec as P


def with_halo(block, sides, width):
    for axis, dim in sides:
        count = lax.axis_size(axis)
        forward = [(i, i + 1) for i in range(count - 1)]
        backward = [(target, source) for source, target in forward]
        low = lax.ppermute(
            lax.slice_in_dim(block, block.shape[dim] - width, None, axis=dim), axis, forward
        )
        high = lax.ppermute(lax.slice_in_dim(block, 0, width, axis=dim), axis, backward)
        block = jnp.concatenate([low, block, high], axis=dim)
    return block


def derive(padded, axis):
    count = padded.shape[axis] - 4

    def part(start):
        return lax.slice_in_dim(padded, start, start + count, axis=axis)

    return (8.0 * (part(3) - part(1)) - (part(4) - part(0))) / 12.0


def rims(elev, masked_x, masked_y):
    padded_x = with_halo(jnp.stack([elev, masked_x]), (("cross", 1),), 2)
    padded_y = with_halo(jnp.stack([elev, masked_y]), (("along", 2),), 2)
    elev_x = padded_x[0]
    mass_x = padded_x[1]
    elev_y = padded_y[0]
    mass_y = padded_y[1]
    return (elev_x, mass_x, elev_y, mass_y)


def tendency(elev, flux_x, flux_y, wet, celerity_sq):
    masked_x = wet * flux_x
    masked_y = wet * flux_y
    elev_x, mass_x, elev_y, mass_y = rims(elev, masked_x, masked_y)
    d_elev = -0.25 * wet * (derive(mass_x, 0) + derive(mass_y, 1))
    friction = 0.02 / celerity_sq
    d_flux_x = -wet * (0.25 * celerity_sq * derive(elev_x, 0) + friction * flux_x)
    d_flux_y = -wet * (0.25 * celerity_sq * derive(elev_y, 1) + friction * flux_y)
    return (d_elev, d_flux_x, d_flux_y)


def body(
    surface,
    flux_cross,
    flux_along,
    celerity_sq,
    wet_mask,
    range_test,
    corange_test,
    core_left,
    core_right,
):
    wet = wet_mask.astype(jnp.float32)
    k1e, k1p, k1q = tendency(surface, flux_cross, flux_along, wet, celerity_sq)
    k2e, k2p, k2q = tendency(surface + k1e, flux_cross + k1p, flux_along + k1q, wet, celerity_sq)
    surface_next = surface + 0.5 * (k1e + k2e)
    flux_cross_next = flux_cross + 0.5 * (k1p + k2p)
    flux_along_next = flux_along + 0.5 * (k1q + k2q)
    high = lax.Precision.HIGHEST
    range_part = jnp.dot(
        surface_next, range_test, precision=high, preferred_element_type=jnp.float32
    )
    corange_part = jnp.dot(
        corange_test, surface_next, precision=high, preferred_element_type=jnp.float32
    )
    right_part = jnp.dot(
        surface_next, core_right, precision=high, preferred_element_type=jnp.float32
    )
    range_sketch, right_rows = lax.psum((range_part, right_part), "along")
    core_part = jnp.dot(core_left, right_rows, precision=high, preferred_element_type=jnp.float32)
    corange_sketch, core_sketch = lax.psum((corange_part, core_part), "cross")
    return (
        surface_next,
        flux_cross_next,
        flux_along_next,
        range_sketch,
        corange_sketch,
        core_sketch,
    )


def solution(mesh):
    return jax.shard_map(
        body,
        mesh=mesh,
        in_specs=(
            P("cross", "along"),
            P("cross", "along"),
            P("cross", "along"),
            P("cross", "along"),
            P("cross", "along"),
            P("along", None),
            P(None, "cross"),
            P(None, "cross"),
            P("along", None),
        ),
        out_specs=(
            P("cross", "along"),
            P("cross", "along"),
            P("cross", "along"),
            P("cross", None),
            P(None, "along"),
            P(),
        ),
        check_vma=False,
    )
```

profile of v0, /device:TPU:0, one launch (start us, length us, event | category | flops | bytes accessed | tf_op | source)
XLA Modules:
  0.0 172.6 jit_solution(2057492898881393866)
XLA Ops:
  7.2 1.2 multiply_bitcast_fusion.3
  8.6 4.9 %collective-permute-start.2 = (f32[2,256,2]{2,1,0:T(8,128)S(1)}, f32[2,256,2]{2,1,0:T(8,128)S(1)}, u32[]{:S(2)}, u32[]{:S(2)}) collective-permute-start(f32[2,256,2]{2,1,0:T(8,128)S(1)} %get-tuple-element.35), channel_id=1, source_target_pairs={{0,1},{1,2},{2,3},{3,4},{4,5},{5,6},{6,7},{8,9},{9,10},{10,11},{11... | collective-permute-start | bytes 12296 | tf_op jit(solution)/shard_map/ppermute | solution.py:12
  13.5 1.3 collective-permute-start.3
  14.8 1.3 collective-permute-start
  16.1 3.0 %collective-permute-start.1 = (f32[2,2,256]{2,1,0:T(2,128)S(1)}, f32[2,2,256]{2,1,0:T(2,128)S(1)}, u32[]{:S(2)}, u32[]{:S(2)}) collective-permute-start(f32[2,2,256]{2,1,0:T(2,128)S(1)} %get-tuple-element.34), channel_id=1, source_target_pairs={{0,8},{8,16},{16,24},{1,9},{9,17},{17,25},{2,10},{10,18},{18,26},{... | collective-permute-start | bytes 12296 | tf_op jit(solution)/shard_map/ppermute | solution.py:12
  19.2 5.5 %collective-permute-done.2 = f32[2,256,2]{2,1,0:T(8,128)S(1)} collective-permute-done((f32[2,256,2]{2,1,0:T(8,128)S(1)}, f32[2,256,2]{2,1,0:T(8,128)S(1)}, u32[]{:S(2)}, u32[]{:S(2)}) %collective-permute-start.2) | collective-permute-done | bytes 4128 | tf_op jit(solution)/shard_map/ppermute | solution.py:12
  24.7 0.3 pad_maximum_fusion
  25.2 0.8 copy-done.2
  26.2 0.4 add_bitcast_fusion
  26.6 1.3 collective-permute-start.4
  27.9 3.2 %collective-permute-start.5 = (f32[2,2,256]{2,1,0:T(2,128)S(1)}, f32[2,2,256]{2,1,0:T(2,128)S(1)}, u32[]{:S(2)}, u32[]{:S(2)}) collective-permute-start(f32[2,2,256]{2,1,0:T(2,128)S(1)} %get-tuple-element.28), channel_id=1, source_target_pairs={{0,8},{8,16},{16,24},{1,9},{9,17},{17,25},{2,10},{10,18},{18,26},{... | collective-permute-start | bytes 12296 | tf_op jit(solution)/shard_map/ppermute | solution.py:12
  31.1 0.8 collective-permute-done.5
  32.0 1.2 fusion.19
  33.2 0.1 fusion
  33.4 4.4 %collective-permute-start.6 = (f32[2,256,2]{2,1,0:T(8,128)S(1)}, f32[2,256,2]{2,1,0:T(8,128)S(1)}, u32[]{:S(2)}, u32[]{:S(2)}) collective-permute-start(f32[2,256,2]{2,1,0:T(8,128)S(1)} %get-tuple-element.29), channel_id=1, source_target_pairs={{0,1},{1,2},{2,3},{3,4},{4,5},{5,6},{6,7},{8,9},{9,10},{10,11},{11... | collective-permute-start | bytes 12296 | tf_op jit(solution)/shard_map/ppermute | solution.py:12
  37.8 1.3 collective-permute-start.7
  39.1 5.2 %collective-permute-done.6 = f32[2,256,2]{2,1,0:T(8,128)S(1)} collective-permute-done((f32[2,256,2]{2,1,0:T(8,128)S(1)}, f32[2,256,2]{2,1,0:T(8,128)S(1)}, u32[]{:S(2)}, u32[]{:S(2)}) %collective-permute-start.6) | collective-permute-done | bytes 4128 | tf_op jit(solution)/shard_map/ppermute | solution.py:12
  44.2 4.8 %collective-permute-done.7 = f32[2,256,2]{2,1,0:T(8,128)S(1)} collective-permute-done((f32[2,256,2]{2,1,0:T(8,128)S(1)}, f32[2,256,2]{2,1,0:T(8,128)S(1)}, u32[]{:S(2)}, u32[]{:S(2)}) %collective-permute-start.7) | collective-permute-done | bytes 4128 | tf_op jit(solution)/shard_map/ppermute | solution.py:15
  49.0 0.3 pad_maximum_fusion.1
  49.4 0.3 fusion.27
  49.8 0.6 copy-done.10
  50.3 1.0 fusion.58
  51.4 1.1 fusion.59
  52.6 0.8 copy-done.11
  53.4 1.2 convolution_bitcast_fusion.1
  54.6 73.0 %all-reduce.5.cloned.1.call-done = (f32[256,128]{1,0:T(8,128)}, f32[256,256]{1,0:T(8,128)}) async-done(((f32[256,128]{1,0:T(8,128)}, f32[256,256]{1,0:T(8,128)}), (f32[256,128]{1,0:T(8,128)}, f32[256,256]{1,0:T(8,128)})) %all-reduce.5.cloned.1.call-update) | async-done | bytes 393232 | tf_op jit(solution)/shard_map/psum | solution.py:77
  127.6 2.2 %convolution_bitcast_fusion = f32[256,256]{0,1:T(8,128)} fusion(f32[256,256]{1,0:T(8,128)} %get-tuple-element.13, f32[256,256]{1,0:T(8,128)S(1)} %copy-done.7), kind=kOutput, calls=%fused_computation | convolution fusion | flops 201326592 | bytes 786432 | tf_op jit(solution)/shard_map/dot_general | solution.py:78
  129.9 1.2 fusion.9
  131.1 31.5 %all-reduce.7.cloned.1.call-done = (f32[128,256]{0,1:T(8,128)}, f32[256,256]{0,1:T(8,128)}) async-done(((f32[128,256]{0,1:T(8,128)}, f32[256,256]{0,1:T(8,128)}), (f32[128,256]{0,1:T(8,128)}, f32[256,256]{0,1:T(8,128)})) %all-reduce.7.cloned.1.call-update) | async-done | bytes 393232 | tf_op jit(solution)/shard_map/psum | solution.py:79
  162.5 1.7 copy.15
  164.2 0.8 copy.16
  165.1 0.7 copy.21
  (36 shorter events, 0.8 us)
Async XLA Ops:
  7.2 44.2 %copy-start = (f32[256,256]{1,0:T(8,128)S(1)}, f32[256,256]{1,0:T(8,128)}, u32[]{:S(2)}) copy-start(f32[256,256]{1,0:T(8,128)} %param.17) | copy-start | bytes 786436
  7.2 1.3 copy-start.1
  7.2 120.4 %all-reduce.5.cloned.1.call-start = ((), (), s32[]{:S(2)}) async-start(), calls=%async_computation | async-start | bytes 786432 | tf_op jit(solution)/shard_map/psum | solution.py:77
  8.6 16.0 %collective-permute-start.2 = (f32[2,256,2]{2,1,0:T(8,128)S(1)}, f32[2,256,2]{2,1,0:T(8,128)S(1)}, u32[]{:S(2)}, u32[]{:S(2)}) collective-permute-start(f32[2,256,2]{2,1,0:T(8,128)S(1)} %get-tuple-element.35), channel_id=1, source_target_pairs={{0,1},{1,2},{2,3},{3,4},{4,5},{5,6},{6,7},{8,9},{9,10},{10,11},{11... | collective-permute-start | bytes 12296 | tf_op jit(solution)/shard_map/ppermute | solution.py:12
  13.5 11.2 %collective-permute-start.3 = (f32[2,256,2]{2,1,0:T(8,128)S(1)}, f32[2,256,2]{2,1,0:T(8,128)S(1)}, u32[]{:S(2)}, u32[]{:S(2)}) collective-permute-start(f32[2,256,2]{2,1,0:T(8,128)S(1)} %get-tuple-element.36), channel_id=1, source_target_pairs={{1,0},{2,1},{3,2},{4,3},{5,4},{6,5},{7,6},{9,8},{10,9},{11,10},{12... | collective-permute-start | bytes 12296 | tf_op jit(solution)/shard_map/ppermute | solution.py:15
  14.8 10.3 %collective-permute-start = (f32[2,2,256]{2,1,0:T(2,128)S(1)}, f32[2,2,256]{2,1,0:T(2,128)S(1)}, u32[]{:S(2)}, u32[]{:S(2)}) collective-permute-start(f32[2,2,256]{2,1,0:T(2,128)S(1)} %get-tuple-element.33), channel_id=1, source_target_pairs={{8,0},{16,8},{24,16},{9,1},{17,9},{25,17},{10,2},{18,10},{26,18},{... | collective-permute-start | bytes 12296 | tf_op jit(solution)/shard_map/ppermute | solution.py:15
  16.1 9.0 %collective-permute-start.1 = (f32[2,2,256]{2,1,0:T(2,128)S(1)}, f32[2,2,256]{2,1,0:T(2,128)S(1)}, u32[]{:S(2)}, u32[]{:S(2)}) collective-permute-start(f32[2,2,256]{2,1,0:T(2,128)S(1)} %get-tuple-element.34), channel_id=1, source_target_pairs={{0,8},{8,16},{16,24},{1,9},{9,17},{17,25},{2,10},{10,18},{18,26},{... | collective-permute-start | bytes 12296 | tf_op jit(solution)/shard_map/ppermute | solution.py:12
  25.1 1.0 copy-start.2
  25.1 1.0 copy-start.4
  25.1 1.1 copy-start.6
  26.6 4.5 %collective-permute-start.4 = (f32[2,2,256]{2,1,0:T(2,128)S(1)}, f32[2,2,256]{2,1,0:T(2,128)S(1)}, u32[]{:S(2)}, u32[]{:S(2)}) collective-permute-start(f32[2,2,256]{2,1,0:T(2,128)S(1)} %get-tuple-element.27), channel_id=1, source_target_pairs={{8,0},{16,8},{24,16},{9,1},{17,9},{25,17},{10,2},{18,10},{26,18},{... | collective-permute-start | bytes 12296 | tf_op jit(solution)/shard_map/ppermute | solution.py:15
  27.9 4.1 %copy-start.5 = (f32[256,256]{1,0:T(8,128)S(1)}, f32[256,256]{1,0:T(8,128)}, u32[]{:S(2)}) copy-start(f32[256,256]{1,0:T(8,128)} %param.11) | copy-start | bytes 786436
  27.9 4.0 %collective-permute-start.5 = (f32[2,2,256]{2,1,0:T(2,128)S(1)}, f32[2,2,256]{2,1,0:T(2,128)S(1)}, u32[]{:S(2)}, u32[]{:S(2)}) collective-permute-start(f32[2,2,256]{2,1,0:T(2,128)S(1)} %get-tuple-element.28), channel_id=1, source_target_pairs={{0,8},{8,16},{16,24},{1,9},{9,17},{17,25},{2,10},{10,18},{18,26},{... | collective-permute-start | bytes 12296 | tf_op jit(solution)/shard_map/ppermute | solution.py:12
  33.4 10.9 %collective-permute-start.6 = (f32[2,256,2]{2,1,0:T(8,128)S(1)}, f32[2,256,2]{2,1,0:T(8,128)S(1)}, u32[]{:S(2)}, u32[]{:S(2)}) collective-permute-start(f32[2,256,2]{2,1,0:T(8,128)S(1)} %get-tuple-element.29), channel_id=1, source_target_pairs={{0,1},{1,2},{2,3},{3,4},{4,5},{5,6},{6,7},{8,9},{9,10},{10,11},{11... | collective-permute-start | bytes 12296 | tf_op jit(solution)/shard_map/ppermute | solution.py:12
  37.8 11.3 %collective-permute-start.7 = (f32[2,256,2]{2,1,0:T(8,128)S(1)}, f32[2,256,2]{2,1,0:T(8,128)S(1)}, u32[]{:S(2)}, u32[]{:S(2)}) collective-permute-start(f32[2,256,2]{2,1,0:T(8,128)S(1)} %get-tuple-element.30), channel_id=1, source_target_pairs={{1,0},{2,1},{3,2},{4,3},{5,4},{6,5},{7,6},{9,8},{10,9},{11,10},{12... | collective-permute-start | bytes 12296 | tf_op jit(solution)/shard_map/ppermute | solution.py:15
  49.4 0.9 copy-start.10
  50.3 2.2 %copy-start.3 = (f32[256,256]{1,0:T(8,128)}, f32[256,256]{1,0:T(8,128)S(1)}, u32[]{:S(2)}) copy-start(f32[256,256]{1,0:T(8,128)S(1)} %fusion.27) | copy-start | bytes 786436
  52.5 0.9 copy-start.11
  52.5 75.1 %copy-start.7 = (f32[256,256]{1,0:T(8,128)S(1)}, f32[256,256]{1,0:T(8,128)}, u32[]{:S(2)}) copy-start(f32[256,256]{1,0:T(8,128)} %param.16) | copy-start | bytes 786436
  52.5 110.0 %all-reduce.7.cloned.1.call-start = ((), (), s32[]{:S(2)}) async-start(), calls=%async_computation.1 | async-start | bytes 786432 | tf_op jit(solution)/shard_map/psum | solution.py:79
  162.5 1.7 copy-start.8
  164.2 0.9 copy-start.9
Sparse Core Ops, SparseCore 0:
  52.6 74.9 all-reduce.4
  130.7 31.7 all-reduce.6
where the time goes:
time: 173 us
  waiting for transfers between devices  121 us (70%)
  starting transfers between devices  20.7 us (12%)
  between operations  14.3 us (8%)
  local copies, waits for them, and re-layouts  5.76 us (3%)
  matrix products  5.61 us (3%)
  other arithmetic  5.5 us (3%)
    psum x1, waiting for transfers between devices, body(): range_sketch, right_rows = lax.psum((range_part, right_part), 'along')  73 us
    psum x1, waiting for transfers between devices, body(): corange_sketch, core_sketch = lax.psum((corange_part, core_part), 'cross')  31.5 us
    ppermute x4, starting transfers between devices, with_halo(): lax.ppermute(lax.slice_in_dim(block, block.shape[dim] - width, None, axis...  15.5 us
    ppermute x4, waiting for transfers between devices, with_halo(): lax.ppermute(lax.slice_in_dim(block, block.shape[dim] - width, None, axis...  11.5 us
    unnamed x27, local copies, waits for them, and re-layouts  5.65 us
    ppermute x4, starting transfers between devices, with_halo(): lax.ppermute(lax.slice_in_dim(block, 0, width, axis=dim), axis, backward)  5.17 us
    ppermute x4, waiting for transfers between devices, with_halo(): lax.ppermute(lax.slice_in_dim(block, 0, width, axis=dim), axis, backward)  4.8 us
  transfers between devices with their start and end apart: 10, of which 6 were waited for; matrix products, arithmetic and copies ran while one was open for 2% of the time, Pallas kernels for 0%

commit v1 on v0

--- a/solution.py
+++ b/solution.py
@@ -47,6 +47,53 @@
     return (d_elev, d_flux_x, d_flux_y)
 
 
+AXES = ("cross", "along")
+ROWS = 8
+LANES = 128
+
+
+def tiles_of(block):
+    down, wide = block.shape[0] // ROWS, block.shape[1] // LANES
+    return block.reshape(down, ROWS, wide, LANES).transpose(0, 2, 1, 3)
+
+
+def block_of(tiles, shape):
+    down, wide = shape[0] // ROWS, shape[1] // LANES
+    return tiles.reshape(down, wide, ROWS, LANES).transpose(0, 2, 1, 3).reshape(shape)
+
+
+def sum_sketches(range_part, corange_part, right_part, core_left):
+    high = lax.Precision.HIGHEST
+    core_part = jnp.dot(core_left, right_part, precision=high, preferred_element_type=jnp.float32)
+    crosses, alongs = lax.axis_size("cross"), lax.axis_size("along")
+    count = crosses * alongs
+    parts = (core_part, range_part, corange_part)
+    if any(part.size % (count * ROWS * LANES) for part in parts):
+        return (
+            lax.psum(range_part, "along"),
+            lax.psum(corange_part, "cross"),
+            lax.psum(core_part, AXES),
+        )
+    shares = [tiles_of(part).reshape(count, -1, ROWS, LANES) for part in parts]
+    sizes = [share.shape[1] for share in shares]
+    cuts = (sizes[0], sizes[0] + sizes[1])
+    sent = jnp.concatenate(shares, axis=1)
+    got = lax.all_to_all(sent, AXES, 0, 0, tiled=True)
+    got = got.reshape((crosses, alongs) + got.shape[1:])
+    core, ranged, coranged = jnp.split(got, cuts, axis=2)
+    core = jnp.broadcast_to(core.sum((0, 1), keepdims=True), core.shape)
+    ranged = jnp.broadcast_to(ranged.sum(1, keepdims=True), ranged.shape)
+    coranged = jnp.broadcast_to(coranged.sum(0, keepdims=True), coranged.shape)
+    totals = jnp.concatenate([core, ranged, coranged], axis=2).reshape(sent.shape)
+    out = lax.all_to_all(totals, AXES, 0, 0, tiled=True)
+    core, ranged, coranged = jnp.split(out, cuts, axis=1)
+    return (
+        block_of(ranged, range_part.shape),
+        block_of(coranged, corange_part.shape),
+        block_of(core, core_part.shape),
+    )
+
+
 def body(
     surface,
     flux_cross,
@@ -74,9 +121,9 @@
     right_part = jnp.dot(
         surface_next, core_right, precision=high, preferred_element_type=jnp.float32
     )
-    range_sketch, right_rows = lax.psum((range_part, right_part), "along")
-    core_part = jnp.dot(core_left, right_rows, precision=high, preferred_element_type=jnp.float32)
-    corange_sketch, core_sketch = lax.psum((corange_part, core_part), "cross")
+    range_sketch, corange_sketch, core_sketch = sum_sketches(
+        range_part, corange_part, right_part, core_left
+    )
     return (
         surface_next,
         flux_cross_next,

time: 173 us -> 93.5 us (0.54)
  waiting for transfers between devices: 121 us -> 31.4 us
  blocking collectives: 0 us -> 24.2 us
  between operations: 14.3 us -> 0.99 us
  matrix products: 5.61 us -> 1.94 us
  starting transfers between devices: 20.7 us -> 23.3 us
    psum x2 -> x0, waiting for transfers between devices: 104 us -> none  [the longest x1 73 us: body(): range_sketch, right_rows = lax.psum((range_part, right_part), 'along')]
    all_to_all x0 -> x1, blocking collectives: none -> 24.2 us  [sum_sketches(): got = lax.all_to_all(sent, AXES, 0, 0, tiled=True)]
    all_to_all x0 -> x1, waiting for transfers between devices: none -> 15.2 us  [sum_sketches(): out = lax.all_to_all(totals, AXES, 0, 0, tiled=True)]
    unnamed x27 -> x20, local copies, waits for them, and re-layouts: 5.65 us -> 2.95 us
    all_to_all x0 -> x1, starting transfers between devices: none -> 2.6 us  [sum_sketches(): out = lax.all_to_all(totals, AXES, 0, 0, tiled=True)]
  transfers between devices with their start and end apart: 10 -> 9, of which waited for: 6 -> 5; matrix products, arithmetic and copies ran while one was open for 2% -> 2% of each run, Pallas kernels for 0% -> 0%
where the time goes in v1:
time: 93.5 us; the launch traced here: 93 us
  waiting for transfers between devices  31.4 us (34%)
  blocking collectives  24.2 us (26%)
  starting transfers between devices  23.3 us (25%)
  other arithmetic  6.42 us (7%)
  local copies, waits for them, and re-layouts  4.75 us (5%)
  matrix products  1.94 us (2%)
  between operations  0.99 us (1%)
    all_to_all x1, blocking collectives, sum_sketches(): got = lax.all_to_all(sent, AXES, 0, 0, tiled=True)  24.2 us
    ppermute x4, starting transfers between devices, with_halo(): lax.ppermute(lax.slice_in_dim(block, block.shape[dim] - width, None, axis...  15.5 us
    all_to_all x1, waiting for transfers between devices, sum_sketches(): out = lax.all_to_all(totals, AXES, 0, 0, tiled=True)  15.2 us
    ppermute x4, waiting for transfers between devices, with_halo(): lax.ppermute(lax.slice_in_dim(block, block.shape[dim] - width, None, axis...  11.5 us
    ppermute x4, starting transfers between devices, with_halo(): lax.ppermute(lax.slice_in_dim(block, 0, width, axis=dim), axis, backward)  5.17 us
    ppermute x4, waiting for transfers between devices, with_halo(): lax.ppermute(lax.slice_in_dim(block, 0, width, axis=dim), axis, backward)  4.8 us
    unnamed x20, local copies, waits for them, and re-layouts  2.95 us
    all_to_all x1, starting transfers between devices, sum_sketches(): out = lax.all_to_all(totals, AXES, 0, 0, tiled=True)  2.6 us
  transfers between devices with their start and end apart: 9, of which 5 were waited for; matrix products, arithmetic and copies ran while one was open for 2% of the time, Pallas kernels for 0%

profile of v1, /device:TPU:0, one launch (start us, length us, event | category | flops | bytes accessed | tf_op | source)
XLA Modules:
  0.0 93.0 jit_solution(8608664881132039582)
XLA Ops:
  0.7 1.2 %multiply_bitcast_fusion.3 = (f32[1,256,256]{2,1,0:T(8,128)S(1)}, f32[1,256,256]{2,1,0:T(8,128)S(1)}) fusion(f32[256,256]{1,0:T(8,128)} %param.10, s32[256,256]{1,0:T(8,128)} %param.13, f32[256,256]{1,0:T(8,128)} %param.11), kind=kLoop, calls=%fused_computation.102 | loop fusion | flops 196608 | bytes 1310720 | tf_op jit(solution)/shard_map/stack | solution.py:30
  2.0 4.9 %collective-permute-start.2 = (f32[2,256,2]{2,1,0:T(8,128)S(1)}, f32[2,256,2]{2,1,0:T(8,128)S(1)}, u32[]{:S(2)}, u32[]{:S(2)}) collective-permute-start(f32[2,256,2]{2,1,0:T(8,128)S(1)} %get-tuple-element.29), channel_id=1, source_target_pairs={{0,1},{1,2},{2,3},{3,4},{4,5},{5,6},{6,7},{8,9},{9,10},{10,11},{11... | collective-permute-start | bytes 12296 | tf_op jit(solution)/shard_map/ppermute | solution.py:12
  6.9 1.3 %collective-permute-start.3 = (f32[2,256,2]{2,1,0:T(8,128)S(1)}, f32[2,256,2]{2,1,0:T(8,128)S(1)}, u32[]{:S(2)}, u32[]{:S(2)}) collective-permute-start(f32[2,256,2]{2,1,0:T(8,128)S(1)} %get-tuple-element.30), channel_id=1, source_target_pairs={{1,0},{2,1},{3,2},{4,3},{5,4},{6,5},{7,6},{9,8},{10,9},{11,10},{12... | collective-permute-start | bytes 12296 | tf_op jit(solution)/shard_map/ppermute | solution.py:15
  8.2 1.3 %collective-permute-start = (f32[2,2,256]{2,1,0:T(2,128)S(1)}, f32[2,2,256]{2,1,0:T(2,128)S(1)}, u32[]{:S(2)}, u32[]{:S(2)}) collective-permute-start(f32[2,2,256]{2,1,0:T(2,128)S(1)} %get-tuple-element.27), channel_id=1, source_target_pairs={{8,0},{16,8},{24,16},{9,1},{17,9},{25,17},{10,2},{18,10},{26,18},{... | collective-permute-start | bytes 12296 | tf_op jit(solution)/shard_map/ppermute | solution.py:15
  9.5 3.0 %collective-permute-start.1 = (f32[2,2,256]{2,1,0:T(2,128)S(1)}, f32[2,2,256]{2,1,0:T(2,128)S(1)}, u32[]{:S(2)}, u32[]{:S(2)}) collective-permute-start(f32[2,2,256]{2,1,0:T(2,128)S(1)} %get-tuple-element.28), channel_id=1, source_target_pairs={{0,8},{8,16},{16,24},{1,9},{9,17},{17,25},{2,10},{10,18},{18,26},{... | collective-permute-start | bytes 12296 | tf_op jit(solution)/shard_map/ppermute | solution.py:12
  12.6 5.5 %collective-permute-done.2 = f32[2,256,2]{2,1,0:T(8,128)S(1)} collective-permute-done((f32[2,256,2]{2,1,0:T(8,128)S(1)}, f32[2,256,2]{2,1,0:T(8,128)S(1)}, u32[]{:S(2)}, u32[]{:S(2)}) %collective-permute-start.2) | collective-permute-done | bytes 4128 | tf_op jit(solution)/shard_map/ppermute | solution.py:12
  18.1 0.3 pad_maximum_fusion
  18.6 0.8 copy-done.2
  19.6 0.4 add_bitcast_fusion
  20.0 1.3 %collective-permute-start.4 = (f32[2,2,256]{2,1,0:T(2,128)S(1)}, f32[2,2,256]{2,1,0:T(2,128)S(1)}, u32[]{:S(2)}, u32[]{:S(2)}) collective-permute-start(f32[2,2,256]{2,1,0:T(2,128)S(1)} %get-tuple-element.21), channel_id=1, source_target_pairs={{8,0},{16,8},{24,16},{9,1},{17,9},{25,17},{10,2},{18,10},{26,18},{... | collective-permute-start | bytes 12296 | tf_op jit(solution)/shard_map/ppermute | solution.py:15
  21.3 3.2 %collective-permute-start.5 = (f32[2,2,256]{2,1,0:T(2,128)S(1)}, f32[2,2,256]{2,1,0:T(2,128)S(1)}, u32[]{:S(2)}, u32[]{:S(2)}) collective-permute-start(f32[2,2,256]{2,1,0:T(2,128)S(1)} %get-tuple-element.22), channel_id=1, source_target_pairs={{0,8},{8,16},{16,24},{1,9},{9,17},{17,25},{2,10},{10,18},{18,26},{... | collective-permute-start | bytes 12296 | tf_op jit(solution)/shard_map/ppermute | solution.py:12
  24.5 0.8 collective-permute-done.5
  25.4 1.2 %fusion.19 = (f32[256,256]{1,0:T(8,128)}, f32[1,256,256]{2,1,0:T(8,128)S(1)}) fusion(f32[256,256]{1,0:T(8,128)S(1)} %copy-done.4, f32[2,258,256]{2,1,0:T(8,128)S(1)} %get-tuple-element.20, f32[2,258,256]{2,1,0:T(8,128)S(1)} %get-tuple-element.19, s32[256,256]{1,0:T(8,128)S(1)} %copy-done.2, f32[256,256]{1,0:T(8,128)S(1)} %copy-done.6, ...), kind=kLoop, calls=%fused_computation.47 | loop fusion | flops 2424832 | bytes 4718592 | tf_op jit(solution)/shard_map/add | solution.py:112
  26.8 4.4 %collective-permute-start.6 = (f32[2,256,2]{2,1,0:T(8,128)S(1)}, f32[2,256,2]{2,1,0:T(8,128)S(1)}, u32[]{:S(2)}, u32[]{:S(2)}) collective-permute-start(f32[2,256,2]{2,1,0:T(8,128)S(1)} %get-tuple-element.23), channel_id=1, source_target_pairs={{0,1},{1,2},{2,3},{3,4},{4,5},{5,6},{6,7},{8,9},{9,10},{10,11},{11... | collective-permute-start | bytes 12296 | tf_op jit(solution)/shard_map/ppermute | solution.py:12
  31.2 1.3 %collective-permute-start.7 = (f32[2,256,2]{2,1,0:T(8,128)S(1)}, f32[2,256,2]{2,1,0:T(8,128)S(1)}, u32[]{:S(2)}, u32[]{:S(2)}) collective-permute-start(f32[2,256,2]{2,1,0:T(8,128)S(1)} %get-tuple-element.24), channel_id=1, source_target_pairs={{1,0},{2,1},{3,2},{4,3},{5,4},{6,5},{7,6},{9,8},{10,9},{11,10},{12... | collective-permute-start | bytes 12296 | tf_op jit(solution)/shard_map/ppermute | solution.py:15
  32.5 5.2 %collective-permute-done.6 = f32[2,256,2]{2,1,0:T(8,128)S(1)} collective-permute-done((f32[2,256,2]{2,1,0:T(8,128)S(1)}, f32[2,256,2]{2,1,0:T(8,128)S(1)}, u32[]{:S(2)}, u32[]{:S(2)}) %collective-permute-start.6) | collective-permute-done | bytes 4128 | tf_op jit(solution)/shard_map/ppermute | solution.py:12
  37.6 4.8 %collective-permute-done.7 = f32[2,256,2]{2,1,0:T(8,128)S(1)} collective-permute-done((f32[2,256,2]{2,1,0:T(8,128)S(1)}, f32[2,256,2]{2,1,0:T(8,128)S(1)}, u32[]{:S(2)}, u32[]{:S(2)}) %collective-permute-start.7) | collective-permute-done | bytes 4128 | tf_op jit(solution)/shard_map/ppermute | solution.py:15
  42.4 0.3 pad_maximum_fusion.1
  43.2 0.6 copy-done.8
  43.7 0.6 convolution_bitcast_fusion.1
  44.5 0.8 copy-done.9
  45.2 0.4 convolution_bitcast_fusion.2
  45.7 0.4 fusion.59
  46.1 0.6 copy-done.7
  46.6 0.6 convolution_bitcast_fusion
  47.4 24.2 %all_to_all.10 = f32[32,4,8,128]{3,2,1,0:T(8,128)S(1)} all-to-all(f32[32,4,8,128]{3,2,1,0:T(8,128)S(1)} %pad_maximum_fusion.4), channel_id=1, replica_groups=mesh['cross'=4,'along'=8] {'cross','along'}, dimensions={0} | all-to-all | bytes 1048576 | tf_op jit(solution)/shard_map/all_to_all | solution.py:81
  71.7 0.9 pad_maximum_fusion.5
  72.6 2.6 %all-to-all-start.1 = ((f32[32,4,8,128]{3,2,1,0:T(8,128)}), f32[32,4,8,128]{3,2,1,0:T(8,128)S(1)}, u32[]{:S(2)}, u32[]{:S(2)}) async-start(f32[32,4,8,128]{3,2,1,0:T(8,128)} %bitcast.24), calls=%async_computation.1 | async-start | bytes 1048576 | tf_op jit(solution)/shard_map/all_to_all | solution.py:88
  75.2 1.2 %fusion.9 = f32[256,256]{1,0:T(8,128)} fusion(f32[256,256]{1,0:T(8,128)S(1)} %copy-done.5, f32[256,260]{1,0:T(8,128)S(1)} %get-tuple-element.11, s32[256,256]{1,0:T(8,128)S(1)} %copy-done.2, f32[256,256]{1,0:T(8,128)S(1)} %copy-done.6, f32[256,260]{1,0:T(8,128)S(1)} %get-tuple-element.13), kind=kLoop, calls=%fused_computation.35 | loop fusion | flops 1703936 | bytes 3145728 | tf_op jit(solution)/shard_map/add | solution.py:113
  76.4 15.2 %all-to-all-done.1 = f32[32,4,8,128]{3,2,1,0:T(8,128)S(1)} async-done(((f32[32,4,8,128]{3,2,1,0:T(8,128)}), f32[32,4,8,128]{3,2,1,0:T(8,128)S(1)}, u32[]{:S(2)}, u32[]{:S(2)}) %all-to-all-start.1) | async-done | bytes 524320 | tf_op jit(solution)/shard_map/all_to_all | solution.py:88
  91.5 0.7 slice_bitcast_fusion.4
  92.3 0.7 fusion.58
  (37 shorter events, 1.4 us)
Async XLA Ops:
  0.6 45.0 %copy-start = (f32[256,256]{1,0:T(8,128)S(1)}, f32[256,256]{1,0:T(8,128)}, u32[]{:S(2)}) copy-start(f32[256,256]{1,0:T(8,128)} %param.17) | copy-start | bytes 786436
  0.6 1.2 %copy-start.1 = (f32[256,256]{1,0:T(8,128)S(1)}, f32[256,256]{1,0:T(8,128)}, u32[]{:S(2)}) copy-start(f32[256,256]{1,0:T(8,128)} %param.9) | copy-start | bytes 786436
  2.0 16.0 %collective-permute-start.2 = (f32[2,256,2]{2,1,0:T(8,128)S(1)}, f32[2,256,2]{2,1,0:T(8,128)S(1)}, u32[]{:S(2)}, u32[]{:S(2)}) collective-permute-start(f32[2,256,2]{2,1,0:T(8,128)S(1)} %get-tuple-element.29), channel_id=1, source_target_pairs={{0,1},{1,2},{2,3},{3,4},{4,5},{5,6},{6,7},{8,9},{9,10},{10,11},{11... | collective-permute-start | bytes 12296 | tf_op jit(solution)/shard_map/ppermute | solution.py:12
  6.9 11.2 %collective-permute-start.3 = (f32[2,256,2]{2,1,0:T(8,128)S(1)}, f32[2,256,2]{2,1,0:T(8,128)S(1)}, u32[]{:S(2)}, u32[]{:S(2)}) collective-permute-start(f32[2,256,2]{2,1,0:T(8,128)S(1)} %get-tuple-element.30), channel_id=1, source_target_pairs={{1,0},{2,1},{3,2},{4,3},{5,4},{6,5},{7,6},{9,8},{10,9},{11,10},{12... | collective-permute-start | bytes 12296 | tf_op jit(solution)/shard_map/ppermute | solution.py:15
  8.2 10.3 %collective-permute-start = (f32[2,2,256]{2,1,0:T(2,128)S(1)}, f32[2,2,256]{2,1,0:T(2,128)S(1)}, u32[]{:S(2)}, u32[]{:S(2)}) collective-permute-start(f32[2,2,256]{2,1,0:T(2,128)S(1)} %get-tuple-element.27), channel_id=1, source_target_pairs={{8,0},{16,8},{24,16},{9,1},{17,9},{25,17},{10,2},{18,10},{26,18},{... | collective-permute-start | bytes 12296 | tf_op jit(solution)/shard_map/ppermute | solution.py:15
  9.5 9.0 %collective-permute-start.1 = (f32[2,2,256]{2,1,0:T(2,128)S(1)}, f32[2,2,256]{2,1,0:T(2,128)S(1)}, u32[]{:S(2)}, u32[]{:S(2)}) collective-permute-start(f32[2,2,256]{2,1,0:T(2,128)S(1)} %get-tuple-element.28), channel_id=1, source_target_pairs={{0,8},{8,16},{16,24},{1,9},{9,17},{17,25},{2,10},{10,18},{18,26},{... | collective-permute-start | bytes 12296 | tf_op jit(solution)/shard_map/ppermute | solution.py:12
  18.5 1.0 %copy-start.2 = (s32[256,256]{1,0:T(8,128)S(1)}, s32[256,256]{1,0:T(8,128)}, u32[]{:S(2)}) copy-start(s32[256,256]{1,0:T(8,128)} %param.13) | copy-start | bytes 786436
  18.5 1.0 %copy-start.4 = (f32[256,256]{1,0:T(8,128)S(1)}, f32[256,256]{1,0:T(8,128)}, u32[]{:S(2)}) copy-start(f32[256,256]{1,0:T(8,128)} %param.10) | copy-start | bytes 786436
  18.5 1.1 %copy-start.6 = (f32[256,256]{1,0:T(8,128)S(1)}, f32[256,256]{1,0:T(8,128)}, u32[]{:S(2)}) copy-start(f32[256,256]{1,0:T(8,128)} %param.12) | copy-start | bytes 786436
  20.0 4.5 %collective-permute-start.4 = (f32[2,2,256]{2,1,0:T(2,128)S(1)}, f32[2,2,256]{2,1,0:T(2,128)S(1)}, u32[]{:S(2)}, u32[]{:S(2)}) collective-permute-start(f32[2,2,256]{2,1,0:T(2,128)S(1)} %get-tuple-element.21), channel_id=1, source_target_pairs={{8,0},{16,8},{24,16},{9,1},{17,9},{25,17},{10,2},{18,10},{26,18},{... | collective-permute-start | bytes 12296 | tf_op jit(solution)/shard_map/ppermute | solution.py:15
  21.3 4.1 %copy-start.5 = (f32[256,256]{1,0:T(8,128)S(1)}, f32[256,256]{1,0:T(8,128)}, u32[]{:S(2)}) copy-start(f32[256,256]{1,0:T(8,128)} %param.11) | copy-start | bytes 786436
  21.3 4.0 %collective-permute-start.5 = (f32[2,2,256]{2,1,0:T(2,128)S(1)}, f32[2,2,256]{2,1,0:T(2,128)S(1)}, u32[]{:S(2)}, u32[]{:S(2)}) collective-permute-start(f32[2,2,256]{2,1,0:T(2,128)S(1)} %get-tuple-element.22), channel_id=1, source_target_pairs={{0,8},{8,16},{16,24},{1,9},{9,17},{17,25},{2,10},{10,18},{18,26},{... | collective-permute-start | bytes 12296 | tf_op jit(solution)/shard_map/ppermute | solution.py:12
  26.8 10.9 %collective-permute-start.6 = (f32[2,256,2]{2,1,0:T(8,128)S(1)}, f32[2,256,2]{2,1,0:T(8,128)S(1)}, u32[]{:S(2)}, u32[]{:S(2)}) collective-permute-start(f32[2,256,2]{2,1,0:T(8,128)S(1)} %get-tuple-element.23), channel_id=1, source_target_pairs={{0,1},{1,2},{2,3},{3,4},{4,5},{5,6},{6,7},{8,9},{9,10},{10,11},{11... | collective-permute-start | bytes 12296 | tf_op jit(solution)/shard_map/ppermute | solution.py:12
  31.2 11.3 %collective-permute-start.7 = (f32[2,256,2]{2,1,0:T(8,128)S(1)}, f32[2,256,2]{2,1,0:T(8,128)S(1)}, u32[]{:S(2)}, u32[]{:S(2)}) collective-permute-start(f32[2,256,2]{2,1,0:T(8,128)S(1)} %get-tuple-element.24), channel_id=1, source_target_pairs={{1,0},{2,1},{3,2},{4,3},{5,4},{6,5},{7,6},{9,8},{10,9},{11,10},{12... | collective-permute-start | bytes 12296 | tf_op jit(solution)/shard_map/ppermute | solution.py:15
  42.8 0.9 copy-start.8
  43.7 1.9 %copy-start.3 = (f32[256,256]{1,0:T(8,128)}, f32[256,256]{1,0:T(8,128)S(1)}, u32[]{:S(2)}) copy-start(f32[256,256]{1,0:T(8,128)S(1)} %fusion.27) | copy-start | bytes 786436
  44.3 0.9 copy-start.9
  45.7 1.0 %copy-start.7 = (f32[256,256]{1,0:T(8,128)S(1)}, f32[256,256]{1,0:T(8,128)}, u32[]{:S(2)}) copy-start(f32[256,256]{1,0:T(8,128)} %param.16) | copy-start | bytes 786436
  72.6 19.0 %all-to-all-start.1 = ((f32[32,4,8,128]{3,2,1,0:T(8,128)}), f32[32,4,8,128]{3,2,1,0:T(8,128)S(1)}, u32[]{:S(2)}, u32[]{:S(2)}) async-start(f32[32,4,8,128]{3,2,1,0:T(8,128)} %bitcast.24), calls=%async_computation.1 | async-start | bytes 1048576 | tf_op jit(solution)/shard_map/all_to_all | solution.py:88

commit v2 on v0

v2 whole, which is shorter than its diff:
```python
import functools

import jax
import jax.numpy as jnp
from jax import lax
from jax.experimental import pallas as pl
from jax.experimental.pallas import tpu as pltpu
from jax.sharding import PartitionSpec as P

AXES = ("cross", "along")
ROWS = 8
LANES = 128
HIGH = lax.Precision.HIGHEST


def f32(*shape):
    return jax.ShapeDtypeStruct(shape, jnp.float32)


def derive(field, axis):
    size = field.shape[axis]

    def part(shift):
        return pltpu.roll(field, (-shift) % size, axis)

    return (part(1) - part(-1)) * (8.0 / 12.0) - (part(2) - part(-2)) * (1.0 / 12.0)


def coefficients(celerity_sq, wet_mask):
    wet = wet_mask > 0
    return jnp.where(wet, 0.25 * celerity_sq, 0.0), jnp.where(wet, 0.02 / celerity_sq, 0.0)


def friction_of(slope):
    wet = slope > 0.0
    return jnp.where(wet, 0.005 / jnp.where(wet, slope, 1.0), 0.0)


def place(shape, axis, dim):
    return lax.broadcasted_iota(jnp.int32, shape, dim)


def pack_kernel(e_ref, p_ref, q_ref, c_ref, w_ref, even_ref, row0, row1, col0, col1):
    rows, cols = e_ref.shape
    wide = (ROWS, cols)
    at = place(wide, ROWS, 0)
    top = pl.ds(0, ROWS)
    e = e_ref[top, :]
    slope, _ = coefficients(c_ref[top, :], w_ref[top, :])
    mass = jnp.where(w_ref[top, :] > 0, p_ref[top, :], 0.0)
    up = jnp.where(
        at < 4, e, jnp.where(at < 6, pltpu.roll(mass, 4, 0), pltpu.roll(slope, 6, 0))
    )
    end = pl.ds(rows - ROWS, ROWS)
    e = e_ref[end, :]
    slope, _ = coefficients(c_ref[end, :], w_ref[end, :])
    mass = jnp.where(w_ref[end, :] > 0, p_ref[end, :], 0.0)
    down = jnp.where(
        at >= 4, e, jnp.where(at >= 2, pltpu.roll(mass, 4, 0), pltpu.roll(slope, 2, 0))
    )
    even = even_ref[0] == 0
    row0[...] = jnp.where(even, down, up)
    row1[...] = jnp.where(even, up, down)
    first, last = slice(0, LANES), slice(cols - LANES, cols)
    lane = place((rows, LANES), LANES, 1)
    left = lane < LANES // 2

    def edge(ref):
        return jnp.where(left, ref[:, first], ref[:, last])

    e, wet = edge(e_ref), edge(w_ref) > 0
    slope = jnp.where(wet, 0.25 * edge(c_ref), 0.0)
    mass = jnp.where(wet, edge(q_ref), 0.0)
    mass = jnp.where(left, pltpu.roll(mass, 4, 1), pltpu.roll(mass, LANES - 4, 1))
    slope = jnp.where(left, pltpu.roll(slope, 6, 1), pltpu.roll(slope, LANES - 6, 1))
    off = jnp.minimum(lane, LANES - 1 - lane)
    turned = jnp.where(off < 4, e, jnp.where(off < 6, mass, slope)).T
    to_left, to_right = turned[:ROWS], turned[LANES - ROWS :]
    even = even_ref[1] == 0
    col0[...] = jnp.where(even, to_right, to_left)
    col1[...] = jnp.where(even, to_left, to_right)


def row_halo(even, first, second):
    below, above = jnp.where(even, first, second), jnp.where(even, second, first)
    at = place(below.shape, ROWS, 0)

    def pick(count, shift_below, shift_above):
        low = pltpu.roll(below, shift_below, 0) if shift_below else below
        high = pltpu.roll(above, shift_above, 0) if shift_above else above
        return jnp.where(at < count, low, jnp.where(at >= ROWS - count, high, 0.0))

    return pick(4, 0, 0), pick(2, 4, 4), pick(2, 2, 6)


def turn_back(even, first, second):
    right, left = jnp.where(even, first, second), jnp.where(even, second, first)
    gap = jnp.zeros((LANES - 2 * ROWS, right.shape[1]), right.dtype)
    return jnp.concatenate([right, gap, left], axis=0).T


def col_halo(even, first, second):
    both = turn_back(even, first, second)
    lane = place(both.shape, LANES, 1)

    def pick(count, shift):
        low = pltpu.roll(both, LANES - shift, 1) if shift else both
        high = pltpu.roll(both, shift, 1) if shift else both
        return jnp.where(lane < count, low, jnp.where(lane >= LANES - count, high, 0.0))

    return pick(4, 0), pick(2, 4), pick(2, 6)


def dot(a, b):
    return jnp.dot(a, b, precision=HIGH, preferred_element_type=jnp.float32)


def join(tile, halo, axis):
    return jnp.concatenate([tile, halo], axis=axis)


def surface_kernel(
    shared, e_ref, p_ref, q_ref, c_ref, w_ref, even_ref, row0, row1, col0, col1,
    r_ref, cr_ref, left_ref, right_ref, s_ref, fp_ref, fq_ref, *part_refs,
):
    rows, cols = e_ref.shape
    e, p, q = e_ref[...], p_ref[...], q_ref[...]
    wet = w_ref[...] > 0
    slope, friction = coefficients(c_ref[...], w_ref[...])

    def twice(tile_flux, axis, halo):
        halo_e, halo_mass, halo_slope = halo
        grad = derive(join(e, halo_e, axis), axis)
        size = (rows, cols)[axis]
        inner = lax.slice_in_dim(grad, 0, size, axis=axis)
        outer = lax.slice_in_dim(grad, size, grad.shape[axis], axis=axis)
        total = 2.0 * tile_flux - (slope * inner + friction * tile_flux)
        halo_total = (2.0 - friction_of(halo_slope)) * halo_mass - halo_slope * outer
        ring = join(jnp.where(wet, total, 0.0), halo_total, axis)
        next_flux = tile_flux - 0.5 * friction * total
        return lax.slice_in_dim(derive(ring, axis), 0, size, axis=axis), next_flux

    change_x, fp_ref[...] = twice(p, 0, row_halo(even_ref[0] == 0, row0[...], row1[...]))
    change_y, fq_ref[...] = twice(q, 1, col_halo(even_ref[1] == 0, col0[...], col1[...]))
    s = e - jnp.where(wet, 0.125 * (change_x + change_y), 0.0)
    s_ref[...] = s
    ranged = dot(s, r_ref[...])
    coranged = dot(cr_ref[...], s)
    core = dot(left_ref[...], dot(s, right_ref[...]))
    if not shared:
        for ref, value in zip(part_refs, (ranged, coranged, core)):
            ref[...] = value
        return
    (out,) = part_refs
    at = 0
    for part in (core, ranged, coranged):
        for k, tile in enumerate(tiles_of(part)):
            per = tile_count(part) // out.shape[0]
            out[k // per, at + k % per] = tile
        at += per


def tile_count(part):
    return part.shape[0] // ROWS * (part.shape[1] // LANES)


def tile_slices(shape):
    return [
        (slice(i, i + ROWS), slice(j, j + LANES))
        for i in range(0, shape[0], ROWS)
        for j in range(0, shape[1], LANES)
    ]


def tiles_of(part):
    return [part[where] for where in tile_slices(part.shape)]


def sum_kernel(crosses, alongs, cuts, got, out):
    first, second, total = cuts
    count = crosses * alongs

    def add(values):
        values = list(values)
        while len(values) > 1:
            values = [sum(values[i : i + 2][1:], values[i]) for i in range(0, len(values), 2)]
        return values[0]

    for t in range(first):
        value = add(got[k, t] for k in range(count))
        for k in range(count):
            out[k, t] = value
    for t in range(first, second):
        for c in range(crosses):
            value = add(got[c * alongs + a, t] for a in range(alongs))
            for a in range(alongs):
                out[c * alongs + a, t] = value
    for t in range(second, total):
        for a in range(alongs):
            value = add(got[c * alongs + a, t] for c in range(crosses))
            for c in range(crosses):
                out[c * alongs + a, t] = value


def unpack_kernel(got, core, ranged, coranged):
    at = 0
    for ref in (core, ranged, coranged):
        per = tile_count(ref) // got.shape[0]
        for k, where in enumerate(tile_slices(ref.shape)):
            ref[where] = got[k // per, at + k % per]
        at += per


def strip_kernel(e_ref, p_ref, q_ref, w_ref, even_ref, row0, row1, col0, col1,
                 s_ref, both_ref, out_row0, out_row1, out_col0, out_col1):
    del s_ref
    rows, cols = e_ref.shape
    wet = w_ref[...] > 0
    _, mass_rows, _ = row_halo(even_ref[0] == 0, row0[...], row1[...])
    _, mass_cols, _ = col_halo(even_ref[1] == 0, col0[...], col1[...])
    mass_x = jnp.where(wet, p_ref[...], 0.0)
    mass_y = jnp.where(wet, q_ref[...], 0.0)
    spread = derive(join(mass_x, mass_rows, 0), 0)[:rows]
    spread += derive(join(mass_y, mass_cols, 1), 1)[:, :cols]
    both = 2.0 * e_ref[...] - jnp.where(wet, 0.25 * spread, 0.0)
    both_ref[...] = both
    up, down = both[:ROWS], both[rows - ROWS :]
    even = even_ref[0] == 0
    out_row0[...] = jnp.where(even, down, up)
    out_row1[...] = jnp.where(even, up, down)
    lane = place((rows, LANES), LANES, 1)
    turned = jnp.where(lane < LANES // 2, both[:, :LANES], both[:, cols - LANES :]).T
    to_left, to_right = turned[:ROWS], turned[LANES - ROWS :]
    even = even_ref[1] == 0
    out_col0[...] = jnp.where(even, to_right, to_left)
    out_col1[...] = jnp.where(even, to_left, to_right)


def flux_kernel(both_ref, fp_ref, fq_ref, c_ref, w_ref, even_ref, row0, row1, col0, col1,
                p_ref, q_ref):
    rows, cols = both_ref.shape
    both = both_ref[...]
    slope, _ = coefficients(c_ref[...], w_ref[...])
    halo_rows, _, _ = row_halo(even_ref[0] == 0, row0[...], row1[...])
    halo_cols, _, _ = col_halo(even_ref[1] == 0, col0[...], col1[...])
    p_ref[...] = fp_ref[...] - 0.5 * slope * derive(join(both, halo_rows, 0), 0)[:rows]
    q_ref[...] = fq_ref[...] - 0.5 * slope * derive(join(both, halo_cols, 1), 1)[:, :cols]


def exchange(messages):
    moved = []
    for axis, (first, second) in zip(AXES, (messages[:2], messages[2:])):
        count = lax.axis_size(axis)
        for start, message in ((0, first), (1, second)):
            pairs = [(i, i + 1) for i in range(start, count - 1, 2)]
            pairs += [(j, i) for i, j in pairs]
            moved.append(lax.ppermute(message, axis, pairs) if pairs else jnp.zeros_like(message))
    return moved


def body(e, p, q, c, w, range_test, corange_test, core_left, core_right):
    crosses, alongs = lax.axis_size("cross"), lax.axis_size("along")
    count = crosses * alongs
    rows, cols = e.shape
    even = jnp.stack([lax.rem(lax.axis_index(a), 2) for a in AXES])
    strip = [f32(ROWS, cols)] * 2 + [f32(ROWS, rows)] * 2

    def run(kernel, outs, flops, *args):
        kinds = [
            pl.BlockSpec(memory_space=pltpu.SMEM if a is even else pltpu.VMEM) for a in args
        ]
        moved = sum(a.size * a.dtype.itemsize for a in args) + sum(o.size * 4 for o in outs)
        return pl.pallas_call(
            kernel,
            out_shape=outs,
            in_specs=kinds,
            out_specs=[pl.BlockSpec(memory_space=pltpu.VMEM)] * len(outs),
            cost_estimate=pl.CostEstimate(flops=flops, bytes_accessed=moved, transcendentals=0),
            compiler_params=pltpu.CompilerParams(vmem_limit_bytes=32 * 1024 * 1024),
        )(*args)

    cells = rows * cols
    halo = exchange(run(pack_kernel, strip, cells, e, p, q, c, w, even))
    range_shape = f32(rows, range_test.shape[1])
    corange_shape = f32(corange_test.shape[0], cols)
    core_shape = f32(core_left.shape[0], core_right.shape[1])
    shapes = (core_shape, range_shape, corange_shape)
    shared = not any(s.size % (count * ROWS * LANES) for s in shapes)
    tile = f32(rows, cols)
    if shared:
        per = [tile_count(s) // count for s in shapes]
        cuts = (per[0], per[0] + per[1], sum(per))
        sheet = f32(count, cuts[2], ROWS, LANES)
        parts = [sheet]
    else:
        parts = [range_shape, corange_shape, core_shape]
    s_next, half_p, half_q, *parts = run(
        functools.partial(surface_kernel, shared), [tile] * 3 + parts, 800 * cells,
        e, p, q, c, w, even, *halo, range_test, corange_test, core_left, core_right,
    )
    if shared:
        got = lax.all_to_all(parts[0], AXES, 0, 0, tiled=True)
        (totals,) = run(
            functools.partial(sum_kernel, crosses, alongs, cuts), [sheet], sheet.size, got
        )
        handed = lax.all_to_all(totals, AXES, 0, 0, tiled=True)
        core, ranged, coranged = run(unpack_kernel, list(shapes), sheet.size, handed)
    else:
        ranged = lax.psum(parts[0], "along")
        coranged = lax.psum(parts[1], "cross")
        core = lax.psum(parts[2], AXES)
    both, *strips = run(
        strip_kernel, [tile] + strip, 20 * cells, e, p, q, w, even, *halo, s_next
    )
    strips = exchange(strips)
    p_next, q_next = run(
        flux_kernel, [tile] * 2, 20 * cells, both, half_p, half_q, c, w, even, *strips
    )
    return s_next, p_next, q_next, ranged, coranged, core


def solution(mesh):
    tile = P("cross", "along")
    return jax.shard_map(
        body,
        mesh=mesh,
        in_specs=(tile,) * 5
        + (P("along", None), P(None, "cross"), P(None, "cross"), P("along", None)),
        out_specs=(tile,) * 3 + (P("cross", None), P(None, "along"), P()),
        check_vma=False,
    )
```

time: 173 us -> 64 us (0.37)
  waiting for transfers between devices: 121 us -> 10.7 us
  blocking collectives: 0 us -> 27.7 us
  between operations: 14.3 us -> 0.81 us
  starting transfers between devices: 20.7 us -> 10.4 us
  Pallas kernels: 0 us -> 9.13 us
  matrix products: 5.61 us -> 0 us
  other arithmetic: 5.5 us -> 0.08 us
    psum x2 -> x0, waiting for transfers between devices: 104 us -> none  [the longest x1 73 us: body(): range_sketch, right_rows = lax.psum((range_part, right_part), 'along')]
    all_to_all x0 -> x1, blocking collectives: none -> 27.7 us  [body(): got = lax.all_to_all(parts[0], AXES, 0, 0, tiled=True)]
    ppermute x8, waiting for transfers between devices: 16.3 us -> 2.26 us  [exchange(): lax.ppermute(message, axis, pairs)]
    ppermute x8, starting transfers between devices: 20.6 us -> 7.65 us  [exchange(): lax.ppermute(message, axis, pairs)]
    pallas_call x0 -> x6, Pallas kernels: none -> 9.13 us  [run(): pl.pallas_call(kernel, out_shape=outs, in_specs=kinds, out_specs=[pl.Bloc...]
    all_to_all x0 -> x1, waiting for transfers between devices: none -> 8.4 us  [body(): handed = lax.all_to_all(totals, AXES, 0, 0, tiled=True)]
    dot_general x4 -> x0, matrix products: 5.61 us -> none  [the longest x1 2.25 us: body(): jnp.dot(core_left, right_rows, precision=high, preferred_element_type=jnp...]
    all_to_all x0 -> x1, starting transfers between devices: none -> 2.75 us  [body(): handed = lax.all_to_all(totals, AXES, 0, 0, tiled=True)]
  transfers between devices with their start and end apart: 10 -> 9, of which waited for: 6 -> 3; matrix products, arithmetic and copies ran while one was open for 2% -> 0% of each run, Pallas kernels for 0% -> 5%
where the time goes in v2:
time: 64 us; the launch traced here: 63.6 us
  blocking collectives  27.7 us (43%)
  waiting for transfers between devices  10.7 us (17%)
  starting transfers between devices  10.4 us (16%)
  Pallas kernels  9.13 us (14%)
  local copies, waits for them, and re-layouts  4.79 us (7%)
  between operations  0.81 us (1%)
    all_to_all x1, blocking collectives, body(): got = lax.all_to_all(parts[0], AXES, 0, 0, tiled=True)  27.7 us
    pallas_call x6, Pallas kernels, run(): pl.pallas_call(kernel, out_shape=outs, in_specs=kinds, out_specs=[pl.Bloc...  9.13 us
    all_to_all x1, waiting for transfers between devices, body(): handed = lax.all_to_all(totals, AXES, 0, 0, tiled=True)  8.4 us
    ppermute x8, starting transfers between devices, exchange(): lax.ppermute(message, axis, pairs)  7.65 us
    unnamed x30, local copies, waits for them, and re-layouts  4.79 us
    all_to_all x1, starting transfers between devices, body(): handed = lax.all_to_all(totals, AXES, 0, 0, tiled=True)  2.75 us
    ppermute x8, waiting for transfers between devices, exchange(): lax.ppermute(message, axis, pairs)  2.26 us
  transfers between devices with their start and end apart: 9, of which 3 were waited for; matrix products, arithmetic and copies ran while one was open for 0% of the time, Pallas kernels for 5%

profile of v2, /device:TPU:0, one launch (start us, length us, event | category | flops | bytes accessed | tf_op | source)
XLA Modules:
  0.0 63.6 jit_solution(712708985012231914)
XLA Ops:
  0.6 0.1 pad_add_fusion.even_ref
  0.7 0.9 %copy-done = s32[256,256]{1,0:T(8,128)S(1)} copy-done((s32[256,256]{1,0:T(8,128)S(1)}, s32[256,256]{1,0:T(8,128)}, u32[]{:S(2)}) %copy-start) | copy-done | bytes 262168
  1.7 0.9 %copy-done.2 = f32[256,256]{1,0:T(8,128)S(1)} copy-done((f32[256,256]{1,0:T(8,128)S(1)}, f32[256,256]{1,0:T(8,128)}, u32[]{:S(2)}) %copy-start.2) | copy-done | bytes 262168
  2.6 0.9 %copy-done.4 = f32[256,256]{1,0:T(8,128)S(1)} copy-done((f32[256,256]{1,0:T(8,128)S(1)}, f32[256,256]{1,0:T(8,128)}, u32[]{:S(2)}) %copy-start.4) | copy-done | bytes 262168
  3.6 0.9 %copy-done.6 = f32[256,256]{1,0:T(8,128)S(1)} copy-done((f32[256,256]{1,0:T(8,128)S(1)}, f32[256,256]{1,0:T(8,128)}, u32[]{:S(2)}) %copy-start.6) | copy-done | bytes 262168
  4.5 0.9 %copy-done.8 = f32[256,256]{1,0:T(8,128)S(1)} copy-done((f32[256,256]{1,0:T(8,128)S(1)}, f32[256,256]{1,0:T(8,128)}, u32[]{:S(2)}) %copy-start.8) | copy-done | bytes 262168
  5.5 0.8 %shard_map.136 = (f32[8,256]{1,0:T(8,128)S(1)}, f32[8,256]{1,0:T(8,128)S(1)}, f32[8,256]{1,0:T(8,128)S(1)}, f32[8,256]{1,0:T(8,128)S(1)}) custom-call(f32[256,256]{1,0:T(8,128)S(1)} %copy-done.2, f32[256,256]{1,0:T(8,128)S(1)} %copy-done.4, f32[256,256]{1,0:T(8,128)S(1)} %copy-done.6, f32[256,256]{1,0:T(8,128)S(1)} %copy-done.8, s32[256,256]{1,0:T(8,128)S(1)} %copy-done, ...), custom_call_target="tpu_custom_call" | custom-call | flops 65536 | bytes 1343496 | tf_op jit(solution)/shard_map/pallas_call | solution.py:273
  6.3 0.5 collective-permute-start
  6.8 0.6 %collective-permute-start.1 = (f32[8,256]{1,0:T(8,128)S(1)}, f32[8,256]{1,0:T(8,128)S(1)}, u32[]{:S(2)}, u32[]{:S(2)}) collective-permute-start(f32[8,256]{1,0:T(8,128)S(1)} %get-tuple-element.25), channel_id=1, source_target_pairs={{8,16},{16,8},{9,17},{17,9},{10,18},{18,10},{11,19},{19,11},{12,20... | collective-permute-start | bytes 24584 | tf_op jit(solution)/shard_map/ppermute | solution.py:257
  7.5 2.6 %collective-permute-start.2 = (f32[8,256]{1,0:T(8,128)S(1)}, f32[8,256]{1,0:T(8,128)S(1)}, u32[]{:S(2)}, u32[]{:S(2)}) collective-permute-start(f32[8,256]{1,0:T(8,128)S(1)} %get-tuple-element.26), channel_id=1, source_target_pairs={{0,1},{2,3},{4,5},{6,7},{1,0},{3,2},{5,4},{7,6},{8,9},{10,11},{12,... | collective-permute-start | bytes 24584 | tf_op jit(solution)/shard_map/ppermute | solution.py:257
  10.1 0.6 %collective-permute-start.3 = (f32[8,256]{1,0:T(8,128)S(1)}, f32[8,256]{1,0:T(8,128)S(1)}, u32[]{:S(2)}, u32[]{:S(2)}) collective-permute-start(f32[8,256]{1,0:T(8,128)S(1)} %get-tuple-element.27), channel_id=1, source_target_pairs={{1,2},{3,4},{5,6},{2,1},{4,3},{6,5},{9,10},{11,12},{13,14},{10,9},... | collective-permute-start | bytes 24584 | tf_op jit(solution)/shard_map/ppermute | solution.py:257
  10.7 0.0 collective-permute-done.row0
  10.7 0.0 collective-permute-done.1.row1
  10.7 1.0 %collective-permute-done.2.col0 = f32[8,256]{1,0:T(8,128)S(1)} collective-permute-done((f32[8,256]{1,0:T(8,128)S(1)}, f32[8,256]{1,0:T(8,128)S(1)}, u32[]{:S(2)}, u32[]{:S(2)}) %collective-permute-start.2) | collective-permute-done | bytes 8224 | tf_op jit(solution)/shard_map/ppermute | solution.py:257
  11.7 0.0 collective-permute-done.3.col1
  11.7 3.3 %shard_map.137 = (f32[256,256]{1,0:T(8,128)}, f32[256,256]{1,0:T(8,128)S(1)}, f32[256,256]{1,0:T(8,128)S(1)}, f32[32,4,8,128]{3,2,1,0:T(8,128)S(1)}) custom-call(f32[256,256]{1,0:T(8,128)S(1)} %copy-done.2, f32[256,256]{1,0:T(8,128)S(1)} %copy-done.4, f32[256,256]{1,0:T(8,128)S(1)} %copy-done.6, f32[256,256]{1,0:T(8,128)S(1)} %copy-done.8, ...), custom_call_target="tpu_custom_call" | custom-call | flops 52428800 | bytes 3440648 | tf_op jit(solution)/shard_map/pallas_call | solution.py:273
  15.0 27.7 %all_to_all.10.got = f32[32,4,8,128]{3,2,1,0:T(8,128)S(1)} all-to-all(f32[32,4,8,128]{3,2,1,0:T(8,128)S(1)} %get-tuple-element.38), channel_id=1, replica_groups=mesh['cross'=4,'along'=8] {'cross','along'}, dimensions={0} | all-to-all | bytes 1048576 | tf_op jit(solution)/shard_map/all_to_all | solution.py:302
  42.7 0.9 %shard_map.140 = f32[32,4,8,128]{3,2,1,0:T(8,128)} custom-call(f32[32,4,8,128]{3,2,1,0:T(8,128)S(1)} %all_to_all.10.got), custom_call_target="tpu_custom_call" | custom-call | flops 131072 | bytes 1048576 | tf_op jit(solution)/shard_map/pallas_call | solution.py:273
  43.6 2.8 %all-to-all-start.1 = ((f32[32,4,8,128]{3,2,1,0:T(8,128)}), f32[32,4,8,128]{3,2,1,0:T(8,128)S(1)}, u32[]{:S(2)}, u32[]{:S(2)}) async-start(f32[32,4,8,128]{3,2,1,0:T(8,128)} %shard_map.140), calls=%async_computation.1 | async-start | bytes 1048576 | tf_op jit(solution)/shard_map/all_to_all | solution.py:306
  46.4 0.0 copy-start.9
  46.5 1.3 %shard_map.138 = (f32[256,256]{1,0:T(8,128)S(1)}, f32[8,256]{1,0:T(8,128)S(1)}, f32[8,256]{1,0:T(8,128)S(1)}, f32[8,256]{1,0:T(8,128)S(1)}, f32[8,256]{1,0:T(8,128)S(1)}) custom-call(f32[256,256]{1,0:T(8,128)S(1)} %copy-done.3, f32[256,256]{1,0:T(8,128)S(1)} %copy-done.5, f32[256,256]{1,0:T(8,128)S(1)} %copy-done.7, s32[256,256]{1,0:T(8,128)S(1)} %copy-done.1, ...), custom_call_target="tpu_custom_call" | custom-call | flops 1310720 | bytes 1638408 | tf_op jit(solution)/shard_map/pallas_call | solution.py:273
  47.8 0.2 collective-permute-start.4
  48.0 0.6 %collective-permute-start.5 = (f32[8,256]{1,0:T(8,128)S(1)}, f32[8,256]{1,0:T(8,128)S(1)}, u32[]{:S(2)}, u32[]{:S(2)}) collective-permute-start(f32[8,256]{1,0:T(8,128)S(1)} %get-tuple-element.33), channel_id=1, source_target_pairs={{8,16},{16,8},{9,17},{17,9},{10,18},{18,10},{11,19},{19,11},{12,20... | collective-permute-start | bytes 24584 | tf_op jit(solution)/shard_map/ppermute | solution.py:257
  48.6 1.8 %collective-permute-start.6 = (f32[8,256]{1,0:T(8,128)S(1)}, f32[8,256]{1,0:T(8,128)S(1)}, u32[]{:S(2)}, u32[]{:S(2)}) collective-permute-start(f32[8,256]{1,0:T(8,128)S(1)} %get-tuple-element.34), channel_id=1, source_target_pairs={{0,1},{2,3},{4,5},{6,7},{1,0},{3,2},{5,4},{7,6},{8,9},{10,11},{12,... | collective-permute-start | bytes 24584 | tf_op jit(solution)/shard_map/ppermute | solution.py:257
  50.4 0.6 %collective-permute-start.7 = (f32[8,256]{1,0:T(8,128)S(1)}, f32[8,256]{1,0:T(8,128)S(1)}, u32[]{:S(2)}, u32[]{:S(2)}) collective-permute-start(f32[8,256]{1,0:T(8,128)S(1)} %get-tuple-element.35), channel_id=1, source_target_pairs={{1,2},{3,4},{5,6},{2,1},{4,3},{6,5},{9,10},{11,12},{13,14},{10,9},... | collective-permute-start | bytes 24584 | tf_op jit(solution)/shard_map/ppermute | solution.py:257
  51.1 0.0 collective-permute-done.4.row0
  51.1 0.0 collective-permute-done.5.row1
  51.1 1.3 %collective-permute-done.6.col0 = f32[8,256]{1,0:T(8,128)S(1)} collective-permute-done((f32[8,256]{1,0:T(8,128)S(1)}, f32[8,256]{1,0:T(8,128)S(1)}, u32[]{:S(2)}, u32[]{:S(2)}) %collective-permute-start.6) | collective-permute-done | bytes 8224 | tf_op jit(solution)/shard_map/ppermute | solution.py:257
  52.4 0.0 collective-permute-done.7.col1
  52.4 2.0 %shard_map.139 = (f32[256,256]{1,0:T(8,128)}, f32[256,256]{1,0:T(8,128)}) custom-call(f32[256,256]{1,0:T(8,128)S(1)} %get-tuple-element.29.both_ref, f32[256,256]{1,0:T(8,128)S(1)} %get-tuple-element.30.fp_ref, f32[256,256]{1,0:T(8,128)S(1)} %get-tuple-element.31.fq_ref, f32[256,256]{1,0:T(8,128)S(1)} %copy-done.9, s32[256,256]{1,0:T(8,128)S(1)} %copy-done.1, ...), custom_call_target="tpu_custom_call" | custom-call | flops 1310720 | bytes 1867784 | tf_op jit(solution)/shard_map/pallas_call | solution.py:273
  54.4 8.4 %all-to-all-done.1.got = f32[32,4,8,128]{3,2,1,0:T(8,128)S(1)} async-done(((f32[32,4,8,128]{3,2,1,0:T(8,128)}), f32[32,4,8,128]{3,2,1,0:T(8,128)S(1)}, u32[]{:S(2)}, u32[]{:S(2)}) %all-to-all-start.1) | async-done | bytes 524320 | tf_op jit(solution)/shard_map/all_to_all | solution.py:306
  62.7 0.8 %shard_map.141 = (f32[256,256]{1,0:T(8,128)}, f32[256,128]{1,0:T(8,128)}, f32[128,256]{1,0:T(8,128)}) custom-call(f32[32,4,8,128]{3,2,1,0:T(8,128)S(1)} %all-to-all-done.1.got), custom_call_target="tpu_custom_call" | custom-call | flops 131072 | bytes 1048576 | tf_op jit(solution)/shard_map/pallas_call | solution.py:273
  (24 shorter events, 0.0 us)
Async XLA Ops:
  0.7 1.0 %copy-start = (s32[256,256]{1,0:T(8,128)S(1)}, s32[256,256]{1,0:T(8,128)}, u32[]{:S(2)}) copy-start(s32[256,256]{1,0:T(8,128)} %w_ref.7) | copy-start | bytes 786436
  1.7 0.9 %copy-start.2 = (f32[256,256]{1,0:T(8,128)S(1)}, f32[256,256]{1,0:T(8,128)}, u32[]{:S(2)}) copy-start(f32[256,256]{1,0:T(8,128)} %e_ref.5) | copy-start | bytes 786436
  2.6 0.9 %copy-start.4 = (f32[256,256]{1,0:T(8,128)S(1)}, f32[256,256]{1,0:T(8,128)}, u32[]{:S(2)}) copy-start(f32[256,256]{1,0:T(8,128)} %p_ref.5) | copy-start | bytes 786436
  3.6 0.9 %copy-start.6 = (f32[256,256]{1,0:T(8,128)S(1)}, f32[256,256]{1,0:T(8,128)}, u32[]{:S(2)}) copy-start(f32[256,256]{1,0:T(8,128)} %q_ref.5) | copy-start | bytes 786436
  4.5 0.9 %copy-start.8 = (f32[256,256]{1,0:T(8,128)S(1)}, f32[256,256]{1,0:T(8,128)}, u32[]{:S(2)}) copy-start(f32[256,256]{1,0:T(8,128)} %c_ref.5) | copy-start | bytes 786436
  5.5 6.2 %copy-start.10 = (f32[256,256]{1,0:T(8,128)S(1)}, f32[256,256]{1,0:T(8,128)}, u32[]{:S(2)}) copy-start(f32[256,256]{1,0:T(8,128)} %left_ref.1) | copy-start | bytes 786436
  5.5 6.2 %copy-start.11 = (f32[256,256]{1,0:T(8,128)S(1)}, f32[256,256]{1,0:T(8,128)}, u32[]{:S(2)}) copy-start(f32[256,256]{1,0:T(8,128)} %right_ref.1) | copy-start | bytes 786436
  5.5 6.2 %copy-start.13 = (f32[256,128]{1,0:T(8,128)S(1)}, f32[256,128]{1,0:T(8,128)}, u32[]{:S(2)}) copy-start(f32[256,128]{1,0:T(8,128)} %r_ref.1) | copy-start | bytes 393220
  5.5 6.2 %copy-start.14 = (f32[128,256]{1,0:T(8,128)S(1)}, f32[128,256]{1,0:T(8,128)}, u32[]{:S(2)}) copy-start(f32[128,256]{1,0:T(8,128)} %cr_ref.1) | copy-start | bytes 393220
  6.3 4.4 %collective-permute-start = (f32[8,256]{1,0:T(8,128)S(1)}, f32[8,256]{1,0:T(8,128)S(1)}, u32[]{:S(2)}, u32[]{:S(2)}) collective-permute-start(f32[8,256]{1,0:T(8,128)S(1)} %get-tuple-element.24), channel_id=1, source_target_pairs={{0,8},{16,24},{8,0},{24,16},{1,9},{17,25},{9,1},{25,17},{2,10},{18... | collective-permute-start | bytes 24584 | tf_op jit(solution)/shard_map/ppermute | solution.py:257
  6.8 3.9 %collective-permute-start.1 = (f32[8,256]{1,0:T(8,128)S(1)}, f32[8,256]{1,0:T(8,128)S(1)}, u32[]{:S(2)}, u32[]{:S(2)}) collective-permute-start(f32[8,256]{1,0:T(8,128)S(1)} %get-tuple-element.25), channel_id=1, source_target_pairs={{8,16},{16,8},{9,17},{17,9},{10,18},{18,10},{11,19},{19,11},{12,20... | collective-permute-start | bytes 24584 | tf_op jit(solution)/shard_map/ppermute | solution.py:257
  7.5 4.2 %collective-permute-start.2 = (f32[8,256]{1,0:T(8,128)S(1)}, f32[8,256]{1,0:T(8,128)S(1)}, u32[]{:S(2)}, u32[]{:S(2)}) collective-permute-start(f32[8,256]{1,0:T(8,128)S(1)} %get-tuple-element.26), channel_id=1, source_target_pairs={{0,1},{2,3},{4,5},{6,7},{1,0},{3,2},{5,4},{7,6},{8,9},{10,11},{12,... | collective-permute-start | bytes 24584 | tf_op jit(solution)/shard_map/ppermute | solution.py:257
  10.1 1.6 %collective-permute-start.3 = (f32[8,256]{1,0:T(8,128)S(1)}, f32[8,256]{1,0:T(8,128)S(1)}, u32[]{:S(2)}, u32[]{:S(2)}) collective-permute-start(f32[8,256]{1,0:T(8,128)S(1)} %get-tuple-element.27), channel_id=1, source_target_pairs={{1,2},{3,4},{5,6},{2,1},{4,3},{6,5},{9,10},{11,12},{13,14},{10,9},... | collective-permute-start | bytes 24584 | tf_op jit(solution)/shard_map/ppermute | solution.py:257
  42.7 3.7 %copy-start.12 = (f32[256,256]{1,0:T(8,128)S(1)}, f32[256,256]{1,0:T(8,128)}, u32[]{:S(2)}) copy-start(f32[256,256]{1,0:T(8,128)} %get-tuple-element.18.s_ref) | copy-start | bytes 786436
  43.6 2.8 %copy-start.1 = (s32[256,256]{1,0:T(8,128)S(1)}, s32[256,256]{1,0:T(8,128)}, u32[]{:S(2)}) copy-start(s32[256,256]{1,0:T(8,128)} %w_ref.7) | copy-start | bytes 786436
  43.6 2.8 %copy-start.3 = (f32[256,256]{1,0:T(8,128)S(1)}, f32[256,256]{1,0:T(8,128)}, u32[]{:S(2)}) copy-start(f32[256,256]{1,0:T(8,128)} %e_ref.5) | copy-start | bytes 786436
  43.6 2.8 %copy-start.5 = (f32[256,256]{1,0:T(8,128)S(1)}, f32[256,256]{1,0:T(8,128)}, u32[]{:S(2)}) copy-start(f32[256,256]{1,0:T(8,128)} %p_ref.5) | copy-start | bytes 786436
  43.6 2.8 %copy-start.7 = (f32[256,256]{1,0:T(8,128)S(1)}, f32[256,256]{1,0:T(8,128)}, u32[]{:S(2)}) copy-start(f32[256,256]{1,0:T(8,128)} %q_ref.5) | copy-start | bytes 786436
  43.6 19.1 %all-to-all-start.1 = ((f32[32,4,8,128]{3,2,1,0:T(8,128)}), f32[32,4,8,128]{3,2,1,0:T(8,128)S(1)}, u32[]{:S(2)}, u32[]{:S(2)}) async-start(f32[32,4,8,128]{3,2,1,0:T(8,128)} %shard_map.140), calls=%async_computation.1 | async-start | bytes 1048576 | tf_op jit(solution)/shard_map/all_to_all | solution.py:306
  46.4 5.9 %copy-start.9 = (f32[256,256]{1,0:T(8,128)S(1)}, f32[256,256]{1,0:T(8,128)}, u32[]{:S(2)}) copy-start(f32[256,256]{1,0:T(8,128)} %c_ref.5) | copy-start | bytes 786436
  47.8 3.3 %collective-permute-start.4 = (f32[8,256]{1,0:T(8,128)S(1)}, f32[8,256]{1,0:T(8,128)S(1)}, u32[]{:S(2)}, u32[]{:S(2)}) collective-permute-start(f32[8,256]{1,0:T(8,128)S(1)} %get-tuple-element.32), channel_id=1, source_target_pairs={{0,8},{16,24},{8,0},{24,16},{1,9},{17,25},{9,1},{25,17},{2,10},{18... | collective-permute-start | bytes 24584 | tf_op jit(solution)/shard_map/ppermute | solution.py:257
  48.0 3.1 %collective-permute-start.5 = (f32[8,256]{1,0:T(8,128)S(1)}, f32[8,256]{1,0:T(8,128)S(1)}, u32[]{:S(2)}, u32[]{:S(2)}) collective-permute-start(f32[8,256]{1,0:T(8,128)S(1)} %get-tuple-element.33), channel_id=1, source_target_pairs={{8,16},{16,8},{9,17},{17,9},{10,18},{18,10},{11,19},{19,11},{12,20... | collective-permute-start | bytes 24584 | tf_op jit(solution)/shard_map/ppermute | solution.py:257
  48.6 3.7 %collective-permute-start.6 = (f32[8,256]{1,0:T(8,128)S(1)}, f32[8,256]{1,0:T(8,128)S(1)}, u32[]{:S(2)}, u32[]{:S(2)}) collective-permute-start(f32[8,256]{1,0:T(8,128)S(1)} %get-tuple-element.34), channel_id=1, source_target_pairs={{0,1},{2,3},{4,5},{6,7},{1,0},{3,2},{5,4},{7,6},{8,9},{10,11},{12,... | collective-permute-start | bytes 24584 | tf_op jit(solution)/shard_map/ppermute | solution.py:257
  50.4 2.0 %collective-permute-start.7 = (f32[8,256]{1,0:T(8,128)S(1)}, f32[8,256]{1,0:T(8,128)S(1)}, u32[]{:S(2)}, u32[]{:S(2)}) collective-permute-start(f32[8,256]{1,0:T(8,128)S(1)} %get-tuple-element.35), channel_id=1, source_target_pairs={{1,2},{3,4},{5,6},{2,1},{4,3},{6,5},{9,10},{11,12},{13,14},{10,9},... | collective-permute-start | bytes 24584 | tf_op jit(solution)/shard_map/ppermute | solution.py:257

commit v3 on v2

v3 whole, which is shorter than its diff:
```python
import functools

import jax
import jax.numpy as jnp
from jax import lax
from jax.experimental import pallas as pl
from jax.experimental.pallas import tpu as pltpu
from jax.sharding import PartitionSpec as P

AXES = ("cross", "along")
ROWS = 8
LANES = 128
HIGH = lax.Precision.HIGHEST


def f32(*shape):
    return jax.ShapeDtypeStruct(shape, jnp.float32)


def derive(field, axis):
    size = field.shape[axis]

    def part(shift):
        return pltpu.roll(field, (-shift) % size, axis)

    return (part(1) - part(-1)) * (8.0 / 12.0) - (part(2) - part(-2)) * (1.0 / 12.0)


def friction_of(slope):
    wet = slope > 0.0
    return jnp.where(wet, 0.005 / jnp.where(wet, slope, 1.0), 0.0)


def place(shape, axis, dim):
    return lax.broadcasted_iota(jnp.int32, shape, dim)


def pack_kernel(e_ref, p_ref, q_ref, a_ref, even_ref, row0, row1, col0, col1):
    rows, cols = e_ref.shape
    at = place((ROWS, cols), ROWS, 0)
    messages = []
    for i, (far, near, turn) in enumerate(((at < 4, at < 6, 6), (at >= 4, at >= 2, 2))):
        here = pl.ds(i * (rows - ROWS), ROWS)
        slope, mass, side = a_ref[here, :], p_ref[here, :], q_ref[here, :]
        first = jnp.where(near, pltpu.roll(mass, 4, 0), pltpu.roll(slope, turn, 0))
        first = jnp.where(far, e_ref[here, :], first)
        messages.append(join(first, jnp.where(far, mass, pltpu.roll(side, 4, 0)), 0))
    up, down = messages
    even = even_ref[0] == 0
    row0[...] = jnp.where(even, down, up)
    row1[...] = jnp.where(even, up, down)
    lane = place((rows, LANES), LANES, 1)
    left = lane < LANES // 2
    off = jnp.minimum(lane, LANES - 1 - lane)

    def edge(ref):
        return jnp.where(left, ref[:, :LANES], ref[:, cols - LANES :])

    def shift(block, count):
        return jnp.where(left, pltpu.roll(block, count, 1), pltpu.roll(block, LANES - count, 1))

    slope, mass, side = edge(a_ref), edge(q_ref), edge(p_ref)
    first = jnp.where(off < 4, edge(e_ref), jnp.where(off < 6, shift(mass, 4), shift(slope, 6))).T
    second = jnp.where(off < 4, mass, shift(side, 4)).T
    to_left = join(first[:ROWS], second[:ROWS], 0)
    to_right = join(first[LANES - ROWS :], second[LANES - ROWS :], 0)
    even = even_ref[1] == 0
    col0[...] = jnp.where(even, to_right, to_left)
    col1[...] = jnp.where(even, to_left, to_right)


def row_pick(even, first, second):
    below, above = jnp.where(even, first, second), jnp.where(even, second, first)
    at = place(below.shape, ROWS, 0)

    def pick(count, shift):
        low = pltpu.roll(below, ROWS - shift, 0) if shift else below
        high = pltpu.roll(above, shift, 0) if shift else above
        return jnp.where(at < count, low, jnp.where(at >= ROWS - count, high, 0.0))

    return pick


def col_pick(even, first, second):
    right, left = jnp.where(even, first, second), jnp.where(even, second, first)
    gap = jnp.zeros((LANES - 2 * ROWS, right.shape[1]), right.dtype)
    both = jnp.concatenate([right, gap, left], axis=0).T
    lane = place(both.shape, LANES, 1)

    def pick(count, shift):
        low = pltpu.roll(both, LANES - shift, 1) if shift else both
        high = pltpu.roll(both, shift, 1) if shift else both
        return jnp.where(lane < count, low, jnp.where(lane >= LANES - count, high, 0.0))

    return pick


def dot(a, b):
    return jnp.dot(a, b, precision=HIGH, preferred_element_type=jnp.float32)


def join(tile, halo, axis):
    return jnp.concatenate([tile, halo], axis=axis)


def surface_kernel(
    e_ref, p_ref, q_ref, a_ref, f_ref, even_ref, row0, row1, col0, col1,
    cr_ref, left_ref, right_ref, s_hbm, s_ref, product_ref, give_ref, corner_ref, sems,
):
    rows, cols = e_ref.shape
    twice_e, slope, friction = e_ref[...], a_ref[...], f_ref[...]

    def change(mass, axis, halo):
        halo_e, halo_mass, halo_slope = halo
        grad = 0.5 * derive(join(twice_e, halo_e, axis), axis)
        size = (rows, cols)[axis]
        inner = lax.slice_in_dim(grad, 0, size, axis=axis)
        outer = lax.slice_in_dim(grad, size, grad.shape[axis], axis=axis)
        total = (2.0 - friction) * mass - slope * inner
        halo_total = (2.0 - friction_of(halo_slope)) * halo_mass - halo_slope * outer
        ring = join(total, halo_total, axis)
        return lax.slice_in_dim(derive(ring, axis), 0, size, axis=axis)

    def halo(pick):
        return pick(4, 0), pick(2, 4), pick(2, 6)

    even_row, even_col = even_ref[0] == 0, even_ref[1] == 0
    pick = row_pick(even_row, row0[:ROWS], row1[:ROWS])
    change_x = change(p_ref[...], 0, halo(pick))
    pick = col_pick(even_col, col0[:ROWS], col1[:ROWS])
    change_y = change(q_ref[...], 1, halo(pick))
    spread = jnp.where(slope > 0.0, 0.125 * (change_x + change_y), 0.0)
    s_ref[...] = 0.5 * twice_e - spread
    part = rows // 4
    copies = [
        pltpu.make_async_copy(s_ref.at[pl.ds(i * part, part), :], s_hbm.at[pl.ds(i * part, part), :], sems.at[i])
        for i in range(4)
    ]
    for copy in copies:
        copy.start()
    s = s_ref[...]
    pick = col_pick(even_col, col0[ROWS:], col1[ROWS:])
    around = join(pick(4, 0), pick(2, 4), 1)
    up, down = around[:ROWS], around[rows - ROWS :]
    give_ref[give_ref.shape[0] - ROWS :, :] = jnp.where(even_row, down, up)
    corner_ref[...] = jnp.where(even_row, up, down)
    product = dot(s, right_ref[...])
    product_ref[...] = product
    give_ref[: give_ref.shape[0] - ROWS, :] = halves(1 - even_ref[0], left_ref, product, cr_ref, s)
    for copy in copies:
        copy.wait()


def halves(side, left_ref, product, cr_ref, s):
    half, thin = left_ref.shape[0] // 2, cr_ref.shape[0] // 2
    core = dot(left_ref[pl.ds(pl.multiple_of(side * half, half), half), :], product)
    coranged = dot(cr_ref[pl.ds(pl.multiple_of(side * thin, thin), thin), :], s)
    return join(core, coranged, 0)


def product_kernel(s_ref, product_ref, even_ref, r_ref, cr_ref, left_ref, keep_ref, range_ref):
    keep_ref[...] = halves(even_ref[0], left_ref, product_ref[...], cr_ref, s_ref[...])
    range_ref[...] = dot(s_ref[...], r_ref[...])


def merge_kernel(half, keep_ref, got_ref, range_ref, out):
    both = keep_ref[...] + got_ref[: keep_ref.shape[0]]
    at = 0
    for part in (both[:half], range_ref[...], both[half:]):
        per = tile_count(part) // out.shape[0]
        for k, tile in enumerate(tiles_of(part)):
            out[k // per, at + k % per] = tile
        at += per


def tile_count(part):
    return part.shape[0] // ROWS * (part.shape[1] // LANES)


def tile_slices(shape):
    return [
        (slice(i, i + ROWS), slice(j, j + LANES))
        for i in range(0, shape[0], ROWS)
        for j in range(0, shape[1], LANES)
    ]


def tiles_of(part):
    return [part[where] for where in tile_slices(part.shape)]


def sum_kernel(crosses, alongs, cuts, got, *rest):
    out = rest[-1]
    first, second, total = cuts
    count = crosses * alongs

    def add(values):
        values = list(values)
        while len(values) > 1:
            values = [sum(values[i : i + 2][1:], values[i]) for i in range(0, len(values), 2)]
        return values[0]

    for t in range(first):
        value = add(got[k, t] for k in range(count))
        for k in range(count):
            out[k, t] = value
    for t in range(first, second):
        for c in range(crosses):
            value = add(got[c * alongs + a, t] for a in range(alongs))
            for a in range(alongs):
                out[c * alongs + a, t] = value
    for t in range(second, total):
        for a in range(alongs):
            value = add(got[c * alongs + a, t] for c in range(crosses))
            for c in range(crosses):
                out[c * alongs + a, t] = value


def unpack_kernel(even_ref, mine, theirs, *refs):
    outs, held, sems = refs[:3], refs[3:6], refs[6]
    count = mine.shape[0]
    even = even_ref[0] == 0
    at = 0
    copies = []
    for out, ref, halved in zip(outs, held, (True, False, True)):
        places = tile_slices(ref.shape)
        keep = len(places) // 2 if halved else len(places)
        per = keep // count
        for k in range(keep):
            tile = mine[k // per, at + k % per]
            if halved:
                other = theirs[k // per, at + k % per]
                ref[places[k]] = jnp.where(even, tile, other)
                ref[places[keep + k]] = jnp.where(even, other, tile)
            else:
                ref[places[k]] = tile
        at += per
        part = ref.shape[0] // 4
        for i in range(0, ref.shape[0], part):
            block = pl.ds(i, part)
            copy = pltpu.make_async_copy(
                ref.at[block, :], out.at[block, :], sems.at[len(copies)]
            )
            copy.start()
            copies.append(copy)
    for copy in copies:
        copy.wait()


def flux_kernel(
    e_ref, mp_ref, mq_ref, a_ref, f_ref, even_ref, row0, row1, col0, col1, got_ref, corner_ref,
    p_ref, q_ref, next_p, next_q, token,
):
    rows, cols = e_ref.shape
    token[...] = jnp.zeros(token.shape, token.dtype)
    twice_e, slope, friction = e_ref[...], a_ref[...], f_ref[...]
    wet = slope > 0.0
    even_row, even_col = even_ref[0] == 0, even_ref[1] == 0
    pick = row_pick(even_row, row0[:ROWS], row1[:ROWS])
    e_rows, wet_rows = pick(4, 0), pick(2, 6) > 0.0
    pick = row_pick(even_row, row0[ROWS:], row1[ROWS:])
    p_rows, q_rows = pick(4, 0), pick(2, 4)
    pick = col_pick(even_col, col0[:ROWS], col1[:ROWS])
    e_cols, wet_cols = pick(4, 0), pick(2, 6) > 0.0
    pick = col_pick(even_col, col0[ROWS:], col1[ROWS:])
    q_cols, p_cols = pick(4, 0), pick(2, 4)
    pick = row_pick(even_row, got_ref[got_ref.shape[0] - ROWS :], corner_ref[...])
    corners = pick(2, 0)
    q_corner, p_corner = corners[:, :LANES], corners[:, LANES:]
    mass_x, mass_y = mp_ref[...], mq_ref[...]
    spread_x = derive(join(mass_x, p_rows, 0), 0)
    spread_y = derive(join(mass_y, q_cols, 1), 1)
    both = twice_e - jnp.where(wet, 0.25 * (spread_x[:rows] + spread_y[:, :cols]), 0.0)
    spread = spread_x[rows:] + derive(join(q_rows, q_corner, 1), 1)[:, :cols]
    both_rows = e_rows - jnp.where(wet_rows, 0.25 * spread, 0.0)
    spread = spread_y[:, cols:] + derive(join(p_cols, p_corner, 0), 0)[:rows]
    both_cols = e_cols - jnp.where(wet_cols, 0.25 * spread, 0.0)

    def step(flux, axis, mass, halo_e, halo_both):
        size = (rows, cols)[axis]
        grad = 0.5 * derive(join(twice_e, halo_e, axis), axis)
        grad = lax.slice_in_dim(grad, 0, size, axis=axis)
        grad_both = derive(join(both, halo_both, axis), axis)
        grad_both = lax.slice_in_dim(grad_both, 0, size, axis=axis)
        total = (2.0 - friction) * mass - slope * grad
        return flux - 0.5 * (slope * grad_both + friction * total)

    next_p[...] = step(p_ref[...], 0, mass_x, e_rows, both_rows)
    next_q[...] = step(q_ref[...], 1, mass_y, e_cols, both_cols)


def pairs_from(start, count):
    pairs = [(i, i + 1) for i in range(start, count - 1, 2)]
    return pairs + [(j, i) for i, j in pairs]


def swap(message, axis, start):
    pairs = pairs_from(start, lax.axis_size(axis))
    return lax.ppermute(message, axis, pairs) if pairs else jnp.zeros_like(message)


def body(e, p, q, c, w, range_test, corange_test, core_left, core_right):
    crosses, alongs = lax.axis_size("cross"), lax.axis_size("along")
    rows, cols = e.shape
    cells = rows * cols
    even = jnp.stack([lax.rem(lax.axis_index(a), 2) for a in AXES])

    def run(kernel, outs, flops, *args, idle=(), scratch=(), to=None):
        kinds = [pl.BlockSpec(memory_space=pltpu.SMEM if a is even else pltpu.VMEM) for a in args]
        kinds += [pl.BlockSpec(memory_space=pl.ANY)] * len(idle)
        moved = sum(a.size * 4 for a in args) + sum(o.size * 4 for o in outs)
        to = to or [pltpu.VMEM] * len(outs)
        return pl.pallas_call(
            kernel,
            out_shape=outs,
            in_specs=kinds,
            out_specs=[pl.BlockSpec(memory_space=kind) for kind in to],
            scratch_shapes=list(scratch),
            cost_estimate=pl.CostEstimate(flops=flops, bytes_accessed=moved, transcendentals=0),
            compiler_params=pltpu.CompilerParams(vmem_limit_bytes=32 * 1024 * 1024),
        )(*args, *idle)

    wet = w > 0
    slope = jnp.where(wet, 0.25 * c, 0.0)
    friction = jnp.where(wet, 0.02 / c, 0.0)
    mass_x, mass_y = jnp.where(wet, p, 0.0), jnp.where(wet, q, 0.0)
    twice_e = e + e
    strip = [f32(2 * ROWS, cols)] * 2 + [f32(2 * ROWS, rows)] * 2
    halo = run(pack_kernel, strip, cells, twice_e, mass_x, mass_y, slope, even)
    order = (3, 1, 2, 0)
    moved = {i: swap(halo[i], AXES[i // 2], i % 2) for i in order}
    halo = [moved[i] for i in range(4)]
    fields = (twice_e, mass_x, mass_y, slope, friction)
    range_shape = f32(rows, range_test.shape[1])
    corange_shape = f32(corange_test.shape[0], cols)
    core_shape = f32(core_left.shape[0], core_right.shape[1])
    tile = f32(rows, cols)
    half, thin = core_shape.shape[0] // 2, corange_shape.shape[0] // 2
    outs = [tile] * 2 + [f32(rows, core_shape.shape[1])]
    outs += [f32(half + thin + ROWS, cols), f32(ROWS, 2 * LANES)]
    s_next, s_held, product, give, corner = run(
        surface_kernel, outs, 600 * cells,
        *fields, even, *halo, corange_test, core_left, core_right,
        to=[pltpu.HBM] + [pltpu.VMEM] * 4, scratch=[pltpu.SemaphoreType.DMA((4,))],
    )
    got = swap(give, "cross", 0)
    corner = swap(corner, "cross", 1)
    p_next, q_next, token = run(
        flux_kernel, [tile] * 2 + [f32(ROWS, LANES)], 80 * cells, *fields, even, *halo, got, corner, p, q
    )
    count = crosses // 2 * alongs
    sizes = (half * core_shape.shape[1], range_shape.size, thin * cols)
    if crosses % 2 == 0 and not any(size % (count * ROWS * LANES) for size in sizes):
        per = [size // (count * ROWS * LANES) for size in sizes]
        cuts = (per[0], per[0] + per[1], sum(per))
        sheet = f32(count, cuts[2], ROWS, LANES)
        groups = [
            [i * alongs + a for i in range(side, crosses, 2) for a in range(alongs)]
            for side in range(2)
        ]

        def spread(x):
            return lax.all_to_all(x, AXES, 0, 0, tiled=True, axis_index_groups=groups)

        keep, ranged = run(
            product_kernel, [f32(half + thin, cols), range_shape], 300 * cells,
            s_held, product, even, range_test, corange_test, core_left,
        )
        (shares,) = run(
            functools.partial(merge_kernel, half), [sheet], sheet.size, keep, got, ranged
        )
        (totals,) = run(
            functools.partial(sum_kernel, crosses // 2, alongs, cuts), [sheet], sheet.size,
            spread(shares), idle=[token],
        )
        mine = spread(totals)
        theirs = swap(mine, "cross", 0)
        shapes = [core_shape, range_shape, corange_shape]
        core, ranged, coranged = run(
            unpack_kernel, shapes, sheet.size, even, mine, theirs, to=[pltpu.HBM] * 3,
            scratch=[pltpu.VMEM(x.shape, x.dtype) for x in shapes]
            + [pltpu.SemaphoreType.DMA((12,))],
        )
    else:
        ranged = lax.psum(dot(s_held, range_test), "along")
        coranged = lax.psum(dot(corange_test, s_held), "cross")
        core = lax.psum(dot(core_left, product), AXES)
    return s_next, p_next, q_next, ranged, coranged, core


def solution(mesh):
    tile = P("cross", "along")
    return jax.shard_map(
        body,
        mesh=mesh,
        in_specs=(tile,) * 5
        + (P("along", None), P(None, "cross"), P(None, "cross"), P("along", None)),
        out_specs=(tile,) * 3 + (P("cross", None), P(None, "along"), P()),
        check_vma=False,
    )
```

time: 64 us -> 57.1 us (0.89)
  blocking collectives: 27.7 us -> 14.3 us
  starting transfers between devices: 10.4 us -> 18 us
  local copies, waits for them, and re-layouts: 4.79 us -> 0.98 us
  Pallas kernels: 9.13 us -> 10.8 us
  other arithmetic: 0.08 us -> 1.34 us
    all_to_all x1, blocking collectives: 27.7 us -> 14.3 us  [spread(): return lax.all_to_all(x, AXES, 0, 0, tiled=True, axis_index_groups=groups)]
    all_to_all x1, starting transfers between devices: 2.75 us -> 10.6 us  [spread(): return lax.all_to_all(x, AXES, 0, 0, tiled=True, axis_index_groups=groups)]
    unnamed x30 -> x16, local copies, waits for them, and re-layouts: 4.79 us -> 0.98 us
    pallas_call x6 -> x7, Pallas kernels: 9.13 us -> 10.8 us  [run(): pl.pallas_call(kernel, out_shape=outs, in_specs=kinds, out_specs=[pl.Bloc...]
    add x0 -> x1, other arithmetic: none -> 1.12 us  [body(): twice_e = e + e]
    ppermute x8 -> x7, waiting for transfers between devices: 2.26 us -> 2.68 us  [swap(): lax.ppermute(message, axis, pairs)]
    ppermute x8 -> x7, starting transfers between devices: 7.65 us -> 7.36 us  [swap(): lax.ppermute(message, axis, pairs)]
  transfers between devices with their start and end apart: 9 -> 8, of which waited for: 3 -> 3; matrix products, arithmetic and copies ran while one was open for 0% -> 0% of each run, Pallas kernels for 5% -> 8%
where the time goes in v3:
time: 57.1 us; the launch traced here: 56.8 us
  starting transfers between devices  18 us (32%)
  blocking collectives  14.3 us (25%)
  Pallas kernels  10.8 us (19%)
  waiting for transfers between devices  10.6 us (19%)
  other arithmetic  1.34 us (2%)
  local copies, waits for them, and re-layouts  0.98 us (2%)
  between operations  0.82 us (1%)
    all_to_all x1, blocking collectives, spread(): return lax.all_to_all(x, AXES, 0, 0, tiled=True, axis_index_groups=groups)  14.3 us
    pallas_call x7, Pallas kernels, run(): pl.pallas_call(kernel, out_shape=outs, in_specs=kinds, out_specs=[pl.Bloc...  10.8 us
    all_to_all x1, starting transfers between devices, spread(): return lax.all_to_all(x, AXES, 0, 0, tiled=True, axis_index_groups=groups)  10.6 us
    all_to_all x1, waiting for transfers between devices, spread(): return lax.all_to_all(x, AXES, 0, 0, tiled=True, axis_index_groups=groups)  7.92 us
    ppermute x7, starting transfers between devices, swap(): lax.ppermute(message, axis, pairs)  7.36 us
    ppermute x7, waiting for transfers between devices, swap(): lax.ppermute(message, axis, pairs)  2.68 us
  transfers between devices with their start and end apart: 8, of which 3 were waited for; matrix products, arithmetic and copies ran while one was open for 0% of the time, Pallas kernels for 8%

profile of v3, /device:TPU:0, one launch (start us, length us, event | category | flops | bytes accessed | tf_op | source)
XLA Modules:
  0.0 56.8 jit_solution(5159900617639585408)
XLA Ops:
  0.7 1.1 %add.3.e_ref = f32[256,256]{1,0:T(8,128)S(1)} add(f32[256,256]{1,0:T(8,128)} %param.9, f32[256,256]{1,0:T(8,128)} %param.9) | non-fusion elementwise | flops 65536 | bytes 786432 | tf_op jit(solution)/shard_map/add | solution.py:327
  1.8 0.1 pad_add_fusion.even_ref
  1.9 0.1 divide_select_fusion
  1.9 0.9 %copy-done = f32[256,256]{1,0:T(8,128)S(1)} copy-done((f32[256,256]{1,0:T(8,128)S(1)}, f32[256,256]{1,0:T(8,128)}, u32[]{:S(2)}) %copy-start) | copy-done | bytes 262168
  2.8 0.1 copy-done.1
  2.9 0.1 multiply_select_fusion
  3.0 0.0 copy-start.2
  3.0 0.0 copy-start.3
  3.0 0.0 copy-start.4
  3.0 0.9 %shard_map.136 = (f32[16,256]{1,0:T(8,128)S(1)}, f32[16,256]{1,0:T(8,128)S(1)}, f32[16,256]{1,0:T(8,128)S(1)}, f32[16,256]{1,0:T(8,128)S(1)}) custom-call(f32[256,256]{1,0:T(8,128)S(1)} %add.3.e_ref, f32[256,256]{1,0:T(8,128)S(1)} %get-tuple-element.44.p_ref.mp_ref, f32[256,256]{1,0:T(8,128)S(1)} %get-tuple-element.43.q_ref.mq_ref, ...), custom_call_target="tpu_custom_call" | custom-call | flops 65536 | bytes 1114120 | tf_op jit(solution)/shard_map/pallas_call | solution.py:313
  3.9 0.5 collective-permute-start
  4.4 0.7 %collective-permute-start.1 = (f32[16,256]{1,0:T(8,128)S(1)}, f32[16,256]{1,0:T(8,128)S(1)}, u32[]{:S(2)}, u32[]{:S(2)}) collective-permute-start(f32[16,256]{1,0:T(8,128)S(1)} %get-tuple-element.24), channel_id=1, source_target_pairs={{8,16},{16,8},{9,17},{17,9},{10,18},{18,10},{11,19},{19,11},{12,20... | collective-permute-start | bytes 49160 | tf_op jit(solution)/shard_map/ppermute | solution.py:299
  5.1 2.6 %collective-permute-start.2 = (f32[16,256]{1,0:T(8,128)S(1)}, f32[16,256]{1,0:T(8,128)S(1)}, u32[]{:S(2)}, u32[]{:S(2)}) collective-permute-start(f32[16,256]{1,0:T(8,128)S(1)} %get-tuple-element.25), channel_id=1, source_target_pairs={{0,1},{2,3},{4,5},{6,7},{1,0},{3,2},{5,4},{7,6},{8,9},{10,11},{12,... | collective-permute-start | bytes 49160 | tf_op jit(solution)/shard_map/ppermute | solution.py:299
  7.7 0.7 %collective-permute-start.3 = (f32[16,256]{1,0:T(8,128)S(1)}, f32[16,256]{1,0:T(8,128)S(1)}, u32[]{:S(2)}, u32[]{:S(2)}) collective-permute-start(f32[16,256]{1,0:T(8,128)S(1)} %get-tuple-element.26), channel_id=1, source_target_pairs={{1,2},{3,4},{5,6},{2,1},{4,3},{6,5},{9,10},{11,12},{13,14},{10,9},... | collective-permute-start | bytes 49160 | tf_op jit(solution)/shard_map/ppermute | solution.py:299
  8.4 0.0 collective-permute-done.row0
  8.4 0.0 collective-permute-done.1.row1
  8.4 1.0 %collective-permute-done.2.col0 = f32[16,256]{1,0:T(8,128)S(1)} collective-permute-done((f32[16,256]{1,0:T(8,128)S(1)}, f32[16,256]{1,0:T(8,128)S(1)}, u32[]{:S(2)}, u32[]{:S(2)}) %collective-permute-start.2) | collective-permute-done | bytes 16416 | tf_op jit(solution)/shard_map/ppermute | solution.py:299
  9.4 0.0 copy-start.5
  9.4 3.3 %shard_map.137 = (f32[256,256]{1,0:T(8,128)}, f32[256,256]{1,0:T(8,128)S(1)}, f32[256,256]{1,0:T(8,128)S(1)}, f32[200,256]{1,0:T(8,128)S(1)}, f32[8,256]{1,0:T(8,128)S(1)}) custom-call(f32[256,256]{1,0:T(8,128)S(1)} %add.3.e_ref, f32[256,256]{1,0:T(8,128)S(1)} %get-tuple-element.44.p_ref.mp_ref, f32[256,256]{1,0:T(8,128)S(1)} %get-tuple-element.43.q_ref.mq_ref, ...), custom_call_target="tpu_custom_call" | custom-call | flops 39321600 | bytes 3031048 | tf_op jit(solution)/shard_map/pallas_call | solution.py:313
  12.8 2.3 %collective-permute-start.4 = (f32[200,256]{1,0:T(8,128)S(1)}, f32[200,256]{1,0:T(8,128)S(1)}, u32[]{:S(2)}, u32[]{:S(2)}) collective-permute-start(f32[200,256]{1,0:T(8,128)S(1)} %get-tuple-element.28), channel_id=1, source_target_pairs={{0,8},{16,24},{8,0},{24,16},{1,9},{17,25},{9,1},{25,17},{2,10},{18... | collective-permute-start | bytes 614408 | tf_op jit(solution)/shard_map/ppermute | solution.py:299
  15.0 1.2 %shard_map.139 = (f32[192,256]{1,0:T(8,128)S(1)}, f32[256,128]{1,0:T(8,128)S(1)}) custom-call(f32[256,256]{1,0:T(8,128)S(1)} %get-tuple-element.32.s_ref, f32[256,256]{1,0:T(8,128)S(1)} %get-tuple-element.33.product_ref, s32[2]{0:T(128)S(1)} %pad_add_fusion.even_ref, f32[256,128]{1,0:T(8,128)S(1)} %copy-done.5, f32[128,256]{1,0:T(8,128)S(1)} %copy-done.3, ...), custom_call_target="tpu_custom_call" | custom-call | flops 19660800 | bytes 1376264 | tf_op jit(solution)/shard_map/pallas_call | solution.py:313
  16.2 0.0 collective-permute-done.4.got_ref
  16.2 0.7 %shard_map.140 = f32[16,5,8,128]{3,2,1,0:T(8,128)} custom-call(f32[192,256]{1,0:T(8,128)S(1)} %get-tuple-element.34.keep_ref, f32[200,256]{1,0:T(8,128)S(1)} %collective-permute-done.4.got_ref, f32[256,128]{1,0:T(8,128)S(1)} %get-tuple-element.35.range_ref), custom_call_target="tpu_custom_call" | custom-call | flops 81920 | bytes 860160 | tf_op jit(solution)/shard_map/pallas_call | solution.py:313
  17.0 10.6 %all-to-all-start = ((f32[16,5,8,128]{3,2,1,0:T(8,128)}), f32[16,5,8,128]{3,2,1,0:T(8,128)S(1)}, u32[]{:S(2)}, u32[]{:S(2)}) async-start(f32[16,5,8,128]{3,2,1,0:T(8,128)} %shard_map.140), calls=%async_computation | async-start | bytes 655360 | tf_op jit(solution)/shard_map/all_to_all | solution.py:363
  27.6 0.7 %collective-permute-start.5 = (f32[8,256]{1,0:T(8,128)S(1)}, f32[8,256]{1,0:T(8,128)S(1)}, u32[]{:S(2)}, u32[]{:S(2)}) collective-permute-start(f32[8,256]{1,0:T(8,128)S(1)} %get-tuple-element.29), channel_id=1, source_target_pairs={{8,16},{16,8},{9,17},{17,9},{10,18},{18,10},{11,19},{19,11},{12,20... | collective-permute-start | bytes 24584 | tf_op jit(solution)/shard_map/ppermute | solution.py:299
  28.3 0.0 collective-permute-done.5.corner_ref
  28.3 3.1 %shard_map.138 = (f32[256,256]{1,0:T(8,128)}, f32[256,256]{1,0:T(8,128)}, f32[8,128]{1,0:T(8,128)S(1)}) custom-call(f32[256,256]{1,0:T(8,128)S(1)} %add.3.e_ref, f32[256,256]{1,0:T(8,128)S(1)} %get-tuple-element.44.p_ref.mp_ref, f32[256,256]{1,0:T(8,128)S(1)} %get-tuple-element.43.q_ref.mq_ref, f32[256,256]{1,0:T(8,128)S(1)} %get-tuple-element.42.a_ref, ...), custom_call_target="tpu_custom_call" | custom-call | flops 5242880 | bytes 2641928 | tf_op jit(solution)/shard_map/pallas_call | solution.py:313
  31.4 7.9 %all-to-all-done.got = f32[16,5,8,128]{3,2,1,0:T(8,128)S(1)} async-done(((f32[16,5,8,128]{3,2,1,0:T(8,128)}), f32[16,5,8,128]{3,2,1,0:T(8,128)S(1)}, u32[]{:S(2)}, u32[]{:S(2)}) %all-to-all-start) | async-done | bytes 327712 | tf_op jit(solution)/shard_map/all_to_all | solution.py:363
  39.4 14.3 %all_to_all.10.mine = f32[16,5,8,128]{3,2,1,0:T(8,128)S(1)} all-to-all(f32[16,5,8,128]{3,2,1,0:T(8,128)S(1)} %shard_map.141), channel_id=1, replica_groups={{0,1,2,3,4,5,6,7,16,17,18,19,20,21,22,23},{8,9,10,11,12,13,14,15,24,25,..., dimensions={0} | all-to-all | bytes 655360 | tf_op jit(solution)/shard_map/all_to_all | solution.py:363
  53.7 0.0 collective-permute-start.6
  53.7 1.6 %collective-permute-done.6.theirs = f32[16,5,8,128]{3,2,1,0:T(8,128)S(1)} collective-permute-done((f32[16,5,8,128]{3,2,1,0:T(8,128)S(1)}, f32[16,5,8,128]{3,2,1,0:T(8,128)S(1)}, u32[]{:S(2)}, u32[]{:S(2)}) %collective-permute-start.6) | collective-permute-done | bytes 327712 | tf_op jit(solution)/shard_map/ppermute | solution.py:299
  55.3 1.4 %shard_map.142 = (f32[256,256]{1,0:T(8,128)}, f32[256,128]{1,0:T(8,128)}, f32[128,256]{1,0:T(8,128)}) custom-call(s32[2]{0:T(128)S(1)} %pad_add_fusion.even_ref, f32[16,5,8,128]{3,2,1,0:T(8,128)S(1)} %all_to_all.10.mine, f32[16,5,8,128]{3,2,1,0:T(8,128)S(1)} %collective-permute-done.6.theirs), custom_call_target="tpu_custom_call" | custom-call | flops 81920 | bytes 1179656 | tf_op jit(solution)/shard_map/pallas_call | solution.py:313
  (12 shorter events, 0.1 us)
Async XLA Ops:
  0.6 1.2 %copy-start.6 = (f32[256,256]{1,0:T(8,128)S(1)}, f32[256,256]{1,0:T(8,128)}, u32[]{:S(2)}) copy-start(f32[256,256]{1,0:T(8,128)} %param.12) | copy-start | bytes 786436
  0.6 1.2 %copy-start.7 = (s32[256,256]{1,0:T(8,128)S(1)}, s32[256,256]{1,0:T(8,128)}, u32[]{:S(2)}) copy-start(s32[256,256]{1,0:T(8,128)} %param.13) | copy-start | bytes 786436
  1.9 1.0 %copy-start = (f32[256,256]{1,0:T(8,128)S(1)}, f32[256,256]{1,0:T(8,128)}, u32[]{:S(2)}) copy-start(f32[256,256]{1,0:T(8,128)} %q_ref.1) | copy-start | bytes 786436
  1.9 1.0 %copy-start.1 = (f32[256,256]{1,0:T(8,128)S(1)}, f32[256,256]{1,0:T(8,128)}, u32[]{:S(2)}) copy-start(f32[256,256]{1,0:T(8,128)} %p_ref.1) | copy-start | bytes 786436
  3.0 6.4 %copy-start.2 = (f32[256,256]{1,0:T(8,128)S(1)}, f32[256,256]{1,0:T(8,128)}, u32[]{:S(2)}) copy-start(f32[256,256]{1,0:T(8,128)} %left_ref.3) | copy-start | bytes 786436
  3.0 6.4 %copy-start.3 = (f32[128,256]{1,0:T(8,128)S(1)}, f32[128,256]{1,0:T(8,128)}, u32[]{:S(2)}) copy-start(f32[128,256]{1,0:T(8,128)} %cr_ref.3) | copy-start | bytes 393220
  3.0 6.4 %copy-start.4 = (f32[256,256]{1,0:T(8,128)S(1)}, f32[256,256]{1,0:T(8,128)}, u32[]{:S(2)}) copy-start(f32[256,256]{1,0:T(8,128)} %right_ref.1) | copy-start | bytes 786436
  3.9 4.4 %collective-permute-start = (f32[16,256]{1,0:T(8,128)S(1)}, f32[16,256]{1,0:T(8,128)S(1)}, u32[]{:S(2)}, u32[]{:S(2)}) collective-permute-start(f32[16,256]{1,0:T(8,128)S(1)} %get-tuple-element.23), channel_id=1, source_target_pairs={{0,8},{16,24},{8,0},{24,16},{1,9},{17,25},{9,1},{25,17},{2,10},{18... | collective-permute-start | bytes 49160 | tf_op jit(solution)/shard_map/ppermute | solution.py:299
  4.4 3.9 %collective-permute-start.1 = (f32[16,256]{1,0:T(8,128)S(1)}, f32[16,256]{1,0:T(8,128)S(1)}, u32[]{:S(2)}, u32[]{:S(2)}) collective-permute-start(f32[16,256]{1,0:T(8,128)S(1)} %get-tuple-element.24), channel_id=1, source_target_pairs={{8,16},{16,8},{9,17},{17,9},{10,18},{18,10},{11,19},{19,11},{12,20... | collective-permute-start | bytes 49160 | tf_op jit(solution)/shard_map/ppermute | solution.py:299
  5.1 4.3 %collective-permute-start.2 = (f32[16,256]{1,0:T(8,128)S(1)}, f32[16,256]{1,0:T(8,128)S(1)}, u32[]{:S(2)}, u32[]{:S(2)}) collective-permute-start(f32[16,256]{1,0:T(8,128)S(1)} %get-tuple-element.25), channel_id=1, source_target_pairs={{0,1},{2,3},{4,5},{6,7},{1,0},{3,2},{5,4},{7,6},{8,9},{10,11},{12,... | collective-permute-start | bytes 49160 | tf_op jit(solution)/shard_map/ppermute | solution.py:299
  7.7 1.7 %collective-permute-start.3 = (f32[16,256]{1,0:T(8,128)S(1)}, f32[16,256]{1,0:T(8,128)S(1)}, u32[]{:S(2)}, u32[]{:S(2)}) collective-permute-start(f32[16,256]{1,0:T(8,128)S(1)} %get-tuple-element.26), channel_id=1, source_target_pairs={{1,2},{3,4},{5,6},{2,1},{4,3},{6,5},{9,10},{11,12},{13,14},{10,9},... | collective-permute-start | bytes 49160 | tf_op jit(solution)/shard_map/ppermute | solution.py:299
  9.4 5.6 %copy-start.5 = (f32[256,128]{1,0:T(8,128)S(1)}, f32[256,128]{1,0:T(8,128)}, u32[]{:S(2)}) copy-start(f32[256,128]{1,0:T(8,128)} %r_ref.1) | copy-start | bytes 393220
  12.8 3.5 %collective-permute-start.4 = (f32[200,256]{1,0:T(8,128)S(1)}, f32[200,256]{1,0:T(8,128)S(1)}, u32[]{:S(2)}, u32[]{:S(2)}) collective-permute-start(f32[200,256]{1,0:T(8,128)S(1)} %get-tuple-element.28), channel_id=1, source_target_pairs={{0,8},{16,24},{8,0},{24,16},{1,9},{17,25},{9,1},{25,17},{2,10},{18... | collective-permute-start | bytes 614408 | tf_op jit(solution)/shard_map/ppermute | solution.py:299
  17.0 22.4 %all-to-all-start = ((f32[16,5,8,128]{3,2,1,0:T(8,128)}), f32[16,5,8,128]{3,2,1,0:T(8,128)S(1)}, u32[]{:S(2)}, u32[]{:S(2)}) async-start(f32[16,5,8,128]{3,2,1,0:T(8,128)} %shard_map.140), calls=%async_computation | async-start | bytes 655360 | tf_op jit(solution)/shard_map/all_to_all | solution.py:363
  27.6 0.7 %collective-permute-start.5 = (f32[8,256]{1,0:T(8,128)S(1)}, f32[8,256]{1,0:T(8,128)S(1)}, u32[]{:S(2)}, u32[]{:S(2)}) collective-permute-start(f32[8,256]{1,0:T(8,128)S(1)} %get-tuple-element.29), channel_id=1, source_target_pairs={{8,16},{16,8},{9,17},{17,9},{10,18},{18,10},{11,19},{19,11},{12,20... | collective-permute-start | bytes 24584 | tf_op jit(solution)/shard_map/ppermute | solution.py:299
  53.7 1.6 %collective-permute-start.6 = (f32[16,5,8,128]{3,2,1,0:T(8,128)S(1)}, f32[16,5,8,128]{3,2,1,0:T(8,128)S(1)}, u32[]{:S(2)}, u32[]{:S(2)}) collective-permute-start(f32[16,5,8,128]{3,2,1,0:T(8,128)S(1)} %all_to_all.10.mine), channel_id=1, source_target_pairs={{0,8},{16,24},{8,0},{24,16},{1,9},{17,25},{9,1},{25,17},{2,10},{18... | collective-permute-start | bytes 983048 | tf_op jit(solution)/shard_map/ppermute | solution.py:299

commit v4 on v3

v4 whole, which is shorter than its diff:
```python
import functools

import jax
import jax.numpy as jnp
from jax import lax
from jax.experimental import pallas as pl
from jax.experimental.pallas import tpu as pltpu
from jax.sharding import PartitionSpec as P

AXES = ("cross", "along")
ROWS = 8
LANES = 128
WINDOW = 64


def f32(*shape):
    return jax.ShapeDtypeStruct(shape, jnp.float32)


def derive(field, axis):
    size = field.shape[axis]

    def part(shift):
        return pltpu.roll(field, (-shift) % size, axis)

    return (part(1) - part(-1)) * (8.0 / 12.0) - (part(2) - part(-2)) * (1.0 / 12.0)


def friction_of(slope):
    wet = slope > 0.0
    return jnp.where(wet, 0.005 / jnp.where(wet, slope, 1.0), 0.0)


def place(shape, axis, dim):
    return lax.broadcasted_iota(jnp.int32, shape, dim)


def parity(axis):
    return lax.rem(lax.axis_index(axis), 2)


def row_kernel(e_hbm, p_hbm, q_hbm, c_hbm, w_hbm, first_ref, second_ref, eb, pb, qb, cb, wb, sems):
    rows, cols = e_hbm.shape
    copies = [
        pltpu.make_async_copy(source.at[pl.ds(i * (rows - ROWS), ROWS), :], to.at[i], sems.at[k, i])
        for k, (source, to) in enumerate(
            ((e_hbm, eb), (p_hbm, pb), (q_hbm, qb), (c_hbm, cb), (w_hbm, wb))
        )
        for i in range(2)
    ]
    for copy in copies:
        copy.start()
    for copy in copies:
        copy.wait()
    at = place((ROWS, cols), ROWS, 0)
    messages = []
    for i, (far, near, turn) in enumerate(((at < 4, at < 6, 6), (at >= 4, at >= 2, 2))):
        wet = wb[i] > 0
        slope = jnp.where(wet, 0.25 * cb[i], 0.0)
        mass, side = jnp.where(wet, pb[i], 0.0), jnp.where(wet, qb[i], 0.0)
        first = jnp.where(near, pltpu.roll(mass, 4, 0), pltpu.roll(slope, turn, 0))
        first = jnp.where(far, 2.0 * eb[i], first)
        messages.append(join(first, jnp.where(far, mass, pltpu.roll(side, 4, 0)), 0))
    up, down = messages
    even = parity("cross") == 0
    first_ref[...] = jnp.where(even, down, up)
    second_ref[...] = jnp.where(even, up, down)


def col_kernel(
    e_in, p_in, q_in, c_in, w_in, e_ref, p_ref, q_ref, a_ref, f_ref, first_ref, second_ref
):
    rows, cols = e_ref.shape
    for start, step in windows(rows):
        here = slice(start, start + step)
        wet, celerity_sq = w_in[here, :] > 0, c_in[here, :]
        e_ref[here, :] = 2.0 * e_in[here, :]
        p_ref[here, :] = jnp.where(wet, p_in[here, :], 0.0)
        q_ref[here, :] = jnp.where(wet, q_in[here, :], 0.0)
        a_ref[here, :] = jnp.where(wet, 0.25 * celerity_sq, 0.0)
        f_ref[here, :] = jnp.where(wet, 0.02 / celerity_sq, 0.0)
    lane = place((rows, LANES), LANES, 1)
    left = lane < LANES // 2
    off = jnp.minimum(lane, LANES - 1 - lane)

    def edge(ref):
        return jnp.where(left, ref[:, :LANES], ref[:, cols - LANES :])

    def shift(block, count):
        return jnp.where(left, pltpu.roll(block, count, 1), pltpu.roll(block, LANES - count, 1))

    slope, mass, side = edge(a_ref), edge(q_ref), edge(p_ref)
    first = jnp.where(off < 4, edge(e_ref), jnp.where(off < 6, shift(mass, 4), shift(slope, 6))).T
    second = jnp.where(off < 4, mass, shift(side, 4)).T
    to_left = join(first[:ROWS], second[:ROWS], 0)
    to_right = join(first[LANES - ROWS :], second[LANES - ROWS :], 0)
    even = parity("along") == 0
    first_ref[...] = jnp.where(even, to_right, to_left)
    second_ref[...] = jnp.where(even, to_left, to_right)


def row_pick(even, first, second):
    below, above = jnp.where(even, first, second), jnp.where(even, second, first)
    at = place(below.shape, ROWS, 0)

    def pick(count, shift):
        low = pltpu.roll(below, ROWS - shift, 0) if shift else below
        high = pltpu.roll(above, shift, 0) if shift else above
        return jnp.where(at < count, low, jnp.where(at >= ROWS - count, high, 0.0))

    return pick


def col_pick(even, first, second):
    right, left = jnp.where(even, first, second), jnp.where(even, second, first)
    gap = jnp.zeros((LANES - 2 * ROWS, right.shape[1]), right.dtype)
    both = jnp.concatenate([right, gap, left], axis=0).T
    lane = place(both.shape, LANES, 1)

    def pick(count, shift):
        low = pltpu.roll(both, LANES - shift, 1) if shift else both
        high = pltpu.roll(both, shift, 1) if shift else both
        return jnp.where(lane < count, low, jnp.where(lane >= LANES - count, high, 0.0))

    return pick


def split(a):
    high = a.astype(jnp.bfloat16)
    return high, (a - high.astype(jnp.float32)).astype(jnp.bfloat16)


def dot_split(a, b):
    (a_high, a_low), (b_high, b_low) = a, b

    def product(x, y):
        return jnp.dot(x, y, preferred_element_type=jnp.float32)

    return product(a_high, b_high) + (product(a_high, b_low) + product(a_low, b_high))


def dot(a, b):
    return dot_split(split(a), split(b))


def join(tile, halo, axis):
    return jnp.concatenate([tile, halo], axis=axis)


def windows(rows):
    step = WINDOW if rows % WINDOW == 0 else ROWS
    for start in range(0, rows, step):
        yield start, step


def with_ring(part, ring, start, step, rows):
    parts = [part]
    if start == 0:
        parts.insert(0, ring)
    if start + step == rows:
        parts.append(ring)
    return jnp.concatenate(parts, axis=0) if len(parts) > 1 else part


def window(tile, ring, start, step):
    rows = tile.shape[0]
    part = tile[max(start - ROWS, 0) : min(start + step + ROWS, rows)]
    return with_ring(part, ring, start, step, rows)


def surface_kernel(
    e_ref, p_ref, q_ref, a_ref, f_ref, row1, row0, col1, col0,
    cr_ref, left_ref, right_ref, s_ref, sum_p, sum_q, product_ref, give_ref,
):
    rows, cols = e_ref.shape
    even_row, even_col = parity("cross") == 0, parity("along") == 0

    def halo(pick):
        e, mass, slope = pick(4, 0), pick(2, 4), pick(2, 6)
        return e, (2.0 - friction_of(slope)) * mass, slope

    e_row, g_row, a_row = halo(row_pick(even_row, row0[:ROWS], row1[:ROWS]))
    e_col, g_col, a_col = halo(col_pick(even_col, col0[:ROWS], col1[:ROWS]))
    for start, step in windows(rows):
        inner = slice(start, start + step)
        grad = derive(window(e_ref, e_row, start, step), 0)
        slope = window(a_ref, a_row, start, step)
        around = slice(max(start - ROWS, 0), min(start + step + ROWS, rows))
        total = with_ring((2.0 - f_ref[around, :]) * p_ref[around, :], g_row, start, step, rows)
        total -= 0.5 * slope * grad
        sum_p[inner, :] = total[ROWS : ROWS + step]
        change = derive(total, 0)[ROWS : ROWS + step]
        grad = derive(join(e_ref[inner, :], e_col[inner], 1), 1)
        slope = a_ref[inner, :]
        total = (2.0 - f_ref[inner, :]) * q_ref[inner, :]
        total = join(total, g_col[inner], 1) - 0.5 * join(slope, a_col[inner], 1) * grad
        sum_q[inner, :] = total[:, :cols]
        change += derive(total, 1)[:, :cols]
        s_ref[inner, :] = 0.5 * e_ref[inner, :] - jnp.where(slope > 0.0, 0.125 * change, 0.0)
    s = split(s_ref[...])
    pick = col_pick(even_col, col0[ROWS:], col1[ROWS:])
    around = join(pick(4, 0), pick(2, 4), 1)
    up, down = around[:ROWS], around[rows - ROWS :]
    tail = give_ref.shape[0] - 2 * ROWS
    give_ref[tail:, :] = jnp.where(even_row, join(down, up, 0), join(up, down, 0))
    product = dot_split(s, split(right_ref[...]))
    product_ref[...] = product
    give_ref[:tail, :] = halves(
        1 - parity("cross"), left_ref, split(product), cr_ref, s
    )


def halves(side, left_ref, product, cr_ref, s):
    half, thin = left_ref.shape[0] // 2, cr_ref.shape[0] // 2
    left = left_ref[pl.ds(pl.multiple_of(side * half, half), half), :]
    core = dot_split(split(left), product)
    thin_rows = cr_ref[pl.ds(pl.multiple_of(side * thin, thin), thin), :]
    return join(core, dot_split(split(thin_rows), s), 0)


def product_kernel(
    s_ref, product_ref, r_ref, cr_ref, left_ref, s_hbm, keep_ref, range_ref, sems
):
    copies = start(pieces(s_ref, s_hbm, sems))
    s = split(s_ref[...])
    keep_ref[...] = halves(parity("cross"), left_ref, split(product_ref[...]), cr_ref, s)
    range_ref[...] = dot_split(s, split(r_ref[...]))
    for copy in copies:
        copy.wait()


def start(copies):
    for copy in copies:
        copy.start()
    return copies


def pieces(source, to, sems, count=4):
    part = source.shape[0] // count
    blocks = [pl.ds(i * part, part) for i in range(count)]
    return [
        pltpu.make_async_copy(source.at[block, :], to.at[block, :], sems.at[i])
        for i, block in enumerate(blocks)
    ]


def merge_kernel(half, keep_ref, got_ref, range_ref, out, across_ref):
    ends = keep_ref.shape[0]
    both = keep_ref[...] + got_ref[:ends]
    at = 0
    for part in (both[:half], range_ref[...]):
        per = tile_count(part) // out.shape[0]
        for k, tile in enumerate(tiles_of(part)):
            out[k // per, at + k % per] = tile
        at += per
    across_ref[...] = join(both[half:], got_ref[ends + ROWS :], 0)


def tile_count(part):
    return part.shape[0] // ROWS * (part.shape[1] // LANES)


def tile_slices(shape):
    return [
        (slice(i, i + ROWS), slice(j, j + LANES))
        for i in range(0, shape[0], ROWS)
        for j in range(0, shape[1], LANES)
    ]


def tiles_of(part):
    return [part[where] for where in tile_slices(part.shape)]


def sum_kernel(crosses, alongs, cuts, got, *rest):
    out = rest[-1]
    first, second = cuts
    count = crosses * alongs

    def add(values):
        values = list(values)
        while len(values) > 1:
            values = [sum(values[i : i + 2][1:], values[i]) for i in range(0, len(values), 2)]
        return values[0]

    for t in range(first):
        value = add(got[k, t] for k in range(count))
        for k in range(count):
            out[k, t] = value
    for t in range(first, second):
        for c in range(crosses):
            value = add(got[c * alongs + a, t] for a in range(alongs))
            for a in range(alongs):
                out[c * alongs + a, t] = value


def unpack_kernel(mine, theirs, thin_mine, thin_theirs, *refs):
    outs, held, sems = refs[:3], refs[3:6], refs[6]
    core, ranged, coranged = held
    count = mine.shape[0]
    even = parity("cross") == 0
    thin = thin_mine.shape[0]
    coranged[:thin] = jnp.where(even, thin_mine[...], thin_theirs[...])
    coranged[thin:] = jnp.where(even, thin_theirs[...], thin_mine[...])
    copies = start(pieces(coranged, outs[2], sems.at[2]))
    places = tile_slices(ranged.shape)
    wide = len(tile_slices(core.shape)) // 2 // count
    per = len(places) // count
    for k, where in enumerate(places):
        ranged[where] = mine[k // per, wide + k % per]
    copies += start(pieces(ranged, outs[1], sems.at[1]))
    places = tile_slices(core.shape)
    keep = len(places) // 2
    for k in range(keep):
        tile, other = mine[k // wide, k % wide], theirs[k // wide, k % wide]
        core[places[k]] = jnp.where(even, tile, other)
        core[places[keep + k]] = jnp.where(even, other, tile)
    copies += start(pieces(core, outs[0], sems.at[0]))
    for copy in copies:
        copy.wait()


def flux_kernel(
    e_ref, mp_ref, mq_ref, a_ref, f_ref, row1, row0, col1, col0, got_ref, corner_ref,
    p_ref, q_ref, sum_p, sum_q, p_hbm, q_hbm, next_p, next_q, sems,
):
    rows, cols = e_ref.shape
    copies = []
    even_row, even_col = parity("cross") == 0, parity("along") == 0
    pick = row_pick(even_row, row0[:ROWS], row1[:ROWS])
    e_row, a_row = pick(4, 0), pick(2, 6)
    pick = row_pick(even_row, row0[ROWS:], row1[ROWS:])
    p_row, q_row = pick(4, 0), pick(2, 4)
    pick = col_pick(even_col, col0[:ROWS], col1[:ROWS])
    e_col, a_col = pick(4, 0), pick(2, 6)
    pick = col_pick(even_col, col0[ROWS:], col1[ROWS:])
    q_col, p_col = pick(4, 0), pick(2, 4)
    row = lax.axis_index("cross")
    inside = (row > 0) & (row < lax.axis_size("cross") - 1)
    beyond = jnp.where(inside, corner_ref[corner_ref.shape[0] - ROWS :], 0.0)
    near = got_ref.shape[0] - 2 * ROWS
    pick = row_pick(even_row, got_ref[near : near + ROWS], beyond)
    corners = pick(2, 0)
    none = jnp.zeros((ROWS, LANES), e_ref.dtype)
    for i, (start, step) in enumerate(windows(rows)):

        def ring(tile, row, col, corner):
            return join(
                window(tile, row, start, step), window(col, corner, start, step), 1
            )

        spread = derive(ring(mp_ref, p_row, p_col, corners[:, LANES:]), 0)
        spread += derive(ring(mq_ref, q_row, q_col, corners[:, :LANES]), 1)
        wet = ring(a_ref, a_row, a_col, none) > 0.0
        both = ring(e_ref, e_row, e_col, none) - jnp.where(wet, 0.25 * spread, 0.0)
        inner = slice(start, start + step)
        grad_x = derive(both[:, :cols], 0)[ROWS : ROWS + step]
        grad_y = derive(both[ROWS : ROWS + step], 1)[:, :cols]
        slope, friction = 0.5 * a_ref[inner, :], 0.5 * f_ref[inner, :]
        next_p[inner, :] = p_ref[inner, :] - (slope * grad_x + friction * sum_p[inner, :])
        next_q[inner, :] = q_ref[inner, :] - (slope * grad_y + friction * sum_q[inner, :])
        for k, (ref, hbm) in enumerate(((next_p, p_hbm), (next_q, q_hbm))):
            copy = pltpu.make_async_copy(ref.at[inner, :], hbm.at[inner, :], sems.at[k, i])
            copy.start()
            copies.append(copy)
    for copy in copies:
        copy.wait()


def pairs_from(start, count):
    pairs = [(i, i + 1) for i in range(start, count - 1, 2)]
    return pairs + [(j, i) for i, j in pairs]


def swap(message, axis, start):
    pairs = pairs_from(start, lax.axis_size(axis))
    return lax.ppermute(message, axis, pairs) if pairs else jnp.zeros_like(message)


def body(e, p, q, c, w, range_test, corange_test, core_left, core_right):
    crosses, alongs = lax.axis_size("cross"), lax.axis_size("along")
    rows, cols = e.shape
    cells = rows * cols

    def run(kernel, outs, flops, *args, idle=(), scratch=(), to=None, space=pltpu.VMEM, limit=32):
        kinds = [pl.BlockSpec(memory_space=space)] * len(args)
        kinds += [pl.BlockSpec(memory_space=pl.ANY)] * len(idle)
        moved = sum(a.size * 4 for a in args) + sum(o.size * 4 for o in outs)
        to = to or [pltpu.VMEM] * len(outs)
        return pl.pallas_call(
            kernel,
            out_shape=outs,
            in_specs=kinds,
            out_specs=[pl.BlockSpec(memory_space=kind) for kind in to],
            scratch_shapes=list(scratch),
            cost_estimate=pl.CostEstimate(flops=flops, bytes_accessed=moved, transcendentals=0),
            compiler_params=pltpu.CompilerParams(vmem_limit_bytes=limit * 1024 * 1024),
        )(*args, *idle)

    held = [pltpu.VMEM((2, ROWS, cols), a.dtype) for a in (e, p, q, c, w)]
    row0, row1 = run(
        row_kernel, [f32(2 * ROWS, cols)] * 2, cells, e, p, q, c, w, space=pltpu.HBM,
        scratch=held + [pltpu.SemaphoreType.DMA((5, 2))], limit=60,
    )
    row1, row0 = swap(row1, "cross", 1), swap(row0, "cross", 0)
    tile = f32(rows, cols)
    *fields, col0, col1 = run(
        col_kernel, [tile] * 5 + [f32(2 * ROWS, rows)] * 2, 10 * cells, e, p, q, c, w
    )
    col1, col0 = swap(col1, "along", 1), swap(col0, "along", 0)
    halo = (row1, row0, col1, col0)
    range_shape = f32(rows, range_test.shape[1])
    corange_shape = f32(corange_test.shape[0], cols)
    core_shape = f32(core_left.shape[0], core_right.shape[1])
    half, thin = core_shape.shape[0] // 2, corange_shape.shape[0] // 2
    outs = [tile] * 3 + [f32(rows, core_shape.shape[1])]
    outs += [f32(half + thin + 2 * ROWS, cols)]
    s_held, sum_p, sum_q, product, give = run(
        surface_kernel, outs, 600 * cells,
        *fields, *halo, corange_test, core_left, core_right,
    )
    got = swap(give, "cross", 0)
    count = crosses // 2 * alongs
    sizes = (half * core_shape.shape[1], range_shape.size)
    keep_shape = f32(half + thin, cols)
    s_next, keep, ranged = run(
        product_kernel, [tile, keep_shape, range_shape], 300 * cells,
        s_held, product, range_test, corange_test, core_left,
        to=[pltpu.HBM, pltpu.VMEM, pltpu.VMEM], scratch=[pltpu.SemaphoreType.DMA((4,))],
    )
    shared = crosses == 4 and not any(size % (count * ROWS * LANES) for size in sizes)
    if shared:
        per = [size // (count * ROWS * LANES) for size in sizes]
        cuts = (per[0], per[0] + per[1])
        sheet = f32(count, cuts[1], ROWS, LANES)
        groups = [
            [i * alongs + a for i in range(side, crosses, 2) for a in range(alongs)]
            for side in range(2)
        ]

        def spread(x):
            return lax.all_to_all(x, AXES, 0, 0, tiled=True, axis_index_groups=groups)

        shares, across = run(
            functools.partial(merge_kernel, half), [sheet, f32(thin + ROWS, cols)], sheet.size,
            keep, got, ranged,
        )
        corner = lax.ppermute(across, "cross", [(i, i ^ 2) for i in range(crosses)])
        thin_mine = across[:thin] + corner[:thin]
        thin_theirs = swap(thin_mine, "cross", 0)
        (totals,) = run(
            functools.partial(sum_kernel, crosses // 2, alongs, cuts), [sheet], sheet.size,
            spread(shares), idle=[thin_mine],
        )
        mine = spread(totals)
        theirs = swap(mine, "cross", 0)
        shapes = [core_shape, range_shape, corange_shape]
        core, ranged, coranged = run(
            unpack_kernel, shapes, sheet.size, mine, theirs, thin_mine, thin_theirs,
            to=[pltpu.HBM] * 3,
            scratch=[pltpu.VMEM(x.shape, x.dtype) for x in shapes]
            + [pltpu.SemaphoreType.DMA((3, 4))],
        )
    else:
        corner = swap(give[-ROWS:], "cross", 1)
        ranged = lax.psum(ranged, "along")
        coranged = lax.psum(dot(corange_test, s_held), "cross")
        core = lax.psum(dot(core_left, product), AXES)
    p_next, q_next = run(
        flux_kernel, [tile] * 2, 80 * cells, *fields, *halo, got, corner, p, q, sum_p, sum_q,
        to=[pltpu.HBM] * 2,
        scratch=[pltpu.VMEM((rows, cols), jnp.float32)] * 2
        + [pltpu.SemaphoreType.DMA((2, len(list(windows(rows)))))],
    )
    return s_next, p_next, q_next, ranged, coranged, core


def solution(mesh):
    tile = P("cross", "along")
    return jax.shard_map(
        body,
        mesh=mesh,
        in_specs=(tile,) * 5
        + (P("along", None), P(None, "cross"), P(None, "cross"), P("along", None)),
        out_specs=(tile,) * 3 + (P("cross", None), P(None, "along"), P()),
        check_vma=False,
    )
```

time: 57.1 us -> 50.8 us (0.89)
  Pallas kernels: 10.8 us -> 8.71 us
  blocking collectives: 14.3 us -> 12.5 us
  other arithmetic: 1.34 us -> 0.01 us
  local copies, waits for them, and re-layouts: 0.98 us -> 0.05 us
    all_to_all x1, starting transfers between devices: 10.6 us -> 5.43 us  [spread(): return lax.all_to_all(x, AXES, 0, 0, tiled=True, axis_index_groups=groups)]
    ppermute x0 -> x1, waiting for transfers between devices: none -> 4 us  [body(): corner = lax.ppermute(across, 'cross', [(i, i ^ 2) for i in range(crosses)])]
    all_to_all x1, waiting for transfers between devices: 7.92 us -> 4.23 us  [spread(): return lax.all_to_all(x, AXES, 0, 0, tiled=True, axis_index_groups=groups)]
    ppermute x7, starting transfers between devices: 7.36 us -> 10.6 us  [swap(): lax.ppermute(message, axis, pairs)]
    pallas_call x7 -> x8, Pallas kernels: 10.8 us -> 8.71 us  [run(): pl.pallas_call(kernel, out_shape=outs, in_specs=kinds, out_specs=[pl.Bloc...]
    ppermute x0 -> x1, starting transfers between devices: none -> 1.93 us  [body(): corner = lax.ppermute(across, 'cross', [(i, i ^ 2) for i in range(crosses)])]
    all_to_all x1, blocking collectives: 14.3 us -> 12.5 us  [spread(): return lax.all_to_all(x, AXES, 0, 0, tiled=True, axis_index_groups=groups)]
    add x1, other arithmetic: 1.12 us -> 0.01 us  [body(): thin_mine = across[:thin] + corner[:thin]]
  transfers between devices with their start and end apart: 8 -> 9, of which waited for: 3 -> 4; matrix products, arithmetic and copies ran while one was open for 0% -> 0% of each run, Pallas kernels for 8% -> 7%
where the time goes in v4:
time: 50.8 us; the launch traced here: 50.4 us
  starting transfers between devices  18 us (35%)
  blocking collectives  12.5 us (25%)
  waiting for transfers between devices  10.4 us (20%)
  Pallas kernels  8.71 us (17%)
  between operations  0.83 us (2%)
    all_to_all x1, blocking collectives, spread(): return lax.all_to_all(x, AXES, 0, 0, tiled=True, axis_index_groups=groups)  12.5 us
    ppermute x7, starting transfers between devices, swap(): lax.ppermute(message, axis, pairs)  10.6 us
    pallas_call x8, Pallas kernels, run(): pl.pallas_call(kernel, out_shape=outs, in_specs=kinds, out_specs=[pl.Bloc...  8.71 us
    all_to_all x1, starting transfers between devices, spread(): return lax.all_to_all(x, AXES, 0, 0, tiled=True, axis_index_groups=groups)  5.43 us
    all_to_all x1, waiting for transfers between devices, spread(): return lax.all_to_all(x, AXES, 0, 0, tiled=True, axis_index_groups=groups)  4.23 us
    ppermute x1, waiting for transfers between devices, body(): corner = lax.ppermute(across, 'cross', [(i, i ^ 2) for i in range(crosses)])  4 us
    ppermute x7, waiting for transfers between devices, swap(): lax.ppermute(message, axis, pairs)  2.15 us
    ppermute x1, starting transfers between devices, body(): corner = lax.ppermute(across, 'cross', [(i, i ^ 2) for i in range(crosses)])  1.93 us
  transfers between devices with their start and end apart: 9, of which 4 were waited for; matrix products, arithmetic and copies ran while one was open for 0% of the time, Pallas kernels for 7%

profile of v4, /device:TPU:0, one launch (start us, length us, event | category | flops | bytes accessed | tf_op | source)
XLA Modules:
  0.0 50.4 jit_solution(15103461598080194326)
XLA Ops:
  0.7 1.6 %shard_map.137 = (f32[16,256]{1,0:T(8,128)}, f32[16,256]{1,0:T(8,128)}) custom-call(f32[256,256]{1,0:T(8,128)} %e_hbm.1, f32[256,256]{1,0:T(8,128)} %p_ref.1, f32[256,256]{1,0:T(8,128)} %q_ref.1, f32[256,256]{1,0:T(8,128)} %c_hbm.1, s32[256,256]{1,0:T(8,128)} %w_hbm.1), custom_call_target="tpu_custom_call" | custom-call | flops 65536 | bytes 1343488 | tf_op jit(solution)/shard_map/pallas_call | solution.py:390
  2.3 0.7 %collective-permute-start = (f32[16,256]{1,0:T(8,128)}, f32[16,256]{1,0:T(8,128)S(1)}, u32[]{:S(2)}, u32[]{:S(2)}) collective-permute-start(f32[16,256]{1,0:T(8,128)} %get-tuple-element.35), channel_id=1, source_target_pairs={{8,16},{16,8},{9,17},{17,9},{10,18},{18,10},{11,19},{19,11},{12,20... | collective-permute-start | bytes 49160 | tf_op jit(solution)/shard_map/ppermute | solution.py:377
  2.9 0.0 copy-start.5
  2.9 0.0 copy-start.6
  3.0 0.0 copy-start.7
  3.0 4.4 %collective-permute-start.1 = (f32[16,256]{1,0:T(8,128)}, f32[16,256]{1,0:T(8,128)S(1)}, u32[]{:S(2)}, u32[]{:S(2)}) collective-permute-start(f32[16,256]{1,0:T(8,128)} %get-tuple-element.36), channel_id=1, source_target_pairs={{0,8},{16,24},{8,0},{24,16},{1,9},{17,25},{9,1},{25,17},{2,10},{18... | collective-permute-start | bytes 49160 | tf_op jit(solution)/shard_map/ppermute | solution.py:377
  7.3 0.0 copy-done
  7.3 0.0 copy-done.3
  7.4 0.4 shard_map.136
  7.8 0.7 %collective-permute-start.2 = (f32[16,256]{1,0:T(8,128)S(1)}, f32[16,256]{1,0:T(8,128)S(1)}, u32[]{:S(2)}, u32[]{:S(2)}) collective-permute-start(f32[16,256]{1,0:T(8,128)S(1)} %get-tuple-element.37), channel_id=1, source_target_pairs={{1,2},{3,4},{5,6},{2,1},{4,3},{6,5},{9,10},{11,12},{13,14},{10,9},... | collective-permute-start | bytes 49160 | tf_op jit(solution)/shard_map/ppermute | solution.py:377
  8.4 4.4 %collective-permute-start.3 = (f32[16,256]{1,0:T(8,128)S(1)}, f32[16,256]{1,0:T(8,128)S(1)}, u32[]{:S(2)}, u32[]{:S(2)}) collective-permute-start(f32[16,256]{1,0:T(8,128)S(1)} %get-tuple-element.38), channel_id=1, source_target_pairs={{0,1},{2,3},{4,5},{6,7},{1,0},{3,2},{5,4},{7,6},{8,9},{10,11},{12,... | collective-permute-start | bytes 49160 | tf_op jit(solution)/shard_map/ppermute | solution.py:377
  12.8 0.0 collective-permute-done.row1
  12.8 0.0 collective-permute-done.1.row0
  12.8 0.0 collective-permute-done.2.col1
  12.8 1.7 %collective-permute-done.3.col0 = f32[16,256]{1,0:T(8,128)S(1)} collective-permute-done((f32[16,256]{1,0:T(8,128)S(1)}, f32[16,256]{1,0:T(8,128)S(1)}, u32[]{:S(2)}, u32[]{:S(2)}) %collective-permute-start.3) | collective-permute-done | bytes 16416 | tf_op jit(solution)/shard_map/ppermute | solution.py:377
  14.5 0.0 copy-start.8
  14.5 1.8 %shard_map.138 = (f32[256,256]{1,0:T(8,128)S(1)}, f32[256,256]{1,0:T(8,128)S(1)}, f32[256,256]{1,0:T(8,128)S(1)}, f32[256,256]{1,0:T(8,128)S(1)}, f32[208,256]{1,0:T(8,128)S(1)}) custom-call(f32[256,256]{1,0:T(8,128)S(1)} %get-tuple-element.30.e_ref, f32[256,256]{1,0:T(8,128)S(1)} %get-tuple-element.31.p_ref.mp_ref, ...), custom_call_target="tpu_custom_call" | custom-call | flops 39321600 | bytes 3293184 | tf_op jit(solution)/shard_map/pallas_call | solution.py:390
  16.3 0.1 collective-permute-start.4
  16.4 1.0 %shard_map.139 = (f32[256,256]{1,0:T(8,128)}, f32[192,256]{1,0:T(8,128)S(1)}, f32[256,128]{1,0:T(8,128)S(1)}) custom-call(f32[256,256]{1,0:T(8,128)S(1)} %get-tuple-element.39.s_ref, f32[256,256]{1,0:T(8,128)S(1)} %get-tuple-element.40.product_ref, f32[256,128]{1,0:T(8,128)S(1)} %copy-done.8, f32[128,256]{1,0:T(8,128)S(1)} %copy-done.6, f32[256,256]{1,0:T(8,128)S(1)} %copy-done.5), custom_call_target="tpu_custom_call" | custom-call | flops 19660800 | bytes 1638400 | tf_op jit(solution)/shard_map/pallas_call | solution.py:390
  17.4 0.4 collective-permute-done.4.got_ref
  17.9 0.7 %shard_map.140 = (f32[16,4,8,128]{3,2,1,0:T(8,128)}, f32[72,256]{1,0:T(8,128)S(1)}) custom-call(f32[192,256]{1,0:T(8,128)S(1)} %get-tuple-element.43.keep_ref, f32[208,256]{1,0:T(8,128)S(1)} %collective-permute-done.4.got_ref, f32[256,128]{1,0:T(8,128)S(1)} %get-tuple-element.44.range_ref), custom_call_target="tpu_custom_call" | custom-call | flops 65536 | bytes 876544 | tf_op jit(solution)/shard_map/pallas_call | solution.py:390
  18.6 5.4 %all-to-all-start = ((f32[16,4,8,128]{3,2,1,0:T(8,128)}), f32[16,4,8,128]{3,2,1,0:T(8,128)S(1)}, u32[]{:S(2)}, u32[]{:S(2)}) async-start(f32[16,4,8,128]{3,2,1,0:T(8,128)} %get-tuple-element.50), calls=%async_computation | async-start | bytes 524288 | tf_op jit(solution)/shard_map/all_to_all | solution.py:442
  24.0 1.9 %collective-permute-start.5 = (f32[72,256]{1,0:T(8,128)S(1)}, f32[72,256]{1,0:T(8,128)S(1)}, u32[]{:S(2)}, u32[]{:S(2)}) collective-permute-start(f32[72,256]{1,0:T(8,128)S(1)} %get-tuple-element.45), channel_id=1, source_target_pairs={{0,16},{8,24},{16,0},{24,8},{1,17},{9,25},{17,1},{25,9},{2,18},{10... | collective-permute-start | bytes 221192 | tf_op jit(solution)/shard_map/ppermute | solution.py:448
  26.0 4.0 %collective-permute-done.5.corner_ref = f32[72,256]{1,0:T(8,128)S(1)} collective-permute-done((f32[72,256]{1,0:T(8,128)S(1)}, f32[72,256]{1,0:T(8,128)S(1)}, u32[]{:S(2)}, u32[]{:S(2)}) %collective-permute-start.5) | collective-permute-done | bytes 73760 | tf_op jit(solution)/shard_map/ppermute | solution.py:448
  30.0 4.2 %all-to-all-done.got = f32[16,4,8,128]{3,2,1,0:T(8,128)S(1)} async-done(((f32[16,4,8,128]{3,2,1,0:T(8,128)}), f32[16,4,8,128]{3,2,1,0:T(8,128)S(1)}, u32[]{:S(2)}, u32[]{:S(2)}) %all-to-all-start) | async-done | bytes 262176 | tf_op jit(solution)/shard_map/all_to_all | solution.py:442
  34.2 12.5 %all_to_all.10.mine = f32[16,4,8,128]{3,2,1,0:T(8,128)S(1)} all-to-all(f32[16,4,8,128]{3,2,1,0:T(8,128)S(1)} %shard_map.142), channel_id=1, replica_groups={{0,1,2,3,4,5,6,7,16,17,18,19,20,21,22,23},{8,9,10,11,12,13,14,15,24,25,..., dimensions={0} | all-to-all | bytes 524288 | tf_op jit(solution)/shard_map/all_to_all | solution.py:442
  46.7 0.0 collective-permute-start.6
  46.7 0.5 %collective-permute-start.7 = (f32[64,256]{1,0:T(8,128)S(1)}, f32[64,256]{1,0:T(8,128)S(1)}, u32[]{:S(2)}, u32[]{:S(2)}) collective-permute-start(f32[64,256]{1,0:T(8,128)S(1)} %slice_add_fusion.rest_0_.thin_mine), channel_id=1, source_target_pairs={{0,8},{16,24},{8,0},{24,16},{1,9},{17,25},{9,1},{25,17},{2,10},{18... | collective-permute-start | bytes 196616 | tf_op jit(solution)/shard_map/ppermute | solution.py:377
  47.2 2.3 %shard_map.141 = (f32[256,256]{1,0:T(8,128)}, f32[256,256]{1,0:T(8,128)}) custom-call(f32[256,256]{1,0:T(8,128)S(1)} %get-tuple-element.30.e_ref, f32[256,256]{1,0:T(8,128)S(1)} %get-tuple-element.31.p_ref.mp_ref, f32[256,256]{1,0:T(8,128)S(1)} %get-tuple-element.32.q_ref.mq_ref, f32[256,256]{1,0:T(8,128)S(1)} %get-tuple-element.33.a_ref, ...), custom_call_target="tpu_custom_call" | custom-call | flops 5242880 | bytes 3235840 | tf_op jit(solution)/shard_map/pallas_call | solution.py:390
  49.5 0.0 collective-permute-done.7.thin_theirs
  49.5 0.0 collective-permute-done.6.theirs
  49.5 0.9 %shard_map.143 = (f32[256,256]{1,0:T(8,128)}, f32[256,128]{1,0:T(8,128)}, f32[128,256]{1,0:T(8,128)}) custom-call(f32[16,4,8,128]{3,2,1,0:T(8,128)S(1)} %all_to_all.10.mine, f32[16,4,8,128]{3,2,1,0:T(8,128)S(1)} %collective-permute-done.6.theirs, f32[64,256]{1,0:T(8,128)S(1)} %slice_add_fusion.rest_0_.thin_mine, f32[64,256]{1,0:T(8,128)S(1)} %collective-permute-done.7.thin_theirs), custom_call_target="tpu_custom_call" | custom-call | flops 65536 | bytes 1179648 | tf_op jit(solution)/shard_map/pallas_call | solution.py:390
  (14 shorter events, 0.1 us)
Async XLA Ops:
  0.6 6.7 %copy-start.1 = (f32[256,256]{1,0:T(8,128)S(1)}, f32[256,256]{1,0:T(8,128)}, u32[]{:S(2)}) copy-start(f32[256,256]{1,0:T(8,128)} %q_ref.1) | copy-start | bytes 786436
  0.6 6.7 %copy-start = (f32[256,256]{1,0:T(8,128)S(1)}, f32[256,256]{1,0:T(8,128)}, u32[]{:S(2)}) copy-start(f32[256,256]{1,0:T(8,128)} %p_ref.1) | copy-start | bytes 786436
  0.7 6.7 %copy-start.4 = (s32[256,256]{1,0:T(8,128)S(1)}, s32[256,256]{1,0:T(8,128)}, u32[]{:S(2)}) copy-start(s32[256,256]{1,0:T(8,128)} %w_hbm.1) | copy-start | bytes 786436
  0.7 6.7 %copy-start.3 = (f32[256,256]{1,0:T(8,128)S(1)}, f32[256,256]{1,0:T(8,128)}, u32[]{:S(2)}) copy-start(f32[256,256]{1,0:T(8,128)} %c_hbm.1) | copy-start | bytes 786436
  0.7 6.7 %copy-start.2 = (f32[256,256]{1,0:T(8,128)S(1)}, f32[256,256]{1,0:T(8,128)}, u32[]{:S(2)}) copy-start(f32[256,256]{1,0:T(8,128)} %e_hbm.1) | copy-start | bytes 786436
  2.3 10.5 %collective-permute-start = (f32[16,256]{1,0:T(8,128)}, f32[16,256]{1,0:T(8,128)S(1)}, u32[]{:S(2)}, u32[]{:S(2)}) collective-permute-start(f32[16,256]{1,0:T(8,128)} %get-tuple-element.35), channel_id=1, source_target_pairs={{8,16},{16,8},{9,17},{17,9},{10,18},{18,10},{11,19},{19,11},{12,20... | collective-permute-start | bytes 49160 | tf_op jit(solution)/shard_map/ppermute | solution.py:377
  2.9 11.6 %copy-start.5 = (f32[256,256]{1,0:T(8,128)S(1)}, f32[256,256]{1,0:T(8,128)}, u32[]{:S(2)}) copy-start(f32[256,256]{1,0:T(8,128)} %left_ref.3) | copy-start | bytes 786436
  2.9 11.5 %copy-start.6 = (f32[128,256]{1,0:T(8,128)S(1)}, f32[128,256]{1,0:T(8,128)}, u32[]{:S(2)}) copy-start(f32[128,256]{1,0:T(8,128)} %cr_ref.3) | copy-start | bytes 393220
  3.0 11.5 %copy-start.7 = (f32[256,256]{1,0:T(8,128)S(1)}, f32[256,256]{1,0:T(8,128)}, u32[]{:S(2)}) copy-start(f32[256,256]{1,0:T(8,128)} %right_ref.1) | copy-start | bytes 786436
  3.0 9.8 %collective-permute-start.1 = (f32[16,256]{1,0:T(8,128)}, f32[16,256]{1,0:T(8,128)S(1)}, u32[]{:S(2)}, u32[]{:S(2)}) collective-permute-start(f32[16,256]{1,0:T(8,128)} %get-tuple-element.36), channel_id=1, source_target_pairs={{0,8},{16,24},{8,0},{24,16},{1,9},{17,25},{9,1},{25,17},{2,10},{18... | collective-permute-start | bytes 49160 | tf_op jit(solution)/shard_map/ppermute | solution.py:377
  7.8 5.0 %collective-permute-start.2 = (f32[16,256]{1,0:T(8,128)S(1)}, f32[16,256]{1,0:T(8,128)S(1)}, u32[]{:S(2)}, u32[]{:S(2)}) collective-permute-start(f32[16,256]{1,0:T(8,128)S(1)} %get-tuple-element.37), channel_id=1, source_target_pairs={{1,2},{3,4},{5,6},{2,1},{4,3},{6,5},{9,10},{11,12},{13,14},{10,9},... | collective-permute-start | bytes 49160 | tf_op jit(solution)/shard_map/ppermute | solution.py:377
  8.4 6.1 %collective-permute-start.3 = (f32[16,256]{1,0:T(8,128)S(1)}, f32[16,256]{1,0:T(8,128)S(1)}, u32[]{:S(2)}, u32[]{:S(2)}) collective-permute-start(f32[16,256]{1,0:T(8,128)S(1)} %get-tuple-element.38), channel_id=1, source_target_pairs={{0,1},{2,3},{4,5},{6,7},{1,0},{3,2},{5,4},{7,6},{8,9},{10,11},{12,... | collective-permute-start | bytes 49160 | tf_op jit(solution)/shard_map/ppermute | solution.py:377
  14.5 1.9 %copy-start.8 = (f32[256,128]{1,0:T(8,128)S(1)}, f32[256,128]{1,0:T(8,128)}, u32[]{:S(2)}) copy-start(f32[256,128]{1,0:T(8,128)} %r_ref.1) | copy-start | bytes 393220
  16.3 1.5 %collective-permute-start.4 = (f32[208,256]{1,0:T(8,128)S(1)}, f32[208,256]{1,0:T(8,128)S(1)}, u32[]{:S(2)}, u32[]{:S(2)}) collective-permute-start(f32[208,256]{1,0:T(8,128)S(1)} %get-tuple-element.42), channel_id=1, source_target_pairs={{0,8},{16,24},{8,0},{24,16},{1,9},{17,25},{9,1},{25,17},{2,10},{18... | collective-permute-start | bytes 638984 | tf_op jit(solution)/shard_map/ppermute | solution.py:377
  18.6 15.6 %all-to-all-start = ((f32[16,4,8,128]{3,2,1,0:T(8,128)}), f32[16,4,8,128]{3,2,1,0:T(8,128)S(1)}, u32[]{:S(2)}, u32[]{:S(2)}) async-start(f32[16,4,8,128]{3,2,1,0:T(8,128)} %get-tuple-element.50), calls=%async_computation | async-start | bytes 524288 | tf_op jit(solution)/shard_map/all_to_all | solution.py:442
  24.0 5.9 %collective-permute-start.5 = (f32[72,256]{1,0:T(8,128)S(1)}, f32[72,256]{1,0:T(8,128)S(1)}, u32[]{:S(2)}, u32[]{:S(2)}) collective-permute-start(f32[72,256]{1,0:T(8,128)S(1)} %get-tuple-element.45), channel_id=1, source_target_pairs={{0,16},{8,24},{16,0},{24,8},{1,17},{9,25},{17,1},{25,9},{2,18},{10... | collective-permute-start | bytes 221192 | tf_op jit(solution)/shard_map/ppermute | solution.py:448
  46.7 2.8 %collective-permute-start.6 = (f32[16,4,8,128]{3,2,1,0:T(8,128)S(1)}, f32[16,4,8,128]{3,2,1,0:T(8,128)S(1)}, u32[]{:S(2)}, u32[]{:S(2)}) collective-permute-start(f32[16,4,8,128]{3,2,1,0:T(8,128)S(1)} %all_to_all.10.mine), channel_id=1, source_target_pairs={{0,8},{16,24},{8,0},{24,16},{1,9},{17,25},{9,1},{25,17},{2,10},{18... | collective-permute-start | bytes 786440 | tf_op jit(solution)/shard_map/ppermute | solution.py:377
  46.7 2.8 %collective-permute-start.7 = (f32[64,256]{1,0:T(8,128)S(1)}, f32[64,256]{1,0:T(8,128)S(1)}, u32[]{:S(2)}, u32[]{:S(2)}) collective-permute-start(f32[64,256]{1,0:T(8,128)S(1)} %slice_add_fusion.rest_0_.thin_mine), channel_id=1, source_target_pairs={{0,8},{16,24},{8,0},{24,16},{1,9},{17,25},{9,1},{25,17},{2,10},{18... | collective-permute-start | bytes 196616 | tf_op jit(solution)/shard_map/ppermute | solution.py:377

commit v5 on v4

--- a/solution.py
+++ b/solution.py
@@ -11,6 +11,7 @@
 ROWS = 8
 LANES = 128
 WINDOW = 64
+ROOM = 56_450_000
 
 
 def f32(*shape):
@@ -111,10 +112,13 @@
     return pick
 
 
-def col_pick(even, first, second):
+def turn_back(even, first, second):
     right, left = jnp.where(even, first, second), jnp.where(even, second, first)
     gap = jnp.zeros((LANES - 2 * ROWS, right.shape[1]), right.dtype)
-    both = jnp.concatenate([right, gap, left], axis=0).T
+    return jnp.concatenate([right, gap, left], axis=0).T
+
+
+def lane_pick(both):
     lane = place(both.shape, LANES, 1)
 
     def pick(count, shift):
@@ -123,6 +127,10 @@
         return jnp.where(lane < count, low, jnp.where(lane >= LANES - count, high, 0.0))
 
     return pick
+
+
+def col_pick(even, first, second):
+    return lane_pick(turn_back(even, first, second))
 
 
 def split(a):
@@ -168,19 +176,17 @@
     return with_ring(part, ring, start, step, rows)
 
 
-def surface_kernel(
-    e_ref, p_ref, q_ref, a_ref, f_ref, row1, row0, col1, col0,
-    cr_ref, left_ref, right_ref, s_ref, sum_p, sum_q, product_ref, give_ref,
+def halo_of(pick):
+    e, mass, slope = pick(4, 0), pick(2, 4), pick(2, 6)
+    return e, (2.0 - friction_of(slope)) * mass, slope
+
+
+def inner_kernel(
+    e_ref, p_ref, q_ref, a_ref, f_ref, row1, row0, cr_ref, left_ref, right_ref,
+    s_ref, sum_p, sum_q, give_ref,
 ):
     rows, cols = e_ref.shape
-    even_row, even_col = parity("cross") == 0, parity("along") == 0
-
-    def halo(pick):
-        e, mass, slope = pick(4, 0), pick(2, 4), pick(2, 6)
-        return e, (2.0 - friction_of(slope)) * mass, slope
-
-    e_row, g_row, a_row = halo(row_pick(even_row, row0[:ROWS], row1[:ROWS]))
-    e_col, g_col, a_col = halo(col_pick(even_col, col0[:ROWS], col1[:ROWS]))
+    e_row, g_row, a_row = halo_of(row_pick(parity("cross") == 0, row0[:ROWS], row1[:ROWS]))
     for start, step in windows(rows):
         inner = slice(start, start + step)
         grad = derive(window(e_ref, e_row, start, step), 0)
@@ -190,41 +196,83 @@
         total -= 0.5 * slope * grad
         sum_p[inner, :] = total[ROWS : ROWS + step]
         change = derive(total, 0)[ROWS : ROWS + step]
-        grad = derive(join(e_ref[inner, :], e_col[inner], 1), 1)
         slope = a_ref[inner, :]
-        total = (2.0 - f_ref[inner, :]) * q_ref[inner, :]
-        total = join(total, g_col[inner], 1) - 0.5 * join(slope, a_col[inner], 1) * grad
-        sum_q[inner, :] = total[:, :cols]
-        change += derive(total, 1)[:, :cols]
+        grad = derive(e_ref[inner, :], 1)
+        total = (2.0 - f_ref[inner, :]) * q_ref[inner, :] - 0.5 * slope * grad
+        sum_q[inner, :] = total
+        lane = place(total.shape, LANES, 1)
+        change += jnp.where((lane >= 4) & (lane < cols - 4), derive(total, 1), 0.0)
         s_ref[inner, :] = 0.5 * e_ref[inner, :] - jnp.where(slope > 0.0, 0.125 * change, 0.0)
+    give_ref[...] = halves(1 - parity("cross"), left_ref, right_ref, cr_ref, s_ref)
+
+
+def surface_kernel(
+    e_ref, q_ref, a_ref, f_ref, s_in, sum_in, give_in, col1, col0, cr_ref, left_ref, right_ref,
+    s_ref, sum_q, give_ref,
+):
+    rows, cols = e_ref.shape
+    even_row, even_col = parity("cross") == 0, parity("along") == 0
+    lane = place((rows, LANES), LANES, 1)
+    half = LANES // 2
+    first, last = slice(0, LANES), slice(cols - LANES, cols)
+
+    def edges(tile, halo):
+        ends = pltpu.roll(tile(last), half, 1)
+        beyond = jnp.where(lane < half + ROWS, pltpu.roll(halo, half, 1), halo)
+        own = jnp.where(lane < ROWS, tile(first), jnp.where(lane < half - ROWS, 0.0, ends))
+        return jnp.where(lane < half, own, beyond)
+
+    e_col, g_col, a_col = halo_of(col_pick(even_col, col0[:ROWS], col1[:ROWS]))
+    e = edges(lambda where: e_ref[:, where], e_col)
+    slope = edges(lambda where: a_ref[:, where], a_col)
+    total = edges(lambda where: (2.0 - f_ref[:, where]) * q_ref[:, where], g_col)
+    total -= 0.5 * slope * derive(e, 1)
+    change = jnp.where(slope > 0.0, 0.125 * derive(total, 1), 0.0)
+    total_last, change_last = pltpu.roll(total, half, 1), pltpu.roll(change, half, 1)
+    sum_q[...] = sum_in[...]
+    sum_q[:, first] = jnp.where(lane < 2, total, sum_in[:, first])
+    sum_q[:, last] = jnp.where(lane >= LANES - 2, total_last, sum_in[:, last])
+    s_ref[...] = s_in[...]
+    s_ref[:, first] = s_in[:, first] - jnp.where(lane < 4, change, 0.0)
+    s_ref[:, last] = s_in[:, last] - jnp.where(lane >= LANES - 4, change_last, 0.0)
+    added = split(jnp.where((lane < 4) | ((lane >= half - 4) & (lane < half)), -change, 0.0))
+    side = 1 - parity("cross")
+    left, thin = half_of(side, left_ref), half_of(side, cr_ref)
+    cut = left.shape[0]
+    partial = dot_split(split(join(left, thin, 0)), added)
+    right = join(right_ref[: half - ROWS, :], right_ref[cols - ROWS :, :], 0)
+    right = join(right, right_ref[:half, :], 0)
+    give_ref[:cut, :] = give_in[:cut, :] + dot_split(split(partial[:cut]), split(right))
+    thin = partial[cut:]
+    tail = give_in.shape[0]
+    give_ref[cut:tail, :] = give_in[cut:, :]
+    at = lane[: tail - cut]
+    give_ref[cut:tail, first] += jnp.where(at < 4, thin, 0.0)
+    give_ref[cut:tail, last] += jnp.where(at >= LANES - 4, pltpu.roll(thin, half, 1), 0.0)
+    both = turn_back(even_col, col0[ROWS:], col1[ROWS:])
+    picks = lane_pick(both[:ROWS]), lane_pick(both[rows - ROWS :])
+    up, down = (join(pick(4, 0), pick(2, 4), 1) for pick in picks)
+    give_ref[tail:, :] = jnp.where(even_row, join(down, up, 0), join(up, down, 0))
+
+
+def half_of(side, ref):
+    count = ref.shape[0] // 2
+    return ref[pl.ds(pl.multiple_of(side * count, count), count), :]
+
+
+def halves(side, left_ref, right_ref, cr_ref, s_ref):
     s = split(s_ref[...])
-    pick = col_pick(even_col, col0[ROWS:], col1[ROWS:])
-    around = join(pick(4, 0), pick(2, 4), 1)
-    up, down = around[:ROWS], around[rows - ROWS :]
-    tail = give_ref.shape[0] - 2 * ROWS
-    give_ref[tail:, :] = jnp.where(even_row, join(down, up, 0), join(up, down, 0))
-    product = dot_split(s, split(right_ref[...]))
-    product_ref[...] = product
-    give_ref[:tail, :] = halves(
-        1 - parity("cross"), left_ref, split(product), cr_ref, s
-    )
-
-
-def halves(side, left_ref, product, cr_ref, s):
-    half, thin = left_ref.shape[0] // 2, cr_ref.shape[0] // 2
-    left = left_ref[pl.ds(pl.multiple_of(side * half, half), half), :]
-    core = dot_split(split(left), product)
-    thin_rows = cr_ref[pl.ds(pl.multiple_of(side * thin, thin), thin), :]
-    return join(core, dot_split(split(thin_rows), s), 0)
+    product = split(dot_split(s, split(right_ref[...])))
+    core = dot_split(split(half_of(side, left_ref)), product)
+    return join(core, dot_split(split(half_of(side, cr_ref)), s), 0)
 
 
 def product_kernel(
-    s_ref, product_ref, r_ref, cr_ref, left_ref, s_hbm, keep_ref, range_ref, sems
+    s_ref, r_ref, cr_ref, left_ref, right_ref, s_hbm, keep_ref, range_ref, sems
 ):
     copies = start(pieces(s_ref, s_hbm, sems))
-    s = split(s_ref[...])
-    keep_ref[...] = halves(parity("cross"), left_ref, split(product_ref[...]), cr_ref, s)
-    range_ref[...] = dot_split(s, split(r_ref[...]))
+    keep_ref[...] = halves(parity("cross"), left_ref, right_ref, cr_ref, s_ref)
+    range_ref[...] = dot(s_ref[...], r_ref[...])
     for copy in copies:
         copy.wait()
 
@@ -320,12 +368,12 @@
         copy.wait()
 
 
-def flux_kernel(
-    e_ref, mp_ref, mq_ref, a_ref, f_ref, row1, row0, col1, col0, got_ref, corner_ref,
-    p_ref, q_ref, sum_p, sum_q, p_hbm, q_hbm, next_p, next_q, sems,
+def both_kernel(
+    e_ref, mp_ref, mq_ref, a_ref, row1, row0, col1, col0, after,
+    both_ref, both_row, both_col, quarter_row, quarter_col,
 ):
+    del after
     rows, cols = e_ref.shape
-    copies = []
     even_row, even_col = parity("cross") == 0, parity("along") == 0
     pick = row_pick(even_row, row0[:ROWS], row1[:ROWS])
     e_row, a_row = pick(4, 0), pick(2, 6)
@@ -335,27 +383,47 @@
     e_col, a_col = pick(4, 0), pick(2, 6)
     pick = col_pick(even_col, col0[ROWS:], col1[ROWS:])
     q_col, p_col = pick(4, 0), pick(2, 4)
+    quarter_row[...] = jnp.where(a_row > 0.0, 0.25, 0.0)
+    quarter_col[...] = jnp.where(a_col > 0.0, 0.25, 0.0)
+    none = jnp.zeros((ROWS, LANES), e_ref.dtype)
+    ends = []
+    for start, step in windows(rows):
+
+        def ring(tile, row, col):
+            return join(window(tile, row, start, step), window(col, none, start, step), 1)
+
+        spread = derive(ring(mp_ref, p_row, p_col), 0) + derive(ring(mq_ref, q_row, q_col), 1)
+        wet = ring(a_ref, a_row, a_col) > 0.0
+        both = ring(e_ref, e_row, e_col) - jnp.where(wet, 0.25 * spread, 0.0)
+        inner = slice(start, start + step)
+        both_ref[inner, :] = both[ROWS : ROWS + step, :cols]
+        both_col[inner, :] = both[ROWS : ROWS + step, cols:]
+        ends += [both[:ROWS, :cols], both[ROWS + step :, :cols]]
+    at = place((ROWS, cols), ROWS, 0)
+    both_row[...] = jnp.where(at < ROWS // 2, ends[-1], ends[0])
+
+
+def flux_kernel(
+    both_ref, both_row, both_col, quarter_row, quarter_col, a_ref, f_ref, got_ref, corner_ref,
+    p_ref, q_ref, sum_p, sum_q, p_hbm, q_hbm, next_p, next_q, sems,
+):
+    rows, cols = both_ref.shape
+    copies = []
     row = lax.axis_index("cross")
     inside = (row > 0) & (row < lax.axis_size("cross") - 1)
     beyond = jnp.where(inside, corner_ref[corner_ref.shape[0] - ROWS :], 0.0)
     near = got_ref.shape[0] - 2 * ROWS
-    pick = row_pick(even_row, got_ref[near : near + ROWS], beyond)
+    pick = row_pick(parity("cross") == 0, got_ref[near : near + ROWS], beyond)
     corners = pick(2, 0)
-    none = jnp.zeros((ROWS, LANES), e_ref.dtype)
+    dtype = both_ref.dtype
+    extra = derive(join(jnp.zeros((ROWS, cols), dtype), corners[:, :LANES], 1), 1)[:, :cols]
+    rim_rows = both_row[...] - quarter_row[...] * extra
+    extra = derive(join(jnp.zeros((rows, LANES), dtype), corners[:, LANES:], 0), 0)[:rows]
+    rim_cols = both_col[...] - quarter_col[...] * extra
     for i, (start, step) in enumerate(windows(rows)):
-
-        def ring(tile, row, col, corner):
-            return join(
-                window(tile, row, start, step), window(col, corner, start, step), 1
-            )
-
-        spread = derive(ring(mp_ref, p_row, p_col, corners[:, LANES:]), 0)
-        spread += derive(ring(mq_ref, q_row, q_col, corners[:, :LANES]), 1)
-        wet = ring(a_ref, a_row, a_col, none) > 0.0
-        both = ring(e_ref, e_row, e_col, none) - jnp.where(wet, 0.25 * spread, 0.0)
         inner = slice(start, start + step)
-        grad_x = derive(both[:, :cols], 0)[ROWS : ROWS + step]
-        grad_y = derive(both[ROWS : ROWS + step], 1)[:, :cols]
+        grad_x = derive(window(both_ref, rim_rows, start, step), 0)[ROWS : ROWS + step]
+        grad_y = derive(join(both_ref[inner, :], rim_cols[inner], 1), 1)[:, :cols]
         slope, friction = 0.5 * a_ref[inner, :], 0.5 * f_ref[inner, :]
         next_p[inner, :] = p_ref[inner, :] - (slope * grad_x + friction * sum_p[inner, :])
         next_q[inner, :] = q_ref[inner, :] - (slope * grad_y + friction * sum_q[inner, :])
@@ -382,7 +450,7 @@
     rows, cols = e.shape
     cells = rows * cols
 
-    def run(kernel, outs, flops, *args, idle=(), scratch=(), to=None, space=pltpu.VMEM, limit=32):
+    def run(kernel, outs, flops, *args, idle=(), scratch=(), to=None, space=pltpu.VMEM, limit=32 << 20):
         kinds = [pl.BlockSpec(memory_space=space)] * len(args)
         kinds += [pl.BlockSpec(memory_space=pl.ANY)] * len(idle)
         moved = sum(a.size * 4 for a in args) + sum(o.size * 4 for o in outs)
@@ -394,13 +462,13 @@
             out_specs=[pl.BlockSpec(memory_space=kind) for kind in to],
             scratch_shapes=list(scratch),
             cost_estimate=pl.CostEstimate(flops=flops, bytes_accessed=moved, transcendentals=0),
-            compiler_params=pltpu.CompilerParams(vmem_limit_bytes=limit * 1024 * 1024),
+            compiler_params=pltpu.CompilerParams(vmem_limit_bytes=limit),
         )(*args, *idle)
 
     held = [pltpu.VMEM((2, ROWS, cols), a.dtype) for a in (e, p, q, c, w)]
     row0, row1 = run(
         row_kernel, [f32(2 * ROWS, cols)] * 2, cells, e, p, q, c, w, space=pltpu.HBM,
-        scratch=held + [pltpu.SemaphoreType.DMA((5, 2))], limit=60,
+        scratch=held + [pltpu.SemaphoreType.DMA((5, 2))], limit=ROOM,
     )
     row1, row0 = swap(row1, "cross", 1), swap(row0, "cross", 0)
     tile = f32(rows, cols)
@@ -413,11 +481,17 @@
     corange_shape = f32(corange_test.shape[0], cols)
     core_shape = f32(core_left.shape[0], core_right.shape[1])
     half, thin = core_shape.shape[0] // 2, corange_shape.shape[0] // 2
-    outs = [tile] * 3 + [f32(rows, core_shape.shape[1])]
-    outs += [f32(half + thin + 2 * ROWS, cols)]
-    s_held, sum_p, sum_q, product, give = run(
-        surface_kernel, outs, 600 * cells,
-        *fields, *halo, corange_test, core_left, core_right,
+    e2, mass_x, mass_y, slope, friction = fields
+    row1, row0, col1, col0 = halo
+    tests = (corange_test, core_left, core_right)
+    s_part, sum_p, sum_q, give = run(
+        inner_kernel, [tile] * 3 + [f32(half + thin, cols)], 600 * cells,
+        *fields, row1, row0, *tests,
+    )
+    outs = [tile] * 2 + [f32(half + thin + 2 * ROWS, cols)]
+    s_held, sum_q, give = run(
+        surface_kernel, outs, 200 * cells,
+        e2, mass_y, slope, friction, s_part, sum_q, give, col1, col0, *tests,
     )
     got = swap(give, "cross", 0)
     count = crosses // 2 * alongs
@@ -425,9 +499,10 @@
     keep_shape = f32(half + thin, cols)
     s_next, keep, ranged = run(
         product_kernel, [tile, keep_shape, range_shape], 300 * cells,
-        s_held, product, range_test, corange_test, core_left,
+        s_held, range_test, *tests,
         to=[pltpu.HBM, pltpu.VMEM, pltpu.VMEM], scratch=[pltpu.SemaphoreType.DMA((4,))],
     )
+    rim_shapes = [tile] + [f32(ROWS, cols), f32(rows, LANES)] * 2
     shared = crosses == 4 and not any(size % (count * ROWS * LANES) for size in sizes)
     if shared:
         per = [size // (count * ROWS * LANES) for size in sizes]
@@ -445,12 +520,13 @@
             functools.partial(merge_kernel, half), [sheet, f32(thin + ROWS, cols)], sheet.size,
             keep, got, ranged,
         )
+        rims = run(both_kernel, rim_shapes, 60 * cells, e2, mass_x, mass_y, slope, *halo, across)
         corner = lax.ppermute(across, "cross", [(i, i ^ 2) for i in range(crosses)])
         thin_mine = across[:thin] + corner[:thin]
         thin_theirs = swap(thin_mine, "cross", 0)
         (totals,) = run(
             functools.partial(sum_kernel, crosses // 2, alongs, cuts), [sheet], sheet.size,
-            spread(shares), idle=[thin_mine],
+            spread(shares), idle=[thin_mine, rims[1]],
         )
         mine = spread(totals)
         theirs = swap(mine, "cross", 0)
@@ -463,11 +539,13 @@
         )
     else:
         corner = swap(give[-ROWS:], "cross", 1)
+        rims = run(both_kernel, rim_shapes, 60 * cells, e2, mass_x, mass_y, slope, *halo, give)
         ranged = lax.psum(ranged, "along")
         coranged = lax.psum(dot(corange_test, s_held), "cross")
-        core = lax.psum(dot(core_left, product), AXES)
+        core = lax.psum(dot(core_left, dot(s_held, core_right)), AXES)
     p_next, q_next = run(
-        flux_kernel, [tile] * 2, 80 * cells, *fields, *halo, got, corner, p, q, sum_p, sum_q,
+        flux_kernel, [tile] * 2, 40 * cells,
+        *rims, slope, friction, got, corner, p, q, sum_p, sum_q,
         to=[pltpu.HBM] * 2,
         scratch=[pltpu.VMEM((rows, cols), jnp.float32)] * 2
         + [pltpu.SemaphoreType.DMA((2, len(list(windows(rows)))))],

time: 50.8 us -> 49 us (0.965)
  waiting for transfers between devices: 10.4 us -> 6.22 us
  local copies, waits for them, and re-layouts: 0.05 us -> 2.14 us
    ppermute x1, waiting for transfers between devices: 4 us -> 1.33 us  [body(): corner = lax.ppermute(across, 'cross', [(i, i ^ 2) for i in range(crosses)])]
    unnamed x18 -> x30, local copies, waits for them, and re-layouts: 0.05 us -> 2.14 us
    ppermute x7, waiting for transfers between devices: 2.15 us -> 0.67 us  [swap(): lax.ppermute(message, axis, pairs)]
    pallas_call x8 -> x10, Pallas kernels: 8.71 us -> 8.71 us  [run(): pl.pallas_call(kernel, out_shape=outs, in_specs=kinds, out_specs=[pl.Bloc...]
  transfers between devices with their start and end apart: 9 -> 9, of which waited for: 4 -> 4; matrix products, arithmetic and copies ran while one was open for 0% -> 0% of each run, Pallas kernels for 7% -> 10%
where the time goes in v5:
time: 49 us; the launch traced here: 48.4 us
  starting transfers between devices  18 us (37%)
  blocking collectives  12.5 us (26%)
  Pallas kernels  8.71 us (18%)
  waiting for transfers between devices  6.22 us (13%)
  local copies, waits for them, and re-layouts  2.14 us (4%)
  between operations  0.88 us (2%)
    all_to_all x1, blocking collectives, spread(): return lax.all_to_all(x, AXES, 0, 0, tiled=True, axis_index_groups=groups)  12.5 us
    ppermute x7, starting transfers between devices, swap(): lax.ppermute(message, axis, pairs)  10.6 us
    pallas_call x10, Pallas kernels, run(): pl.pallas_call(kernel, out_shape=outs, in_specs=kinds, out_specs=[pl.Bloc...  8.71 us
    all_to_all x1, starting transfers between devices, spread(): return lax.all_to_all(x, AXES, 0, 0, tiled=True, axis_index_groups=groups)  5.42 us
    all_to_all x1, waiting for transfers between devices, spread(): return lax.all_to_all(x, AXES, 0, 0, tiled=True, axis_index_groups=groups)  4.22 us
    unnamed x30, local copies, waits for them, and re-layouts  2.14 us
    ppermute x1, starting transfers between devices, body(): corner = lax.ppermute(across, 'cross', [(i, i ^ 2) for i in range(crosses)])  1.93 us
    ppermute x1, waiting for transfers between devices, body(): corner = lax.ppermute(across, 'cross', [(i, i ^ 2) for i in range(crosses)])  1.33 us
  transfers between devices with their start and end apart: 9, of which 4 were waited for; matrix products, arithmetic and copies ran while one was open for 0% of the time, Pallas kernels for 10%

profile of v5, /device:TPU:0, one launch (start us, length us, event | category | flops | bytes accessed | tf_op | source)
XLA Modules:
  0.0 48.4 jit_solution(11448237958428141723)
XLA Ops:
  0.7 1.0 %shard_map.137 = (f32[16,256]{1,0:T(8,128)S(1)}, f32[16,256]{1,0:T(8,128)S(1)}) custom-call(f32[256,256]{1,0:T(8,128)} %e_hbm.1, f32[256,256]{1,0:T(8,128)} %p_ref.1, f32[256,256]{1,0:T(8,128)} %q_ref.1, f32[256,256]{1,0:T(8,128)} %c_hbm.1, s32[256,256]{1,0:T(8,128)} %w_hbm.1), custom_call_target="tpu_custom_call" | custom-call | flops 65536 | bytes 1343488 | tf_op jit(solution)/shard_map/pallas_call | solution.py:458
  1.7 0.7 %collective-permute-start = (f32[16,256]{1,0:T(8,128)S(1)}, f32[16,256]{1,0:T(8,128)S(1)}, u32[]{:S(2)}, u32[]{:S(2)}) collective-permute-start(f32[16,256]{1,0:T(8,128)S(1)} %get-tuple-element.42), channel_id=1, source_target_pairs={{8,16},{16,8},{9,17},{17,9},{10,18},{18,10},{11,19},{19,11},{12,20... | collective-permute-start | bytes 49160 | tf_op jit(solution)/shard_map/ppermute | solution.py:445
  2.3 0.0 copy-start.2
  2.3 0.0 copy-start.3
  2.3 0.0 copy-start.4
  2.4 4.4 %collective-permute-start.1 = (f32[16,256]{1,0:T(8,128)S(1)}, f32[16,256]{1,0:T(8,128)S(1)}, u32[]{:S(2)}, u32[]{:S(2)}) collective-permute-start(f32[16,256]{1,0:T(8,128)S(1)} %get-tuple-element.43), channel_id=1, source_target_pairs={{0,8},{16,24},{8,0},{24,16},{1,9},{17,25},{9,1},{25,17},{2,10},{18... | collective-permute-start | bytes 49160 | tf_op jit(solution)/shard_map/ppermute | solution.py:445
  6.8 0.4 shard_map.136
  7.2 0.7 %collective-permute-start.2 = (f32[16,256]{1,0:T(8,128)S(1)}, f32[16,256]{1,0:T(8,128)S(1)}, u32[]{:S(2)}, u32[]{:S(2)}) collective-permute-start(f32[16,256]{1,0:T(8,128)S(1)} %get-tuple-element.47), channel_id=1, source_target_pairs={{1,2},{3,4},{5,6},{2,1},{4,3},{6,5},{9,10},{11,12},{13,14},{10,9},... | collective-permute-start | bytes 49160 | tf_op jit(solution)/shard_map/ppermute | solution.py:445
  7.8 4.4 %collective-permute-start.3 = (f32[16,256]{1,0:T(8,128)S(1)}, f32[16,256]{1,0:T(8,128)S(1)}, u32[]{:S(2)}, u32[]{:S(2)}) collective-permute-start(f32[16,256]{1,0:T(8,128)S(1)} %get-tuple-element.48), channel_id=1, source_target_pairs={{0,1},{2,3},{4,5},{6,7},{1,0},{3,2},{5,4},{7,6},{8,9},{10,11},{12,... | collective-permute-start | bytes 49160 | tf_op jit(solution)/shard_map/ppermute | solution.py:445
  12.2 0.0 collective-permute-done.row1
  12.2 0.0 collective-permute-done.1.row0
  12.2 1.3 %shard_map.138 = (f32[256,256]{1,0:T(8,128)S(1)}, f32[256,256]{1,0:T(8,128)S(1)}, f32[256,256]{1,0:T(8,128)S(1)}, f32[192,256]{1,0:T(8,128)S(1)}) custom-call(f32[256,256]{1,0:T(8,128)S(1)} %get-tuple-element.37.e_ref, f32[256,256]{1,0:T(8,128)S(1)} %get-tuple-element.41.p_ref.mp_ref, f32[256,256]{1,0:T(8,128)S(1)} %get-tuple-element.38.q_ref.mq_ref, ...), custom_call_target="tpu_custom_call" | custom-call | flops 39321600 | bytes 2981888 | tf_op jit(solution)/shard_map/pallas_call | solution.py:458
  13.6 0.3 collective-permute-done.3.col0
  13.9 1.2 %shard_map.139 = (f32[256,256]{1,0:T(8,128)S(1)}, f32[256,256]{1,0:T(8,128)S(1)}, f32[208,256]{1,0:T(8,128)S(1)}) custom-call(f32[256,256]{1,0:T(8,128)S(1)} %get-tuple-element.37.e_ref, f32[256,256]{1,0:T(8,128)S(1)} %get-tuple-element.38.q_ref.mq_ref, f32[256,256]{1,0:T(8,128)S(1)} %get-tuple-element.39.a_ref, f32[256,256]{1,0:T(8,128)S(1)} %get-tuple-element.40.f_ref, ...), custom_call_target="tpu_custom_call" | custom-call | flops 13107200 | bytes 3194880 | tf_op jit(solution)/shard_map/pallas_call | solution.py:458
  15.1 0.1 collective-permute-start.4
  15.2 1.1 %shard_map.140 = (f32[256,256]{1,0:T(8,128)}, f32[192,256]{1,0:T(8,128)S(1)}, f32[256,128]{1,0:T(8,128)S(1)}) custom-call(f32[256,256]{1,0:T(8,128)S(1)} %get-tuple-element.49.s_ref, f32[256,128]{1,0:T(8,128)S(1)} %copy-done.8, f32[128,256]{1,0:T(8,128)S(1)} %copy-done.4, f32[256,256]{1,0:T(8,128)S(1)} %copy-done.2, f32[256,256]{1,0:T(8,128)S(1)} %copy-done.3), custom_call_target="tpu_custom_call" | custom-call | flops 19660800 | bytes 1638400 | tf_op jit(solution)/shard_map/pallas_call | solution.py:458
  16.3 0.3 collective-permute-done.4.got_ref
  16.6 0.7 %shard_map.141 = (f32[16,4,8,128]{3,2,1,0:T(8,128)}, f32[72,256]{1,0:T(8,128)S(1)}) custom-call(f32[192,256]{1,0:T(8,128)S(1)} %get-tuple-element.51.keep_ref, f32[208,256]{1,0:T(8,128)S(1)} %collective-permute-done.4.got_ref, f32[256,128]{1,0:T(8,128)S(1)} %get-tuple-element.53.range_ref), custom_call_target="tpu_custom_call" | custom-call | flops 65536 | bytes 876544 | tf_op jit(solution)/shard_map/pallas_call | solution.py:458
  17.4 5.4 %all-to-all-start = ((f32[16,4,8,128]{3,2,1,0:T(8,128)}), f32[16,4,8,128]{3,2,1,0:T(8,128)S(1)}, u32[]{:S(2)}, u32[]{:S(2)}) async-start(f32[16,4,8,128]{3,2,1,0:T(8,128)} %get-tuple-element.64), calls=%async_computation | async-start | bytes 524288 | tf_op jit(solution)/shard_map/all_to_all | solution.py:517
  22.8 1.9 %collective-permute-start.5 = (f32[72,256]{1,0:T(8,128)S(1)}, f32[72,256]{1,0:T(8,128)S(1)}, u32[]{:S(2)}, u32[]{:S(2)}) collective-permute-start(f32[72,256]{1,0:T(8,128)S(1)} %get-tuple-element.54.after), channel_id=1, source_target_pairs={{0,16},{8,24},{16,0},{24,8},{1,17},{9,25},{17,1},{25,9},{2,18},{10... | collective-permute-start | bytes 221192 | tf_op jit(solution)/shard_map/ppermute | solution.py:524
  24.7 0.7 %copy-done.10 = f32[16,256]{1,0:T(8,128)S(1)} copy-done((f32[16,256]{1,0:T(8,128)S(1)}, f32[16,256]{1,0:T(8,128)}, u32[]{:S(2)}) %copy-start.10) | copy-done | bytes 16408
  25.5 0.8 %shard_map.142 = (f32[256,256]{1,0:T(8,128)S(1)}, f32[8,256]{1,0:T(8,128)S(1)}, f32[256,128]{1,0:T(8,128)S(1)}, f32[8,256]{1,0:T(8,128)S(1)}, f32[256,128]{1,0:T(8,128)S(1)}) custom-call(f32[256,256]{1,0:T(8,128)S(1)} %get-tuple-element.37.e_ref, f32[256,256]{1,0:T(8,128)S(1)} %get-tuple-element.41.p_ref.mp_ref, ...), custom_call_target="tpu_custom_call" | custom-call | flops 3932160 | bytes 1728512 | tf_op jit(solution)/shard_map/pallas_call | solution.py:458
  26.3 0.0 copy-start.11
  26.3 0.6 %copy-done.11 = f32[8,256]{1,0:T(8,128)} copy-done((f32[8,256]{1,0:T(8,128)}, f32[8,256]{1,0:T(8,128)S(1)}, u32[]{:S(2)}) %copy-start.11) | copy-done | bytes 8216
  26.9 0.6 %copy-done.13 = f32[8,256]{1,0:T(8,128)} copy-done((f32[8,256]{1,0:T(8,128)}, f32[8,256]{1,0:T(8,128)S(1)}, u32[]{:S(2)}) %copy-start.13) | copy-done | bytes 8216
  27.5 1.3 %collective-permute-done.5.corner_ref = f32[72,256]{1,0:T(8,128)S(1)} collective-permute-done((f32[72,256]{1,0:T(8,128)S(1)}, f32[72,256]{1,0:T(8,128)S(1)}, u32[]{:S(2)}, u32[]{:S(2)}) %collective-permute-start.5) | collective-permute-done | bytes 73760 | tf_op jit(solution)/shard_map/ppermute | solution.py:524
  28.8 4.2 %all-to-all-done.got = f32[16,4,8,128]{3,2,1,0:T(8,128)S(1)} async-done(((f32[16,4,8,128]{3,2,1,0:T(8,128)}), f32[16,4,8,128]{3,2,1,0:T(8,128)S(1)}, u32[]{:S(2)}, u32[]{:S(2)}) %all-to-all-start) | async-done | bytes 262176 | tf_op jit(solution)/shard_map/all_to_all | solution.py:517
  33.1 12.5 %all_to_all.10.mine = f32[16,4,8,128]{3,2,1,0:T(8,128)S(1)} all-to-all(f32[16,4,8,128]{3,2,1,0:T(8,128)S(1)} %shard_map.144), channel_id=1, replica_groups={{0,1,2,3,4,5,6,7,16,17,18,19,20,21,22,23},{8,9,10,11,12,13,14,15,24,25,..., dimensions={0} | all-to-all | bytes 524288 | tf_op jit(solution)/shard_map/all_to_all | solution.py:517
  45.6 0.5 %collective-permute-start.7 = (f32[64,256]{1,0:T(8,128)S(1)}, f32[64,256]{1,0:T(8,128)S(1)}, u32[]{:S(2)}, u32[]{:S(2)}) collective-permute-start(f32[64,256]{1,0:T(8,128)S(1)} %slice_add_fusion.rest_0_.thin_mine), channel_id=1, source_target_pairs={{0,8},{16,24},{8,0},{24,16},{1,9},{17,25},{9,1},{25,17},{2,10},{18... | collective-permute-start | bytes 196616 | tf_op jit(solution)/shard_map/ppermute | solution.py:445
  46.1 0.2 copy-done.14
  46.2 1.2 %shard_map.143 = (f32[256,256]{1,0:T(8,128)}, f32[256,256]{1,0:T(8,128)}) custom-call(f32[256,256]{1,0:T(8,128)S(1)} %get-tuple-element.55.both_ref, f32[8,256]{1,0:T(8,128)S(1)} %copy-done.12, f32[256,128]{1,0:T(8,128)S(1)} %get-tuple-element.57.both_col, f32[8,256]{1,0:T(8,128)S(1)} %copy-done.14, f32[256,128]{1,0:T(8,128)S(1)} %get-tuple-element.59.quarter_col, ...), custom_call_target="tpu_custom_call" | custom-call | flops 2621440 | bytes 2924544 | tf_op jit(solution)/shard_map/pallas_call | solution.py:458
  47.5 0.9 %shard_map.145 = (f32[256,256]{1,0:T(8,128)}, f32[256,128]{1,0:T(8,128)}, f32[128,256]{1,0:T(8,128)}) custom-call(f32[16,4,8,128]{3,2,1,0:T(8,128)S(1)} %all_to_all.10.mine, f32[16,4,8,128]{3,2,1,0:T(8,128)S(1)} %collective-permute-done.6.theirs, f32[64,256]{1,0:T(8,128)S(1)} %slice_add_fusion.rest_0_.thin_mine, f32[64,256]{1,0:T(8,128)S(1)} %collective-permute-done.7.thin_theirs), custom_call_target="tpu_custom_call" | custom-call | flops 65536 | bytes 1179648 | tf_op jit(solution)/shard_map/pallas_call | solution.py:458
  (28 shorter events, 0.1 us)
Async XLA Ops:
  0.6 6.1 %copy-start.1 = (f32[256,256]{1,0:T(8,128)S(1)}, f32[256,256]{1,0:T(8,128)}, u32[]{:S(2)}) copy-start(f32[256,256]{1,0:T(8,128)} %q_ref.1) | copy-start | bytes 786436
  0.6 6.1 %copy-start = (f32[256,256]{1,0:T(8,128)S(1)}, f32[256,256]{1,0:T(8,128)}, u32[]{:S(2)}) copy-start(f32[256,256]{1,0:T(8,128)} %p_ref.1) | copy-start | bytes 786436
  0.7 6.1 %copy-start.7 = (s32[256,256]{1,0:T(8,128)S(1)}, s32[256,256]{1,0:T(8,128)}, u32[]{:S(2)}) copy-start(s32[256,256]{1,0:T(8,128)} %w_hbm.1) | copy-start | bytes 786436
  0.7 6.1 %copy-start.6 = (f32[256,256]{1,0:T(8,128)S(1)}, f32[256,256]{1,0:T(8,128)}, u32[]{:S(2)}) copy-start(f32[256,256]{1,0:T(8,128)} %c_hbm.1) | copy-start | bytes 786436
  0.7 6.1 %copy-start.5 = (f32[256,256]{1,0:T(8,128)S(1)}, f32[256,256]{1,0:T(8,128)}, u32[]{:S(2)}) copy-start(f32[256,256]{1,0:T(8,128)} %e_hbm.1) | copy-start | bytes 786436
  1.7 10.5 %collective-permute-start = (f32[16,256]{1,0:T(8,128)S(1)}, f32[16,256]{1,0:T(8,128)S(1)}, u32[]{:S(2)}, u32[]{:S(2)}) collective-permute-start(f32[16,256]{1,0:T(8,128)S(1)} %get-tuple-element.42), channel_id=1, source_target_pairs={{8,16},{16,8},{9,17},{17,9},{10,18},{18,10},{11,19},{19,11},{12,20... | collective-permute-start | bytes 49160 | tf_op jit(solution)/shard_map/ppermute | solution.py:445
  2.3 9.9 %copy-start.2 = (f32[256,256]{1,0:T(8,128)S(1)}, f32[256,256]{1,0:T(8,128)}, u32[]{:S(2)}) copy-start(f32[256,256]{1,0:T(8,128)} %left_ref.5) | copy-start | bytes 786436
  2.3 9.8 %copy-start.3 = (f32[256,256]{1,0:T(8,128)S(1)}, f32[256,256]{1,0:T(8,128)}, u32[]{:S(2)}) copy-start(f32[256,256]{1,0:T(8,128)} %right_ref.5) | copy-start | bytes 786436
  2.3 9.8 %copy-start.4 = (f32[128,256]{1,0:T(8,128)S(1)}, f32[128,256]{1,0:T(8,128)}, u32[]{:S(2)}) copy-start(f32[128,256]{1,0:T(8,128)} %cr_ref.5) | copy-start | bytes 393220
  2.4 9.8 %collective-permute-start.1 = (f32[16,256]{1,0:T(8,128)S(1)}, f32[16,256]{1,0:T(8,128)S(1)}, u32[]{:S(2)}, u32[]{:S(2)}) collective-permute-start(f32[16,256]{1,0:T(8,128)S(1)} %get-tuple-element.43), channel_id=1, source_target_pairs={{0,8},{16,24},{8,0},{24,16},{1,9},{17,25},{9,1},{25,17},{2,10},{18... | collective-permute-start | bytes 49160 | tf_op jit(solution)/shard_map/ppermute | solution.py:445
  7.2 6.4 %collective-permute-start.2 = (f32[16,256]{1,0:T(8,128)S(1)}, f32[16,256]{1,0:T(8,128)S(1)}, u32[]{:S(2)}, u32[]{:S(2)}) collective-permute-start(f32[16,256]{1,0:T(8,128)S(1)} %get-tuple-element.47), channel_id=1, source_target_pairs={{1,2},{3,4},{5,6},{2,1},{4,3},{6,5},{9,10},{11,12},{13,14},{10,9},... | collective-permute-start | bytes 49160 | tf_op jit(solution)/shard_map/ppermute | solution.py:445
  7.8 6.1 %collective-permute-start.3 = (f32[16,256]{1,0:T(8,128)S(1)}, f32[16,256]{1,0:T(8,128)S(1)}, u32[]{:S(2)}, u32[]{:S(2)}) collective-permute-start(f32[16,256]{1,0:T(8,128)S(1)} %get-tuple-element.48), channel_id=1, source_target_pairs={{0,1},{2,3},{4,5},{6,7},{1,0},{3,2},{5,4},{7,6},{8,9},{10,11},{12,... | collective-permute-start | bytes 49160 | tf_op jit(solution)/shard_map/ppermute | solution.py:445
  13.9 1.2 %copy-start.9 = (f32[16,256]{1,0:T(8,128)}, f32[16,256]{1,0:T(8,128)S(1)}, u32[]{:S(2)}) copy-start(f32[16,256]{1,0:T(8,128)S(1)} %collective-permute-done.3.col0) | copy-start | bytes 49156
  13.9 1.3 %copy-start.8 = (f32[256,128]{1,0:T(8,128)S(1)}, f32[256,128]{1,0:T(8,128)}, u32[]{:S(2)}) copy-start(f32[256,128]{1,0:T(8,128)} %r_ref.1) | copy-start | bytes 393220
  15.1 1.5 %collective-permute-start.4 = (f32[208,256]{1,0:T(8,128)S(1)}, f32[208,256]{1,0:T(8,128)S(1)}, u32[]{:S(2)}, u32[]{:S(2)}) collective-permute-start(f32[208,256]{1,0:T(8,128)S(1)} %get-tuple-element.52), channel_id=1, source_target_pairs={{0,8},{16,24},{8,0},{24,16},{1,9},{17,25},{9,1},{25,17},{2,10},{18... | collective-permute-start | bytes 638984 | tf_op jit(solution)/shard_map/ppermute | solution.py:445
  17.4 15.6 %all-to-all-start = ((f32[16,4,8,128]{3,2,1,0:T(8,128)}), f32[16,4,8,128]{3,2,1,0:T(8,128)S(1)}, u32[]{:S(2)}, u32[]{:S(2)}) async-start(f32[16,4,8,128]{3,2,1,0:T(8,128)} %get-tuple-element.64), calls=%async_computation | async-start | bytes 524288 | tf_op jit(solution)/shard_map/all_to_all | solution.py:517
  22.8 6.0 %collective-permute-start.5 = (f32[72,256]{1,0:T(8,128)S(1)}, f32[72,256]{1,0:T(8,128)S(1)}, u32[]{:S(2)}, u32[]{:S(2)}) collective-permute-start(f32[72,256]{1,0:T(8,128)S(1)} %get-tuple-element.54.after), channel_id=1, source_target_pairs={{0,16},{8,24},{16,0},{24,8},{1,17},{9,25},{17,1},{25,9},{2,18},{10... | collective-permute-start | bytes 221192 | tf_op jit(solution)/shard_map/ppermute | solution.py:524
  24.7 0.7 %copy-start.10 = (f32[16,256]{1,0:T(8,128)S(1)}, f32[16,256]{1,0:T(8,128)}, u32[]{:S(2)}) copy-start(f32[16,256]{1,0:T(8,128)} %copy-done.9) | copy-start | bytes 49156
  26.3 0.6 %copy-start.11 = (f32[8,256]{1,0:T(8,128)}, f32[8,256]{1,0:T(8,128)S(1)}, u32[]{:S(2)}) copy-start(f32[8,256]{1,0:T(8,128)S(1)} %get-tuple-element.56.both_row.rest_1_) | copy-start | bytes 24580
  26.9 0.6 %copy-start.13 = (f32[8,256]{1,0:T(8,128)}, f32[8,256]{1,0:T(8,128)S(1)}, u32[]{:S(2)}) copy-start(f32[8,256]{1,0:T(8,128)S(1)} %get-tuple-element.58.quarter_row) | copy-start | bytes 24580
  28.8 4.2 %copy-start.12 = (f32[8,256]{1,0:T(8,128)S(1)}, f32[8,256]{1,0:T(8,128)}, u32[]{:S(2)}) copy-start(f32[8,256]{1,0:T(8,128)} %copy-done.11) | copy-start | bytes 24580
  45.6 0.7 %copy-start.14 = (f32[8,256]{1,0:T(8,128)S(1)}, f32[8,256]{1,0:T(8,128)}, u32[]{:S(2)}) copy-start(f32[8,256]{1,0:T(8,128)} %copy-done.13) | copy-start | bytes 24580
  45.6 1.9 %collective-permute-start.6 = (f32[16,4,8,128]{3,2,1,0:T(8,128)S(1)}, f32[16,4,8,128]{3,2,1,0:T(8,128)S(1)}, u32[]{:S(2)}, u32[]{:S(2)}) collective-permute-start(f32[16,4,8,128]{3,2,1,0:T(8,128)S(1)} %all_to_all.10.mine), channel_id=1, source_target_pairs={{0,8},{16,24},{8,0},{24,16},{1,9},{17,25},{9,1},{25,17},{2,10},{18... | collective-permute-start | bytes 786440 | tf_op jit(solution)/shard_map/ppermute | solution.py:445
  45.6 1.9 %collective-permute-start.7 = (f32[64,256]{1,0:T(8,128)S(1)}, f32[64,256]{1,0:T(8,128)S(1)}, u32[]{:S(2)}, u32[]{:S(2)}) collective-permute-start(f32[64,256]{1,0:T(8,128)S(1)} %slice_add_fusion.rest_0_.thin_mine), channel_id=1, source_target_pairs={{0,8},{16,24},{8,0},{24,16},{1,9},{17,25},{9,1},{25,17},{2,10},{18... | collective-permute-start | bytes 196616 | tf_op jit(solution)/shard_map/ppermute | solution.py:445

commit v6 on v5

--- a/solution.py
+++ b/solution.py
@@ -68,8 +68,114 @@
     second_ref[...] = jnp.where(even, up, down)
 
 
-def col_kernel(
-    e_in, p_in, q_in, c_in, w_in, e_ref, p_ref, q_ref, a_ref, f_ref, first_ref, second_ref
+def col_kernel(e_ref, p_ref, q_ref, c_ref, w_ref, first_ref, second_ref):
+    rows, cols = e_ref.shape
+    lane = place((rows, LANES), LANES, 1)
+    left = lane < LANES // 2
+    off = jnp.minimum(lane, LANES - 1 - lane)
+
+    def edge(ref):
+        return jnp.where(left, ref[:, :LANES], ref[:, cols - LANES :])
+
+    def shift(block, count):
+        return jnp.where(left, pltpu.roll(block, count, 1), pltpu.roll(block, LANES - count, 1))
+
+    wet = edge(w_ref) > 0
+    slope = jnp.where(wet, 0.25 * edge(c_ref), 0.0)
+    mass, side = jnp.where(wet, edge(q_ref), 0.0), jnp.where(wet, edge(p_ref), 0.0)
+    first = jnp.where(off < 4, 2.0 * edge(e_ref), jnp.where(off < 6, shift(mass, 4), shift(slope, 6))).T
+    second = jnp.where(off < 4, mass, shift(side, 4)).T
+    to_left = join(first[:ROWS], second[:ROWS], 0)
+    to_right = join(first[LANES - ROWS :], second[LANES - ROWS :], 0)
+    even = parity("along") == 0
+    first_ref[...] = jnp.where(even, to_right, to_left)
+    second_ref[...] = jnp.where(even, to_left, to_right)
+
+
+def row_pick(even, first, second):
+    below, above = jnp.where(even, first, second), jnp.where(even, second, first)
+    at = place(below.shape, ROWS, 0)
+
+    def pick(count, shift):
+        low = pltpu.roll(below, ROWS - shift, 0) if shift else below
+        high = pltpu.roll(above, shift, 0) if shift else above
+        return jnp.where(at < count, low, jnp.where(at >= ROWS - count, high, 0.0))
+
+    return pick
+
+
+def turn_back(even, first, second):
+    right, left = jnp.where(even, first, second), jnp.where(even, second, first)
+    gap = jnp.zeros((LANES - 2 * ROWS, right.shape[1]), right.dtype)
+    return jnp.concatenate([right, gap, left], axis=0).T
+
+
+def lane_pick(both):
+    lane = place(both.shape, LANES, 1)
+
+    def pick(count, shift):
+        low = pltpu.roll(both, LANES - shift, 1) if shift else both
+        high = pltpu.roll(both, shift, 1) if shift else both
+        return jnp.where(lane < count, low, jnp.where(lane >= LANES - count, high, 0.0))
+
+    return pick
+
+
+def col_pick(even, first, second):
+    return lane_pick(turn_back(even, first, second))
+
+
+def split(a):
+    high = a.astype(jnp.bfloat16)
+    return high, (a - high.astype(jnp.float32)).astype(jnp.bfloat16)
+
+
+def dot_split(a, b):
+    (a_high, a_low), (b_high, b_low) = a, b
+
+    def product(x, y):
+        return jnp.dot(x, y, preferred_element_type=jnp.float32)
+
+    return product(a_high, b_high) + (product(a_high, b_low) + product(a_low, b_high))
+
+
+def dot(a, b):
+    return dot_split(split(a), split(b))
+
+
+def join(tile, halo, axis):
+    return jnp.concatenate([tile, halo], axis=axis)
+
+
+def windows(rows):
+    step = WINDOW if rows % WINDOW == 0 else ROWS
+    for start in range(0, rows, step):
+        yield start, step
+
+
+def with_ring(part, ring, start, step, rows):
+    parts = [part]
+    if start == 0:
+        parts.insert(0, ring)
+    if start + step == rows:
+        parts.append(ring)
+    return jnp.concatenate(parts, axis=0) if len(parts) > 1 else part
+
+
+def window(tile, ring, start, step):
+    rows = tile.shape[0]
+    part = tile[max(start - ROWS, 0) : min(start + step + ROWS, rows)]
+    return with_ring(part, ring, start, step, rows)
+
+
+def halo_of(pick):
+    e, mass, slope = pick(4, 0), pick(2, 4), pick(2, 6)
+    return e, (2.0 - friction_of(slope)) * mass, slope
+
+
+def inner_kernel(
+    e_in, p_in, q_in, c_in, w_in, row1, row0, cr_ref, left_ref, right_ref,
+    e_ref, p_ref, q_ref, a_ref, f_ref, s_ref, sum_p, sum_q, give_ref,
 ):
     rows, cols = e_ref.shape
     for start, step in windows(rows):
@@ -80,112 +186,6 @@
         q_ref[here, :] = jnp.where(wet, q_in[here, :], 0.0)
         a_ref[here, :] = jnp.where(wet, 0.25 * celerity_sq, 0.0)
         f_ref[here, :] = jnp.where(wet, 0.02 / celerity_sq, 0.0)
-    lane = place((rows, LANES), LANES, 1)
-    left = lane < LANES // 2
-    off = jnp.minimum(lane, LANES - 1 - lane)
-
-    def edge(ref):
-        return jnp.where(left, ref[:, :LANES], ref[:, cols - LANES :])
-
-    def shift(block, count):
-        return jnp.where(left, pltpu.roll(block, count, 1), pltpu.roll(block, LANES - count, 1))
-
-    slope, mass, side = edge(a_ref), edge(q_ref), edge(p_ref)
-    first = jnp.where(off < 4, edge(e_ref), jnp.where(off < 6, shift(mass, 4), shift(slope, 6))).T
-    second = jnp.where(off < 4, mass, shift(side, 4)).T
-    to_left = join(first[:ROWS], second[:ROWS], 0)
-    to_right = join(first[LANES - ROWS :], second[LANES - ROWS :], 0)
-    even = parity("along") == 0
-    first_ref[...] = jnp.where(even, to_right, to_left)
-    second_ref[...] = jnp.where(even, to_left, to_right)
-
-
-def row_pick(even, first, second):
-    below, above = jnp.where(even, first, second), jnp.where(even, second, first)
-    at = place(below.shape, ROWS, 0)
-
-    def pick(count, shift):
-        low = pltpu.roll(below, ROWS - shift, 0) if shift else below
-        high = pltpu.roll(above, shift, 0) if shift else above
-        return jnp.where(at < count, low, jnp.where(at >= ROWS - count, high, 0.0))
-
-    return pick
-
-
-def turn_back(even, first, second):
-    right, left = jnp.where(even, first, second), jnp.where(even, second, first)
-    gap = jnp.zeros((LANES - 2 * ROWS, right.shape[1]), right.dtype)
-    return jnp.concatenate([right, gap, left], axis=0).T
-
-
-def lane_pick(both):
-    lane = place(both.shape, LANES, 1)
-
-    def pick(count, shift):
-        low = pltpu.roll(both, LANES - shift, 1) if shift else both
-        high = pltpu.roll(both, shift, 1) if shift else both
-        return jnp.where(lane < count, low, jnp.where(lane >= LANES - count, high, 0.0))
-
-    return pick
-
-
-def col_pick(even, first, second):
-    return lane_pick(turn_back(even, first, second))
-
-
-def split(a):
-    high = a.astype(jnp.bfloat16)
-    return high, (a - high.astype(jnp.float32)).astype(jnp.bfloat16)
-
-
-def dot_split(a, b):
-    (a_high, a_low), (b_high, b_low) = a, b
-
-    def product(x, y):
-        return jnp.dot(x, y, preferred_element_type=jnp.float32)
-
-    return product(a_high, b_high) + (product(a_high, b_low) + product(a_low, b_high))
-
-
-def dot(a, b):
-    return dot_split(split(a), split(b))
-
-
-def join(tile, halo, axis):
-    return jnp.concatenate([tile, halo], axis=axis)
-
-
-def windows(rows):
-    step = WINDOW if rows % WINDOW == 0 else ROWS
-    for start in range(0, rows, step):
-        yield start, step
-
-
-def with_ring(part, ring, start, step, rows):
-    parts = [part]
-    if start == 0:
-        parts.insert(0, ring)
-    if start + step == rows:
-        parts.append(ring)
-    return jnp.concatenate(parts, axis=0) if len(parts) > 1 else part
-
-
-def window(tile, ring, start, step):
-    rows = tile.shape[0]
-    part = tile[max(start - ROWS, 0) : min(start + step + ROWS, rows)]
-    return with_ring(part, ring, start, step, rows)
-
-
-def halo_of(pick):
-    e, mass, slope = pick(4, 0), pick(2, 4), pick(2, 6)
-    return e, (2.0 - friction_of(slope)) * mass, slope
-
-
-def inner_kernel(
-    e_ref, p_ref, q_ref, a_ref, f_ref, row1, row0, cr_ref, left_ref, right_ref,
-    s_ref, sum_p, sum_q, give_ref,
-):
-    rows, cols = e_ref.shape
     e_row, g_row, a_row = halo_of(row_pick(parity("cross") == 0, row0[:ROWS], row1[:ROWS]))
     for start, step in windows(rows):
         inner = slice(start, start + step)
@@ -342,28 +342,41 @@
                 out[c * alongs + a, t] = value
 
 
-def unpack_kernel(mine, theirs, thin_mine, thin_theirs, *refs):
-    outs, held, sems = refs[:3], refs[3:6], refs[6]
-    core, ranged, coranged = held
-    count = mine.shape[0]
+def unpack_kernel(mine, core_hbm, range_hbm, core, ranged, sems):
+    wide = unpack_core(mine, core)
+    copies = start(pieces(core, rows_of(core_hbm, parity("cross")), sems.at[0]))
+    places = tile_slices(ranged.shape)
+    per = len(places) // mine.shape[0]
+    for k, where in enumerate(places):
+        ranged[where] = mine[k // per, wide + k % per]
+    copies += start(pieces(ranged, range_hbm, sems.at[1]))
+    for copy in copies:
+        copy.wait()
+
+
+def unpack_core(handed, core):
+    places = tile_slices(core.shape)
+    wide = len(places) // handed.shape[0]
+    for k, where in enumerate(places):
+        core[where] = handed[k // wide, k % wide]
+    return wide
+
+
+def rows_of(ref, side):
+    count = ref.shape[0] // 2
+    return ref.at[pl.ds(pl.multiple_of(side * count, count), count), :]
+
+
+def complete_kernel(theirs, core_in, thin_mine, thin_theirs, core_hbm, corange_hbm,
+                    core, coranged, sems):
+    del core_in
+    unpack_core(theirs, core)
+    copies = start(pieces(core, rows_of(core_hbm, 1 - parity("cross")), sems.at[0]))
+    thin = thin_mine.shape[0]
     even = parity("cross") == 0
-    thin = thin_mine.shape[0]
     coranged[:thin] = jnp.where(even, thin_mine[...], thin_theirs[...])
     coranged[thin:] = jnp.where(even, thin_theirs[...], thin_mine[...])
-    copies = start(pieces(coranged, outs[2], sems.at[2]))
-    places = tile_slices(ranged.shape)
-    wide = len(tile_slices(core.shape)) // 2 // count
-    per = len(places) // count
-    for k, where in enumerate(places):
-        ranged[where] = mine[k // per, wide + k % per]
-    copies += start(pieces(ranged, outs[1], sems.at[1]))
-    places = tile_slices(core.shape)
-    keep = len(places) // 2
-    for k in range(keep):
-        tile, other = mine[k // wide, k % wide], theirs[k // wide, k % wide]
-        core[places[k]] = jnp.where(even, tile, other)
-        core[places[keep + k]] = jnp.where(even, other, tile)
-    copies += start(pieces(core, outs[0], sems.at[0]))
+    copies += start(pieces(coranged, corange_hbm, sems.at[1]))
     for copy in copies:
         copy.wait()
 
@@ -405,9 +418,10 @@
 
 def flux_kernel(
     both_ref, both_row, both_col, quarter_row, quarter_col, a_ref, f_ref, got_ref, corner_ref,
-    p_ref, q_ref, sum_p, sum_q, p_hbm, q_hbm, next_p, next_q, sems,
+    p_ref, q_ref, sum_p, sum_q, p_hbm, q_hbm, token, next_p, next_q, sems,
 ):
     rows, cols = both_ref.shape
+    token[...] = jnp.zeros(token.shape, token.dtype)
     copies = []
     row = lax.axis_index("cross")
     inside = (row > 0) & (row < lax.axis_size("cross") - 1)
@@ -450,8 +464,11 @@
     rows, cols = e.shape
     cells = rows * cols
 
-    def run(kernel, outs, flops, *args, idle=(), scratch=(), to=None, space=pltpu.VMEM, limit=32 << 20):
+    def run(kernel, outs, flops, *args, idle=(), scratch=(), to=None, space=pltpu.VMEM, limit=32 << 20,
+            alias=None):
         kinds = [pl.BlockSpec(memory_space=space)] * len(args)
+        for i in alias or {}:
+            kinds[i] = pl.BlockSpec(memory_space=pltpu.HBM)
         kinds += [pl.BlockSpec(memory_space=pl.ANY)] * len(idle)
         moved = sum(a.size * 4 for a in args) + sum(o.size * 4 for o in outs)
         to = to or [pltpu.VMEM] * len(outs)
@@ -461,6 +478,7 @@
             in_specs=kinds,
             out_specs=[pl.BlockSpec(memory_space=kind) for kind in to],
             scratch_shapes=list(scratch),
+            input_output_aliases=alias or {},
             cost_estimate=pl.CostEstimate(flops=flops, bytes_accessed=moved, transcendentals=0),
             compiler_params=pltpu.CompilerParams(vmem_limit_bytes=limit),
         )(*args, *idle)
@@ -472,21 +490,18 @@
     )
     row1, row0 = swap(row1, "cross", 1), swap(row0, "cross", 0)
     tile = f32(rows, cols)
-    *fields, col0, col1 = run(
-        col_kernel, [tile] * 5 + [f32(2 * ROWS, rows)] * 2, 10 * cells, e, p, q, c, w
-    )
+    col0, col1 = run(col_kernel, [f32(2 * ROWS, rows)] * 2, 10 * cells, e, p, q, c, w)
     col1, col0 = swap(col1, "along", 1), swap(col0, "along", 0)
     halo = (row1, row0, col1, col0)
     range_shape = f32(rows, range_test.shape[1])
     corange_shape = f32(corange_test.shape[0], cols)
     core_shape = f32(core_left.shape[0], core_right.shape[1])
     half, thin = core_shape.shape[0] // 2, corange_shape.shape[0] // 2
-    e2, mass_x, mass_y, slope, friction = fields
     row1, row0, col1, col0 = halo
     tests = (corange_test, core_left, core_right)
-    s_part, sum_p, sum_q, give = run(
-        inner_kernel, [tile] * 3 + [f32(half + thin, cols)], 600 * cells,
-        *fields, row1, row0, *tests,
+    e2, mass_x, mass_y, slope, friction, s_part, sum_p, sum_q, give = run(
+        inner_kernel, [tile] * 8 + [f32(half + thin, cols)], 600 * cells,
+        e, p, q, c, w, row1, row0, *tests,
     )
     outs = [tile] * 2 + [f32(half + thin + 2 * ROWS, cols)]
     s_held, sum_q, give = run(
@@ -503,6 +518,15 @@
         to=[pltpu.HBM, pltpu.VMEM, pltpu.VMEM], scratch=[pltpu.SemaphoreType.DMA((4,))],
     )
     rim_shapes = [tile] + [f32(ROWS, cols), f32(rows, LANES)] * 2
+    def fluxes(rims, corner):
+        return run(
+            flux_kernel, [tile] * 2 + [f32(ROWS, LANES)], 40 * cells,
+            *rims, slope, friction, got, corner, p, q, sum_p, sum_q,
+            to=[pltpu.HBM] * 2 + [pltpu.VMEM],
+            scratch=[pltpu.VMEM((rows, cols), jnp.float32)] * 2
+            + [pltpu.SemaphoreType.DMA((2, len(list(windows(rows)))))],
+        )
+
     shared = crosses == 4 and not any(size % (count * ROWS * LANES) for size in sizes)
     if shared:
         per = [size // (count * ROWS * LANES) for size in sizes]
@@ -524,32 +548,31 @@
         corner = lax.ppermute(across, "cross", [(i, i ^ 2) for i in range(crosses)])
         thin_mine = across[:thin] + corner[:thin]
         thin_theirs = swap(thin_mine, "cross", 0)
+        p_next, q_next, token = fluxes(rims, corner)
         (totals,) = run(
             functools.partial(sum_kernel, crosses // 2, alongs, cuts), [sheet], sheet.size,
-            spread(shares), idle=[thin_mine, rims[1]],
+            spread(shares), idle=[thin_mine, token],
         )
         mine = spread(totals)
         theirs = swap(mine, "cross", 0)
-        shapes = [core_shape, range_shape, corange_shape]
-        core, ranged, coranged = run(
-            unpack_kernel, shapes, sheet.size, mine, theirs, thin_mine, thin_theirs,
-            to=[pltpu.HBM] * 3,
-            scratch=[pltpu.VMEM(x.shape, x.dtype) for x in shapes]
-            + [pltpu.SemaphoreType.DMA((3, 4))],
+        held = [f32(half, core_shape.shape[1]), range_shape, corange_shape]
+        held = [pltpu.VMEM(x.shape, x.dtype) for x in held]
+        core, ranged = run(
+            unpack_kernel, [core_shape, range_shape], sheet.size, mine,
+            to=[pltpu.HBM] * 2, scratch=held[:2] + [pltpu.SemaphoreType.DMA((2, 4))],
+        )
+        core, coranged = run(
+            complete_kernel, [core_shape, corange_shape], sheet.size,
+            theirs, core, thin_mine, thin_theirs, to=[pltpu.HBM] * 2, alias={1: 0},
+            scratch=[held[0], held[2], pltpu.SemaphoreType.DMA((2, 4))],
         )
     else:
         corner = swap(give[-ROWS:], "cross", 1)
         rims = run(both_kernel, rim_shapes, 60 * cells, e2, mass_x, mass_y, slope, *halo, give)
+        p_next, q_next, _ = fluxes(rims, corner)
         ranged = lax.psum(ranged, "along")
         coranged = lax.psum(dot(corange_test, s_held), "cross")
         core = lax.psum(dot(core_left, dot(s_held, core_right)), AXES)
-    p_next, q_next = run(
-        flux_kernel, [tile] * 2, 40 * cells,
-        *rims, slope, friction, got, corner, p, q, sum_p, sum_q,
-        to=[pltpu.HBM] * 2,
-        scratch=[pltpu.VMEM((rows, cols), jnp.float32)] * 2
-        + [pltpu.SemaphoreType.DMA((2, len(list(windows(rows)))))],
-    )
     return s_next, p_next, q_next, ranged, coranged, core
 
 

time: 49 us -> 48.3 us (0.986)
  local copies, waits for them, and re-layouts: 2.14 us -> 0.04 us
  waiting for transfers between devices: 6.22 us -> 7.13 us
  Pallas kernels: 8.71 us -> 9.42 us
    unnamed x30 -> x18, local copies, waits for them, and re-layouts: 2.14 us -> 0.04 us
    ppermute x1, waiting for transfers between devices: 1.33 us -> 3.23 us  [body(): corner = lax.ppermute(across, 'cross', [(i, i ^ 2) for i in range(crosses)])]
    all_to_all x1, waiting for transfers between devices: 4.22 us -> 2.95 us  [spread(): return lax.all_to_all(x, AXES, 0, 0, tiled=True, axis_index_groups=groups)]
    pallas_call x10 -> x11, Pallas kernels: 8.71 us -> 9.42 us  [run(): pl.pallas_call(kernel, out_shape=outs, in_specs=kinds, out_specs=[pl.Bloc...]
  transfers between devices with their start and end apart: 9 -> 9, of which waited for: 4 -> 5; matrix products, arithmetic and copies ran while one was open for 0% -> 0% of each run, Pallas kernels for 10% -> 12%
where the time goes in v6:
time: 48.3 us; the launch traced here: 47.9 us
  starting transfers between devices  18 us (37%)
  blocking collectives  12.5 us (26%)
  Pallas kernels  9.42 us (20%)
  waiting for transfers between devices  7.13 us (15%)
  between operations  0.85 us (2%)
    all_to_all x1, blocking collectives, spread(): return lax.all_to_all(x, AXES, 0, 0, tiled=True, axis_index_groups=groups)  12.5 us
    ppermute x7, starting transfers between devices, swap(): lax.ppermute(message, axis, pairs)  10.6 us
    pallas_call x11, Pallas kernels, run(): pl.pallas_call(kernel, out_shape=outs, in_specs=kinds, out_specs=[pl.Bloc...  9.42 us
    all_to_all x1, starting transfers between devices, spread(): return lax.all_to_all(x, AXES, 0, 0, tiled=True, axis_index_groups=groups)  5.42 us
    ppermute x1, waiting for transfers between devices, body(): corner = lax.ppermute(across, 'cross', [(i, i ^ 2) for i in range(crosses)])  3.23 us
    all_to_all x1, waiting for transfers between devices, spread(): return lax.all_to_all(x, AXES, 0, 0, tiled=True, axis_index_groups=groups)  2.95 us
    ppermute x1, starting transfers between devices, body(): corner = lax.ppermute(across, 'cross', [(i, i ^ 2) for i in range(crosses)])  1.93 us
  transfers between devices with their start and end apart: 9, of which 5 were waited for; matrix products, arithmetic and copies ran while one was open for 0% of the time, Pallas kernels for 12%

profile of v6, /device:TPU:0, one launch (start us, length us, event | category | flops | bytes accessed | tf_op | source)
XLA Modules:
  0.0 47.9 jit_solution(17546195172265082910)
XLA Ops:
  0.7 1.0 %shard_map.136 = (f32[16,256]{1,0:T(8,128)S(1)}, f32[16,256]{1,0:T(8,128)S(1)}) custom-call(f32[256,256]{1,0:T(8,128)} %e_ref.1, f32[256,256]{1,0:T(8,128)} %p_ref.3, f32[256,256]{1,0:T(8,128)} %q_ref.3, f32[256,256]{1,0:T(8,128)} %c_ref.1, s32[256,256]{1,0:T(8,128)} %w_ref.1), custom_call_target="tpu_custom_call" | custom-call | flops 65536 | bytes 1343488 | tf_op jit(solution)/shard_map/pallas_call | solution.py:475
  1.7 0.7 %collective-permute-start = (f32[16,256]{1,0:T(8,128)S(1)}, f32[16,256]{1,0:T(8,128)S(1)}, u32[]{:S(2)}, u32[]{:S(2)}) collective-permute-start(f32[16,256]{1,0:T(8,128)S(1)} %get-tuple-element.39), channel_id=1, source_target_pairs={{8,16},{16,8},{9,17},{17,9},{10,18},{18,10},{11,19},{19,11},{12,20... | collective-permute-start | bytes 49160 | tf_op jit(solution)/shard_map/ppermute | solution.py:459
  2.3 0.0 copy-start.5
  2.3 0.0 copy-start.6
  2.3 0.0 copy-start.7
  2.4 4.4 %collective-permute-start.1 = (f32[16,256]{1,0:T(8,128)S(1)}, f32[16,256]{1,0:T(8,128)S(1)}, u32[]{:S(2)}, u32[]{:S(2)}) collective-permute-start(f32[16,256]{1,0:T(8,128)S(1)} %get-tuple-element.40), channel_id=1, source_target_pairs={{0,8},{16,24},{8,0},{24,16},{1,9},{17,25},{9,1},{25,17},{2,10},{18... | collective-permute-start | bytes 49160 | tf_op jit(solution)/shard_map/ppermute | solution.py:459
  6.8 0.4 shard_map.138
  7.1 0.7 %collective-permute-start.2 = (f32[16,256]{1,0:T(8,128)S(1)}, f32[16,256]{1,0:T(8,128)S(1)}, u32[]{:S(2)}, u32[]{:S(2)}) collective-permute-start(f32[16,256]{1,0:T(8,128)S(1)} %get-tuple-element.48), channel_id=1, source_target_pairs={{1,2},{3,4},{5,6},{2,1},{4,3},{6,5},{9,10},{11,12},{13,14},{10,9},... | collective-permute-start | bytes 49160 | tf_op jit(solution)/shard_map/ppermute | solution.py:459
  7.8 4.4 %collective-permute-start.3 = (f32[16,256]{1,0:T(8,128)S(1)}, f32[16,256]{1,0:T(8,128)S(1)}, u32[]{:S(2)}, u32[]{:S(2)}) collective-permute-start(f32[16,256]{1,0:T(8,128)S(1)} %get-tuple-element.49), channel_id=1, source_target_pairs={{0,1},{2,3},{4,5},{6,7},{1,0},{3,2},{5,4},{7,6},{8,9},{10,11},{12,... | collective-permute-start | bytes 49160 | tf_op jit(solution)/shard_map/ppermute | solution.py:459
  12.1 0.0 collective-permute-done.row1
  12.2 0.0 collective-permute-done.1.row0
  12.2 1.4 %shard_map.137 = (f32[256,256]{1,0:T(8,128)S(1)}, f32[256,256]{1,0:T(8,128)S(1)}, f32[256,256]{1,0:T(8,128)S(1)}, f32[256,256]{1,0:T(8,128)S(1)}, f32[256,256]{1...) custom-call(f32[256,256]{1,0:T(8,128)S(1)} %copy-done.2, ...), custom_call_target="tpu_custom_call" | custom-call | flops 39321600 | bytes 4292608 | tf_op jit(solution)/shard_map/pallas_call | solution.py:475
  13.6 0.0 collective-permute-done.2.col1
  13.6 0.3 collective-permute-done.3.col0
  13.9 1.2 %shard_map.139 = (f32[256,256]{1,0:T(8,128)S(1)}, f32[256,256]{1,0:T(8,128)S(1)}, f32[208,256]{1,0:T(8,128)S(1)}) custom-call(f32[256,256]{1,0:T(8,128)S(1)} %get-tuple-element.41.e_ref, f32[256,256]{1,0:T(8,128)S(1)} %get-tuple-element.42.q_ref.mq_ref, f32[256,256]{1,0:T(8,128)S(1)} %get-tuple-element.43.a_ref, f32[256,256]{1,0:T(8,128)S(1)} %get-tuple-element.44.f_ref, ...), custom_call_target="tpu_custom_call" | custom-call | flops 13107200 | bytes 3194880 | tf_op jit(solution)/shard_map/pallas_call | solution.py:475
  15.1 0.1 collective-permute-start.4
  15.2 1.1 %shard_map.140 = (f32[256,256]{1,0:T(8,128)}, f32[192,256]{1,0:T(8,128)S(1)}, f32[256,128]{1,0:T(8,128)S(1)}) custom-call(f32[256,256]{1,0:T(8,128)S(1)} %get-tuple-element.50.s_ref, f32[256,128]{1,0:T(8,128)S(1)} %copy-done.8, f32[128,256]{1,0:T(8,128)S(1)} %copy-done.7, f32[256,256]{1,0:T(8,128)S(1)} %copy-done.5, f32[256,256]{1,0:T(8,128)S(1)} %copy-done.6), custom_call_target="tpu_custom_call" | custom-call | flops 19660800 | bytes 1638400 | tf_op jit(solution)/shard_map/pallas_call | solution.py:475
  16.3 0.3 collective-permute-done.4.got_ref
  16.6 0.7 %shard_map.141 = (f32[16,4,8,128]{3,2,1,0:T(8,128)}, f32[72,256]{1,0:T(8,128)S(1)}) custom-call(f32[192,256]{1,0:T(8,128)S(1)} %get-tuple-element.53.keep_ref, f32[208,256]{1,0:T(8,128)S(1)} %collective-permute-done.4.got_ref, f32[256,128]{1,0:T(8,128)S(1)} %get-tuple-element.55.range_ref), custom_call_target="tpu_custom_call" | custom-call | flops 65536 | bytes 876544 | tf_op jit(solution)/shard_map/pallas_call | solution.py:475
  17.3 5.4 %all-to-all-start = ((f32[16,4,8,128]{3,2,1,0:T(8,128)}), f32[16,4,8,128]{3,2,1,0:T(8,128)S(1)}, u32[]{:S(2)}, u32[]{:S(2)}) async-start(f32[16,4,8,128]{3,2,1,0:T(8,128)} %get-tuple-element.66), calls=%async_computation | async-start | bytes 524288 | tf_op jit(solution)/shard_map/all_to_all | solution.py:541
  22.8 1.9 %collective-permute-start.5 = (f32[72,256]{1,0:T(8,128)S(1)}, f32[72,256]{1,0:T(8,128)S(1)}, u32[]{:S(2)}, u32[]{:S(2)}) collective-permute-start(f32[72,256]{1,0:T(8,128)S(1)} %get-tuple-element.56.after), channel_id=1, source_target_pairs={{0,16},{8,24},{16,0},{24,8},{1,17},{9,25},{17,1},{25,9},{2,18},{10... | collective-permute-start | bytes 221192 | tf_op jit(solution)/shard_map/ppermute | solution.py:548
  24.7 0.8 %shard_map.142 = (f32[256,256]{1,0:T(8,128)S(1)}, f32[8,256]{1,0:T(8,128)S(1)}, f32[256,128]{1,0:T(8,128)S(1)}, f32[8,256]{1,0:T(8,128)S(1)}, f32[256,128]{1,0:T(8,128)S(1)}) custom-call(f32[256,256]{1,0:T(8,128)S(1)} %get-tuple-element.41.e_ref, f32[256,256]{1,0:T(8,128)S(1)} %get-tuple-element.52.mp_ref, f32[256,256]{1,0:T(8,128)S(1)} %get-tuple-element.42.q_ref.mq_ref, ...), custom_call_target="tpu_custom_call" | custom-call | flops 3932160 | bytes 1728512 | tf_op jit(solution)/shard_map/pallas_call | solution.py:475
  25.5 3.2 %collective-permute-done.5.corner_ref = f32[72,256]{1,0:T(8,128)S(1)} collective-permute-done((f32[72,256]{1,0:T(8,128)S(1)}, f32[72,256]{1,0:T(8,128)S(1)}, u32[]{:S(2)}, u32[]{:S(2)}) %collective-permute-start.5) | collective-permute-done | bytes 73760 | tf_op jit(solution)/shard_map/ppermute | solution.py:548
  28.7 1.3 %shard_map.143 = (f32[256,256]{1,0:T(8,128)}, f32[256,256]{1,0:T(8,128)}, f32[8,128]{1,0:T(8,128)S(1)}) custom-call(f32[256,256]{1,0:T(8,128)S(1)} %get-tuple-element.57.both_ref, f32[8,256]{1,0:T(8,128)S(1)} %get-tuple-element.58.both_row, f32[256,128]{1,0:T(8,128)S(1)} %get-tuple-element.59.both_col, f32[8,256]{1,0:T(8,128)S(1)} %get-tuple-element.60.quarter_row, ...), custom_call_target="tpu_custom_call" | custom-call | flops 2621440 | bytes 2928640 | tf_op jit(solution)/shard_map/pallas_call | solution.py:475
  30.0 2.9 %all-to-all-done.got = f32[16,4,8,128]{3,2,1,0:T(8,128)S(1)} async-done(((f32[16,4,8,128]{3,2,1,0:T(8,128)}), f32[16,4,8,128]{3,2,1,0:T(8,128)S(1)}, u32[]{:S(2)}, u32[]{:S(2)}) %all-to-all-start) | async-done | bytes 262176 | tf_op jit(solution)/shard_map/all_to_all | solution.py:541
  33.0 12.5 %all_to_all.10.mine = f32[16,4,8,128]{3,2,1,0:T(8,128)S(1)} all-to-all(f32[16,4,8,128]{3,2,1,0:T(8,128)S(1)} %shard_map.144), channel_id=1, replica_groups={{0,1,2,3,4,5,6,7,16,17,18,19,20,21,22,23},{8,9,10,11,12,13,14,15,24,25,..., dimensions={0} | all-to-all | bytes 524288 | tf_op jit(solution)/shard_map/all_to_all | solution.py:541
  45.5 0.0 collective-permute-start.6
  45.5 0.5 %collective-permute-start.7 = (f32[64,256]{1,0:T(8,128)S(1)}, f32[64,256]{1,0:T(8,128)S(1)}, u32[]{:S(2)}, u32[]{:S(2)}) collective-permute-start(f32[64,256]{1,0:T(8,128)S(1)} %slice_add_fusion.rest_0_.thin_mine), channel_id=1, source_target_pairs={{0,8},{16,24},{8,0},{24,16},{1,9},{17,25},{9,1},{25,17},{2,10},{18... | collective-permute-start | bytes 196616 | tf_op jit(solution)/shard_map/ppermute | solution.py:459
  46.0 0.8 %shard_map.145 = (f32[256,256]{1,0:T(8,128)}, f32[256,128]{1,0:T(8,128)}) custom-call(f32[16,4,8,128]{3,2,1,0:T(8,128)S(1)} %all_to_all.10.mine), custom_call_target="tpu_custom_call" | custom-call | flops 65536 | bytes 655360 | tf_op jit(solution)/shard_map/pallas_call | solution.py:475
  46.8 0.3 collective-permute-done.7.thin_theirs
  47.1 0.0 collective-permute-done.6.theirs
  47.1 0.8 %shard_map.146 = (f32[256,256]{1,0:T(8,128)}, f32[128,256]{1,0:T(8,128)}) custom-call(f32[16,4,8,128]{3,2,1,0:T(8,128)S(1)} %collective-permute-done.6.theirs, f32[256,256]{1,0:T(8,128)} %get-tuple-element.69.core_in, f32[64,256]{1,0:T(8,128)S(1)} %slice_add_fusion.rest_0_.thin_mine, ...), custom_call_target="tpu_custom_call", output_to_operand_aliasing={{0}: (1, {})} | custom-call | flops 65536 | bytes 1048576 | tf_op jit(solution)/shard_map/pallas_call | solution.py:475
  (17 shorter events, 0.1 us)
Async XLA Ops:
  0.6 6.1 %copy-start.1 = (f32[256,256]{1,0:T(8,128)S(1)}, f32[256,256]{1,0:T(8,128)}, u32[]{:S(2)}) copy-start(f32[256,256]{1,0:T(8,128)} %q_ref.3) | copy-start | bytes 786436
  0.6 6.1 %copy-start = (f32[256,256]{1,0:T(8,128)S(1)}, f32[256,256]{1,0:T(8,128)}, u32[]{:S(2)}) copy-start(f32[256,256]{1,0:T(8,128)} %p_ref.3) | copy-start | bytes 786436
  0.7 6.1 %copy-start.4 = (s32[256,256]{1,0:T(8,128)S(1)}, s32[256,256]{1,0:T(8,128)}, u32[]{:S(2)}) copy-start(s32[256,256]{1,0:T(8,128)} %w_ref.1) | copy-start | bytes 786436
  0.7 6.1 %copy-start.3 = (f32[256,256]{1,0:T(8,128)S(1)}, f32[256,256]{1,0:T(8,128)}, u32[]{:S(2)}) copy-start(f32[256,256]{1,0:T(8,128)} %c_ref.1) | copy-start | bytes 786436
  0.7 6.1 %copy-start.2 = (f32[256,256]{1,0:T(8,128)S(1)}, f32[256,256]{1,0:T(8,128)}, u32[]{:S(2)}) copy-start(f32[256,256]{1,0:T(8,128)} %e_ref.1) | copy-start | bytes 786436
  1.7 10.5 %collective-permute-start = (f32[16,256]{1,0:T(8,128)S(1)}, f32[16,256]{1,0:T(8,128)S(1)}, u32[]{:S(2)}, u32[]{:S(2)}) collective-permute-start(f32[16,256]{1,0:T(8,128)S(1)} %get-tuple-element.39), channel_id=1, source_target_pairs={{8,16},{16,8},{9,17},{17,9},{10,18},{18,10},{11,19},{19,11},{12,20... | collective-permute-start | bytes 49160 | tf_op jit(solution)/shard_map/ppermute | solution.py:459
  2.3 9.8 %copy-start.5 = (f32[256,256]{1,0:T(8,128)S(1)}, f32[256,256]{1,0:T(8,128)}, u32[]{:S(2)}) copy-start(f32[256,256]{1,0:T(8,128)} %left_ref.5) | copy-start | bytes 786436
  2.3 9.8 %copy-start.6 = (f32[256,256]{1,0:T(8,128)S(1)}, f32[256,256]{1,0:T(8,128)}, u32[]{:S(2)}) copy-start(f32[256,256]{1,0:T(8,128)} %right_ref.5) | copy-start | bytes 786436
  2.3 9.8 %copy-start.7 = (f32[128,256]{1,0:T(8,128)S(1)}, f32[128,256]{1,0:T(8,128)}, u32[]{:S(2)}) copy-start(f32[128,256]{1,0:T(8,128)} %cr_ref.5) | copy-start | bytes 393220
  2.4 9.8 %collective-permute-start.1 = (f32[16,256]{1,0:T(8,128)S(1)}, f32[16,256]{1,0:T(8,128)S(1)}, u32[]{:S(2)}, u32[]{:S(2)}) collective-permute-start(f32[16,256]{1,0:T(8,128)S(1)} %get-tuple-element.40), channel_id=1, source_target_pairs={{0,8},{16,24},{8,0},{24,16},{1,9},{17,25},{9,1},{25,17},{2,10},{18... | collective-permute-start | bytes 49160 | tf_op jit(solution)/shard_map/ppermute | solution.py:459
  7.1 6.5 %collective-permute-start.2 = (f32[16,256]{1,0:T(8,128)S(1)}, f32[16,256]{1,0:T(8,128)S(1)}, u32[]{:S(2)}, u32[]{:S(2)}) collective-permute-start(f32[16,256]{1,0:T(8,128)S(1)} %get-tuple-element.48), channel_id=1, source_target_pairs={{1,2},{3,4},{5,6},{2,1},{4,3},{6,5},{9,10},{11,12},{13,14},{10,9},... | collective-permute-start | bytes 49160 | tf_op jit(solution)/shard_map/ppermute | solution.py:459
  7.8 6.1 %collective-permute-start.3 = (f32[16,256]{1,0:T(8,128)S(1)}, f32[16,256]{1,0:T(8,128)S(1)}, u32[]{:S(2)}, u32[]{:S(2)}) collective-permute-start(f32[16,256]{1,0:T(8,128)S(1)} %get-tuple-element.49), channel_id=1, source_target_pairs={{0,1},{2,3},{4,5},{6,7},{1,0},{3,2},{5,4},{7,6},{8,9},{10,11},{12,... | collective-permute-start | bytes 49160 | tf_op jit(solution)/shard_map/ppermute | solution.py:459
  13.9 1.3 %copy-start.8 = (f32[256,128]{1,0:T(8,128)S(1)}, f32[256,128]{1,0:T(8,128)}, u32[]{:S(2)}) copy-start(f32[256,128]{1,0:T(8,128)} %r_ref.1) | copy-start | bytes 393220
  15.1 1.5 %collective-permute-start.4 = (f32[208,256]{1,0:T(8,128)S(1)}, f32[208,256]{1,0:T(8,128)S(1)}, u32[]{:S(2)}, u32[]{:S(2)}) collective-permute-start(f32[208,256]{1,0:T(8,128)S(1)} %get-tuple-element.54), channel_id=1, source_target_pairs={{0,8},{16,24},{8,0},{24,16},{1,9},{17,25},{9,1},{25,17},{2,10},{18... | collective-permute-start | bytes 638984 | tf_op jit(solution)/shard_map/ppermute | solution.py:459
  17.3 15.6 %all-to-all-start = ((f32[16,4,8,128]{3,2,1,0:T(8,128)}), f32[16,4,8,128]{3,2,1,0:T(8,128)S(1)}, u32[]{:S(2)}, u32[]{:S(2)}) async-start(f32[16,4,8,128]{3,2,1,0:T(8,128)} %get-tuple-element.66), calls=%async_computation | async-start | bytes 524288 | tf_op jit(solution)/shard_map/all_to_all | solution.py:541
  22.8 6.0 %collective-permute-start.5 = (f32[72,256]{1,0:T(8,128)S(1)}, f32[72,256]{1,0:T(8,128)S(1)}, u32[]{:S(2)}, u32[]{:S(2)}) collective-permute-start(f32[72,256]{1,0:T(8,128)S(1)} %get-tuple-element.56.after), channel_id=1, source_target_pairs={{0,16},{8,24},{16,0},{24,8},{1,17},{9,25},{17,1},{25,9},{2,18},{10... | collective-permute-start | bytes 221192 | tf_op jit(solution)/shard_map/ppermute | solution.py:548
  45.5 1.6 %collective-permute-start.6 = (f32[16,4,8,128]{3,2,1,0:T(8,128)S(1)}, f32[16,4,8,128]{3,2,1,0:T(8,128)S(1)}, u32[]{:S(2)}, u32[]{:S(2)}) collective-permute-start(f32[16,4,8,128]{3,2,1,0:T(8,128)S(1)} %all_to_all.10.mine), channel_id=1, source_target_pairs={{0,8},{16,24},{8,0},{24,16},{1,9},{17,25},{9,1},{25,17},{2,10},{18... | collective-permute-start | bytes 786440 | tf_op jit(solution)/shard_map/ppermute | solution.py:459
  45.5 1.6 %collective-permute-start.7 = (f32[64,256]{1,0:T(8,128)S(1)}, f32[64,256]{1,0:T(8,128)S(1)}, u32[]{:S(2)}, u32[]{:S(2)}) collective-permute-start(f32[64,256]{1,0:T(8,128)S(1)} %slice_add_fusion.rest_0_.thin_mine), channel_id=1, source_target_pairs={{0,8},{16,24},{8,0},{24,16},{1,9},{17,25},{9,1},{25,17},{2,10},{18... | collective-permute-start | bytes 196616 | tf_op jit(solution)/shard_map/ppermute | solution.py:459

commit v7 on v6

--- a/solution.py
+++ b/solution.py
@@ -268,13 +268,10 @@
 
 
 def product_kernel(
-    s_ref, r_ref, cr_ref, left_ref, right_ref, s_hbm, keep_ref, range_ref, sems
+    s_ref, r_ref, cr_ref, left_ref, right_ref, keep_ref, range_ref
 ):
-    copies = start(pieces(s_ref, s_hbm, sems))
     keep_ref[...] = halves(parity("cross"), left_ref, right_ref, cr_ref, s_ref)
     range_ref[...] = dot(s_ref[...], r_ref[...])
-    for copy in copies:
-        copy.wait()
 
 
 def start(copies):
@@ -382,10 +379,13 @@
 
 
 def both_kernel(
-    e_ref, mp_ref, mq_ref, a_ref, row1, row0, col1, col0, after,
-    both_ref, both_row, both_col, quarter_row, quarter_col,
+    e_ref, mp_ref, mq_ref, a_ref, row1, row0, col1, col0, s_ref, after,
+    both_ref, both_row, both_col, quarter_row, quarter_col, s_hbm, sems,
 ):
     del after
+    copies = pieces(s_ref, s_hbm, sems)
+    for copy in copies:
+        copy.start()
     rows, cols = e_ref.shape
     even_row, even_col = parity("cross") == 0, parity("along") == 0
     pick = row_pick(even_row, row0[:ROWS], row1[:ROWS])
@@ -414,6 +414,8 @@
         ends += [both[:ROWS, :cols], both[ROWS + step :, :cols]]
     at = place((ROWS, cols), ROWS, 0)
     both_row[...] = jnp.where(at < ROWS // 2, ends[-1], ends[0])
+    for copy in copies:
+        copy.wait()
 
 
 def flux_kernel(
@@ -512,12 +514,19 @@
     count = crosses // 2 * alongs
     sizes = (half * core_shape.shape[1], range_shape.size)
     keep_shape = f32(half + thin, cols)
-    s_next, keep, ranged = run(
-        product_kernel, [tile, keep_shape, range_shape], 300 * cells,
-        s_held, range_test, *tests,
-        to=[pltpu.HBM, pltpu.VMEM, pltpu.VMEM], scratch=[pltpu.SemaphoreType.DMA((4,))],
+    keep, ranged = run(
+        product_kernel, [keep_shape, range_shape], 300 * cells, s_held, range_test, *tests
     )
     rim_shapes = [tile] + [f32(ROWS, cols), f32(rows, LANES)] * 2
+
+    def beside(after):
+        *rims, s_next = run(
+            both_kernel, rim_shapes + [tile], 60 * cells,
+            e2, mass_x, mass_y, slope, *halo, s_held, after,
+            to=[pltpu.VMEM] * 5 + [pltpu.HBM], scratch=[pltpu.SemaphoreType.DMA((4,))],
+        )
+        return rims, s_next
+
     def fluxes(rims, corner):
         return run(
             flux_kernel, [tile] * 2 + [f32(ROWS, LANES)], 40 * cells,
@@ -544,7 +553,7 @@
             functools.partial(merge_kernel, half), [sheet, f32(thin + ROWS, cols)], sheet.size,
             keep, got, ranged,
         )
-        rims = run(both_kernel, rim_shapes, 60 * cells, e2, mass_x, mass_y, slope, *halo, across)
+        rims, s_next = beside(across)
         corner = lax.ppermute(across, "cross", [(i, i ^ 2) for i in range(crosses)])
         thin_mine = across[:thin] + corner[:thin]
         thin_theirs = swap(thin_mine, "cross", 0)
@@ -568,7 +577,7 @@
         )
     else:
         corner = swap(give[-ROWS:], "cross", 1)
-        rims = run(both_kernel, rim_shapes, 60 * cells, e2, mass_x, mass_y, slope, *halo, give)
+        rims, s_next = beside(give)
         p_next, q_next, _ = fluxes(rims, corner)
         ranged = lax.psum(ranged, "along")
         coranged = lax.psum(dot(corange_test, s_held), "cross")

time: 48.3 us -> 48.3 us (level)
    ppermute x1, waiting for transfers between devices: 3.23 us -> 2.62 us  [body(): corner = lax.ppermute(across, 'cross', [(i, i ^ 2) for i in range(crosses)])]
where the time goes in v7:
time: 48.3 us; the launch traced here: 47.9 us
  starting transfers between devices  18 us (37%)
  blocking collectives  12.5 us (26%)
  Pallas kernels  9.62 us (20%)
  waiting for transfers between devices  6.88 us (14%)
  between operations  0.85 us (2%)
    all_to_all x1, blocking collectives, spread(): return lax.all_to_all(x, AXES, 0, 0, tiled=True, axis_index_groups=groups)  12.5 us
    ppermute x7, starting transfers between devices, swap(): lax.ppermute(message, axis, pairs)  10.6 us
    pallas_call x11, Pallas kernels, run(): pl.pallas_call(kernel, out_shape=outs, in_specs=kinds, out_specs=[pl.Bloc...  9.62 us
    all_to_all x1, starting transfers between devices, spread(): return lax.all_to_all(x, AXES, 0, 0, tiled=True, axis_index_groups=groups)  5.42 us
    all_to_all x1, waiting for transfers between devices, spread(): return lax.all_to_all(x, AXES, 0, 0, tiled=True, axis_index_groups=groups)  2.96 us
    ppermute x1, waiting for transfers between devices, body(): corner = lax.ppermute(across, 'cross', [(i, i ^ 2) for i in range(crosses)])  2.62 us
    ppermute x1, starting transfers between devices, body(): corner = lax.ppermute(across, 'cross', [(i, i ^ 2) for i in range(crosses)])  1.93 us
    ppermute x7, waiting for transfers between devices, swap(): lax.ppermute(message, axis, pairs)  1.3 us
  transfers between devices with their start and end apart: 9, of which 5 were waited for; matrix products, arithmetic and copies ran while one was open for 0% of the time, Pallas kernels for 12%

profile of v7, /device:TPU:0, one launch (start us, length us, event | category | flops | bytes accessed | tf_op | source)
XLA Modules:
  0.0 47.9 jit_solution(11456305918551511075)
XLA Ops:
  0.7 1.0 %shard_map.136 = (f32[16,256]{1,0:T(8,128)S(1)}, f32[16,256]{1,0:T(8,128)S(1)}) custom-call(f32[256,256]{1,0:T(8,128)} %e_ref.1, f32[256,256]{1,0:T(8,128)} %p_ref.3, f32[256,256]{1,0:T(8,128)} %q_ref.3, f32[256,256]{1,0:T(8,128)} %c_ref.1, s32[256,256]{1,0:T(8,128)} %w_ref.1), custom_call_target="tpu_custom_call" | custom-call | flops 65536 | bytes 1343488 | tf_op jit(solution)/shard_map/pallas_call | solution.py:477
  1.7 0.7 %collective-permute-start = (f32[16,256]{1,0:T(8,128)S(1)}, f32[16,256]{1,0:T(8,128)S(1)}, u32[]{:S(2)}, u32[]{:S(2)}) collective-permute-start(f32[16,256]{1,0:T(8,128)S(1)} %get-tuple-element.39), channel_id=1, source_target_pairs={{8,16},{16,8},{9,17},{17,9},{10,18},{18,10},{11,19},{19,11},{12,20... | collective-permute-start | bytes 49160 | tf_op jit(solution)/shard_map/ppermute | solution.py:461
  2.3 0.0 copy-start.5
  2.3 0.0 copy-start.6
  2.3 0.0 copy-start.7
  2.4 4.4 %collective-permute-start.1 = (f32[16,256]{1,0:T(8,128)S(1)}, f32[16,256]{1,0:T(8,128)S(1)}, u32[]{:S(2)}, u32[]{:S(2)}) collective-permute-start(f32[16,256]{1,0:T(8,128)S(1)} %get-tuple-element.40), channel_id=1, source_target_pairs={{0,8},{16,24},{8,0},{24,16},{1,9},{17,25},{9,1},{25,17},{2,10},{18... | collective-permute-start | bytes 49160 | tf_op jit(solution)/shard_map/ppermute | solution.py:461
  6.8 0.4 shard_map.138
  7.1 0.7 %collective-permute-start.2 = (f32[16,256]{1,0:T(8,128)S(1)}, f32[16,256]{1,0:T(8,128)S(1)}, u32[]{:S(2)}, u32[]{:S(2)}) collective-permute-start(f32[16,256]{1,0:T(8,128)S(1)} %get-tuple-element.45), channel_id=1, source_target_pairs={{1,2},{3,4},{5,6},{2,1},{4,3},{6,5},{9,10},{11,12},{13,14},{10,9},... | collective-permute-start | bytes 49160 | tf_op jit(solution)/shard_map/ppermute | solution.py:461
  7.8 4.4 %collective-permute-start.3 = (f32[16,256]{1,0:T(8,128)S(1)}, f32[16,256]{1,0:T(8,128)S(1)}, u32[]{:S(2)}, u32[]{:S(2)}) collective-permute-start(f32[16,256]{1,0:T(8,128)S(1)} %get-tuple-element.46), channel_id=1, source_target_pairs={{0,1},{2,3},{4,5},{6,7},{1,0},{3,2},{5,4},{7,6},{8,9},{10,11},{12,... | collective-permute-start | bytes 49160 | tf_op jit(solution)/shard_map/ppermute | solution.py:461
  12.1 0.0 collective-permute-done.row1
  12.2 0.0 collective-permute-done.1.row0
  12.2 1.4 %shard_map.137 = (f32[256,256]{1,0:T(8,128)S(1)}, f32[256,256]{1,0:T(8,128)S(1)}, f32[256,256]{1,0:T(8,128)S(1)}, f32[256,256]{1,0:T(8,128)S(1)}, f32[256,256]{1...) custom-call(f32[256,256]{1,0:T(8,128)S(1)} %copy-done.2, ...), custom_call_target="tpu_custom_call" | custom-call | flops 39321600 | bytes 4292608 | tf_op jit(solution)/shard_map/pallas_call | solution.py:477
  13.6 0.0 collective-permute-done.2.col1
  13.6 0.3 collective-permute-done.3.col0
  13.9 1.2 %shard_map.139 = (f32[256,256]{1,0:T(8,128)S(1)}, f32[256,256]{1,0:T(8,128)S(1)}, f32[208,256]{1,0:T(8,128)S(1)}) custom-call(f32[256,256]{1,0:T(8,128)S(1)} %get-tuple-element.41.e_ref, f32[256,256]{1,0:T(8,128)S(1)} %get-tuple-element.43.q_ref.mq_ref, f32[256,256]{1,0:T(8,128)S(1)} %get-tuple-element.44.a_ref, f32[256,256]{1,0:T(8,128)S(1)} %get-tuple-element.47.f_ref, ...), custom_call_target="tpu_custom_call" | custom-call | flops 13107200 | bytes 3194880 | tf_op jit(solution)/shard_map/pallas_call | solution.py:477
  15.1 0.1 collective-permute-start.4
  15.2 0.8 %shard_map.140 = (f32[192,256]{1,0:T(8,128)S(1)}, f32[256,128]{1,0:T(8,128)S(1)}) custom-call(f32[256,256]{1,0:T(8,128)S(1)} %get-tuple-element.51.s_ref, f32[256,128]{1,0:T(8,128)S(1)} %copy-done.8, f32[128,256]{1,0:T(8,128)S(1)} %copy-done.7, f32[256,256]{1,0:T(8,128)S(1)} %copy-done.5, f32[256,256]{1,0:T(8,128)S(1)} %copy-done.6), custom_call_target="tpu_custom_call" | custom-call | flops 19660800 | bytes 1376256 | tf_op jit(solution)/shard_map/pallas_call | solution.py:477
  15.9 0.7 %collective-permute-done.4.got_ref = f32[208,256]{1,0:T(8,128)S(1)} collective-permute-done((f32[208,256]{1,0:T(8,128)S(1)}, f32[208,256]{1,0:T(8,128)S(1)}, u32[]{:S(2)}, u32[]{:S(2)}) %collective-permute-start.4) | collective-permute-done | bytes 213024 | tf_op jit(solution)/shard_map/ppermute | solution.py:461
  16.6 0.7 %shard_map.141 = (f32[16,4,8,128]{3,2,1,0:T(8,128)}, f32[72,256]{1,0:T(8,128)S(1)}) custom-call(f32[192,256]{1,0:T(8,128)S(1)} %get-tuple-element.52.keep_ref, f32[208,256]{1,0:T(8,128)S(1)} %collective-permute-done.4.got_ref, f32[256,128]{1,0:T(8,128)S(1)} %get-tuple-element.54.range_ref), custom_call_target="tpu_custom_call" | custom-call | flops 65536 | bytes 876544 | tf_op jit(solution)/shard_map/pallas_call | solution.py:477
  17.3 5.4 %all-to-all-start = ((f32[16,4,8,128]{3,2,1,0:T(8,128)}), f32[16,4,8,128]{3,2,1,0:T(8,128)S(1)}, u32[]{:S(2)}, u32[]{:S(2)}) async-start(f32[16,4,8,128]{3,2,1,0:T(8,128)} %get-tuple-element.66), calls=%async_computation | async-start | bytes 524288 | tf_op jit(solution)/shard_map/all_to_all | solution.py:550
  22.8 1.9 %collective-permute-start.5 = (f32[72,256]{1,0:T(8,128)S(1)}, f32[72,256]{1,0:T(8,128)S(1)}, u32[]{:S(2)}, u32[]{:S(2)}) collective-permute-start(f32[72,256]{1,0:T(8,128)S(1)} %get-tuple-element.55.after), channel_id=1, source_target_pairs={{0,16},{8,24},{16,0},{24,8},{1,17},{9,25},{17,1},{25,9},{2,18},{10... | collective-permute-start | bytes 221192 | tf_op jit(solution)/shard_map/ppermute | solution.py:557
  24.7 1.4 %shard_map.142 = (f32[256,256]{1,0:T(8,128)S(1)}, f32[8,256]{1,0:T(8,128)S(1)}, f32[256,128]{1,0:T(8,128)S(1)}, f32[8,256]{1,0:T(8,128)S(1)}, f32[256,128]{1,0:T(8,128)S(1)}, /*index=5*/f32[256,256]{1,0:T(8,128)}) custom-call(f32[256,256]{1,0:T(8,128)S(1)} %get-tuple-element.41.e_ref, f32[256,256]{1,0:T(8,128)S(1)} %get-tuple-element.42.mp_ref, ...), custom_call_target="tpu_custom_call" | custom-call | flops 3932160 | bytes 2252800 | tf_op jit(solution)/shard_map/pallas_call | solution.py:477
  26.1 2.6 %collective-permute-done.5.corner_ref = f32[72,256]{1,0:T(8,128)S(1)} collective-permute-done((f32[72,256]{1,0:T(8,128)S(1)}, f32[72,256]{1,0:T(8,128)S(1)}, u32[]{:S(2)}, u32[]{:S(2)}) %collective-permute-start.5) | collective-permute-done | bytes 73760 | tf_op jit(solution)/shard_map/ppermute | solution.py:557
  28.7 1.3 %shard_map.143 = (f32[256,256]{1,0:T(8,128)}, f32[256,256]{1,0:T(8,128)}, f32[8,128]{1,0:T(8,128)S(1)}) custom-call(f32[256,256]{1,0:T(8,128)S(1)} %get-tuple-element.57.both_ref, f32[8,256]{1,0:T(8,128)S(1)} %get-tuple-element.58.both_row, f32[256,128]{1,0:T(8,128)S(1)} %get-tuple-element.59.both_col, f32[8,256]{1,0:T(8,128)S(1)} %get-tuple-element.60.quarter_row, ...), custom_call_target="tpu_custom_call" | custom-call | flops 2621440 | bytes 2928640 | tf_op jit(solution)/shard_map/pallas_call | solution.py:477
  30.0 3.0 %all-to-all-done.got = f32[16,4,8,128]{3,2,1,0:T(8,128)S(1)} async-done(((f32[16,4,8,128]{3,2,1,0:T(8,128)}), f32[16,4,8,128]{3,2,1,0:T(8,128)S(1)}, u32[]{:S(2)}, u32[]{:S(2)}) %all-to-all-start) | async-done | bytes 262176 | tf_op jit(solution)/shard_map/all_to_all | solution.py:550
  33.0 12.5 %all_to_all.10.mine = f32[16,4,8,128]{3,2,1,0:T(8,128)S(1)} all-to-all(f32[16,4,8,128]{3,2,1,0:T(8,128)S(1)} %shard_map.144), channel_id=1, replica_groups={{0,1,2,3,4,5,6,7,16,17,18,19,20,21,22,23},{8,9,10,11,12,13,14,15,24,25,..., dimensions={0} | all-to-all | bytes 524288 | tf_op jit(solution)/shard_map/all_to_all | solution.py:550
  45.5 0.0 collective-permute-start.6
  45.5 0.5 %collective-permute-start.7 = (f32[64,256]{1,0:T(8,128)S(1)}, f32[64,256]{1,0:T(8,128)S(1)}, u32[]{:S(2)}, u32[]{:S(2)}) collective-permute-start(f32[64,256]{1,0:T(8,128)S(1)} %slice_add_fusion.rest_0_.thin_mine), channel_id=1, source_target_pairs={{0,8},{16,24},{8,0},{24,16},{1,9},{17,25},{9,1},{25,17},{2,10},{18... | collective-permute-start | bytes 196616 | tf_op jit(solution)/shard_map/ppermute | solution.py:461
  46.0 0.8 %shard_map.145 = (f32[256,256]{1,0:T(8,128)}, f32[256,128]{1,0:T(8,128)}) custom-call(f32[16,4,8,128]{3,2,1,0:T(8,128)S(1)} %all_to_all.10.mine), custom_call_target="tpu_custom_call" | custom-call | flops 65536 | bytes 655360 | tf_op jit(solution)/shard_map/pallas_call | solution.py:477
  46.8 0.3 collective-permute-done.7.thin_theirs
  47.1 0.0 collective-permute-done.6.theirs
  47.1 0.8 %shard_map.146 = (f32[256,256]{1,0:T(8,128)}, f32[128,256]{1,0:T(8,128)}) custom-call(f32[16,4,8,128]{3,2,1,0:T(8,128)S(1)} %collective-permute-done.6.theirs, f32[256,256]{1,0:T(8,128)} %get-tuple-element.69.core_in, f32[64,256]{1,0:T(8,128)S(1)} %slice_add_fusion.rest_0_.thin_mine, ...), custom_call_target="tpu_custom_call", output_to_operand_aliasing={{0}: (1, {})} | custom-call | flops 65536 | bytes 1048576 | tf_op jit(solution)/shard_map/pallas_call | solution.py:477
  (17 shorter events, 0.1 us)
Async XLA Ops:
  0.6 6.1 %copy-start.1 = (f32[256,256]{1,0:T(8,128)S(1)}, f32[256,256]{1,0:T(8,128)}, u32[]{:S(2)}) copy-start(f32[256,256]{1,0:T(8,128)} %q_ref.3) | copy-start | bytes 786436
  0.6 6.1 %copy-start = (f32[256,256]{1,0:T(8,128)S(1)}, f32[256,256]{1,0:T(8,128)}, u32[]{:S(2)}) copy-start(f32[256,256]{1,0:T(8,128)} %p_ref.3) | copy-start | bytes 786436
  0.7 6.1 %copy-start.4 = (s32[256,256]{1,0:T(8,128)S(1)}, s32[256,256]{1,0:T(8,128)}, u32[]{:S(2)}) copy-start(s32[256,256]{1,0:T(8,128)} %w_ref.1) | copy-start | bytes 786436
  0.7 6.1 %copy-start.3 = (f32[256,256]{1,0:T(8,128)S(1)}, f32[256,256]{1,0:T(8,128)}, u32[]{:S(2)}) copy-start(f32[256,256]{1,0:T(8,128)} %c_ref.1) | copy-start | bytes 786436
  0.7 6.1 %copy-start.2 = (f32[256,256]{1,0:T(8,128)S(1)}, f32[256,256]{1,0:T(8,128)}, u32[]{:S(2)}) copy-start(f32[256,256]{1,0:T(8,128)} %e_ref.1) | copy-start | bytes 786436
  1.7 10.5 %collective-permute-start = (f32[16,256]{1,0:T(8,128)S(1)}, f32[16,256]{1,0:T(8,128)S(1)}, u32[]{:S(2)}, u32[]{:S(2)}) collective-permute-start(f32[16,256]{1,0:T(8,128)S(1)} %get-tuple-element.39), channel_id=1, source_target_pairs={{8,16},{16,8},{9,17},{17,9},{10,18},{18,10},{11,19},{19,11},{12,20... | collective-permute-start | bytes 49160 | tf_op jit(solution)/shard_map/ppermute | solution.py:461
  2.3 9.8 %copy-start.5 = (f32[256,256]{1,0:T(8,128)S(1)}, f32[256,256]{1,0:T(8,128)}, u32[]{:S(2)}) copy-start(f32[256,256]{1,0:T(8,128)} %left_ref.5) | copy-start | bytes 786436
  2.3 9.8 %copy-start.6 = (f32[256,256]{1,0:T(8,128)S(1)}, f32[256,256]{1,0:T(8,128)}, u32[]{:S(2)}) copy-start(f32[256,256]{1,0:T(8,128)} %right_ref.5) | copy-start | bytes 786436
  2.3 9.8 %copy-start.7 = (f32[128,256]{1,0:T(8,128)S(1)}, f32[128,256]{1,0:T(8,128)}, u32[]{:S(2)}) copy-start(f32[128,256]{1,0:T(8,128)} %cr_ref.5) | copy-start | bytes 393220
  2.4 9.8 %collective-permute-start.1 = (f32[16,256]{1,0:T(8,128)S(1)}, f32[16,256]{1,0:T(8,128)S(1)}, u32[]{:S(2)}, u32[]{:S(2)}) collective-permute-start(f32[16,256]{1,0:T(8,128)S(1)} %get-tuple-element.40), channel_id=1, source_target_pairs={{0,8},{16,24},{8,0},{24,16},{1,9},{17,25},{9,1},{25,17},{2,10},{18... | collective-permute-start | bytes 49160 | tf_op jit(solution)/shard_map/ppermute | solution.py:461
  7.1 6.5 %collective-permute-start.2 = (f32[16,256]{1,0:T(8,128)S(1)}, f32[16,256]{1,0:T(8,128)S(1)}, u32[]{:S(2)}, u32[]{:S(2)}) collective-permute-start(f32[16,256]{1,0:T(8,128)S(1)} %get-tuple-element.45), channel_id=1, source_target_pairs={{1,2},{3,4},{5,6},{2,1},{4,3},{6,5},{9,10},{11,12},{13,14},{10,9},... | collective-permute-start | bytes 49160 | tf_op jit(solution)/shard_map/ppermute | solution.py:461
  7.8 6.1 %collective-permute-start.3 = (f32[16,256]{1,0:T(8,128)S(1)}, f32[16,256]{1,0:T(8,128)S(1)}, u32[]{:S(2)}, u32[]{:S(2)}) collective-permute-start(f32[16,256]{1,0:T(8,128)S(1)} %get-tuple-element.46), channel_id=1, source_target_pairs={{0,1},{2,3},{4,5},{6,7},{1,0},{3,2},{5,4},{7,6},{8,9},{10,11},{12,... | collective-permute-start | bytes 49160 | tf_op jit(solution)/shard_map/ppermute | solution.py:461
  13.9 1.3 %copy-start.8 = (f32[256,128]{1,0:T(8,128)S(1)}, f32[256,128]{1,0:T(8,128)}, u32[]{:S(2)}) copy-start(f32[256,128]{1,0:T(8,128)} %r_ref.1) | copy-start | bytes 393220
  15.1 1.5 %collective-permute-start.4 = (f32[208,256]{1,0:T(8,128)S(1)}, f32[208,256]{1,0:T(8,128)S(1)}, u32[]{:S(2)}, u32[]{:S(2)}) collective-permute-start(f32[208,256]{1,0:T(8,128)S(1)} %get-tuple-element.53), channel_id=1, source_target_pairs={{0,8},{16,24},{8,0},{24,16},{1,9},{17,25},{9,1},{25,17},{2,10},{18... | collective-permute-start | bytes 638984 | tf_op jit(solution)/shard_map/ppermute | solution.py:461
  17.3 15.6 %all-to-all-start = ((f32[16,4,8,128]{3,2,1,0:T(8,128)}), f32[16,4,8,128]{3,2,1,0:T(8,128)S(1)}, u32[]{:S(2)}, u32[]{:S(2)}) async-start(f32[16,4,8,128]{3,2,1,0:T(8,128)} %get-tuple-element.66), calls=%async_computation | async-start | bytes 524288 | tf_op jit(solution)/shard_map/all_to_all | solution.py:550
  22.8 5.9 %collective-permute-start.5 = (f32[72,256]{1,0:T(8,128)S(1)}, f32[72,256]{1,0:T(8,128)S(1)}, u32[]{:S(2)}, u32[]{:S(2)}) collective-permute-start(f32[72,256]{1,0:T(8,128)S(1)} %get-tuple-element.55.after), channel_id=1, source_target_pairs={{0,16},{8,24},{16,0},{24,8},{1,17},{9,25},{17,1},{25,9},{2,18},{10... | collective-permute-start | bytes 221192 | tf_op jit(solution)/shard_map/ppermute | solution.py:557
  45.5 1.6 %collective-permute-start.6 = (f32[16,4,8,128]{3,2,1,0:T(8,128)S(1)}, f32[16,4,8,128]{3,2,1,0:T(8,128)S(1)}, u32[]{:S(2)}, u32[]{:S(2)}) collective-permute-start(f32[16,4,8,128]{3,2,1,0:T(8,128)S(1)} %all_to_all.10.mine), channel_id=1, source_target_pairs={{0,8},{16,24},{8,0},{24,16},{1,9},{17,25},{9,1},{25,17},{2,10},{18... | collective-permute-start | bytes 786440 | tf_op jit(solution)/shard_map/ppermute | solution.py:461
  45.5 1.6 %collective-permute-start.7 = (f32[64,256]{1,0:T(8,128)S(1)}, f32[64,256]{1,0:T(8,128)S(1)}, u32[]{:S(2)}, u32[]{:S(2)}) collective-permute-start(f32[64,256]{1,0:T(8,128)S(1)} %slice_add_fusion.rest_0_.thin_mine), channel_id=1, source_target_pairs={{0,8},{16,24},{8,0},{24,16},{1,9},{17,25},{9,1},{25,17},{2,10},{18... | collective-permute-start | bytes 196616 | tf_op jit(solution)/shard_map/ppermute | solution.py:461
